TPU v7x, 32 devices: a whole 2x2x4 slice. The times are simulated.
32 devices in a mesh: dp: 16 (over z, x, core), tensor: 2 (over y).
Axes of the slice: x: 2, y: 2, z: 4, core: 2. Of those that a mesh axis runs over, the one named last changes fastest.
Arguments:
- tokens: bfloat16 [16384, 2048], P(('dp', 'tensor')), may hold values from -6 to 6
- cotangent: bfloat16 [16384, 2048], P(('dp', 'tensor')), may hold values from -6 to 6
- routes: int32 [1, 16384, 2], P(None, 'dp'), may hold values from 0 to 3, all different within a row; in each aligned block of 1024 rows (0 to 1023, 1024 to 2047, ..., all dimensions but the last counted through in order) at most 576 rows name the same one
- route_weights: float32 [1, 16384, 2], P(None, 'dp'), may hold values from 0.3 to 1
- query_weight: bfloat16 [1, 2048, 4096], P(None, 'dp', 'tensor'), may hold values from -0.125 to 0.125
- key_weight: bfloat16 [1, 2048, 512], P(None, 'dp', 'tensor'), may hold values from -0.125 to 0.125
- value_weight: bfloat16 [1, 2048, 512], P(None, 'dp', 'tensor'), may hold values from -0.125 to 0.125
- out_weight: bfloat16 [1, 2048, 4096], P(None, 'dp', 'tensor'), may hold values from -0.375 to 0.375
- gate_weight: bfloat16 [1, 2048, 4, 768], P(None, 'dp', None, 'tensor'), may hold values from -0.125 to 0.125
- up_weight: bfloat16 [1, 2048, 4, 768], P(None, 'dp', None, 'tensor'), may hold values from -0.125 to 0.125
- down_weight: bfloat16 [1, 2048, 4, 768], P(None, 'dp', None, 'tensor'), may hold values from -0.625 to 0.625
- attn_gain: float32 [1, 2048], replicated, may hold values from 0.1 to 1.9
- ffn_gain: float32 [1, 2048], replicated, may hold values from 0.1 to 1.9
- query_gain: float32 [1, 128], replicated, may hold values from 0.1 to 1.9
- key_gain: float32 [1, 128], replicated, may hold values from 0.1 to 1.9
Outputs:
- layer_out: bfloat16 [16384, 2048], P(('dp', 'tensor'))
- tokens_grad: float32 [16384, 2048], P(('dp', 'tensor'))
- query_grad: float32 [1, 2048, 4096], P(None, 'dp', 'tensor')
- key_grad: float32 [1, 2048, 512], P(None, 'dp', 'tensor')
- value_grad: float32 [1, 2048, 512], P(None, 'dp', 'tensor')
- out_grad: float32 [1, 2048, 4096], P(None, 'dp', 'tensor')
- gate_grad: float32 [1, 2048, 4, 768], P(None, 'dp', None, 'tensor')
- up_grad: float32 [1, 2048, 4, 768], P(None, 'dp', None, 'tensor')
- down_grad: float32 [1, 2048, 4, 768], P(None, 'dp', None, 'tensor')
- attn_gain_grad: float32 [1, 2048], replicated
- ffn_gain_grad: float32 [1, 2048], replicated
- query_gain_grad: float32 [1, 128], replicated
- key_gain_grad: float32 [1, 128], replicated
Inputs may be any that keep to these rules, and one draw needn't show every extreme that they name: `routes`: each row names 2 different experts; among the 1024 rows of one sequence in one layer no expert is named more than 576 times, and in some sequence some expert exactly 576 times.
All inputs are finite; a program needn't handle non-finite values.
Results may differ from a plain program's by a relative error of at most 0.02.
Values may be sent and summed in bfloat16 or wider, within the bound.
No kernel may reach another device: no remote copies, remote signals or barrier semaphores. Data moves between devices by JAX's collectives and lax.ppermute only.
A program may use at most 448 MiB of HBM per device.

v0:
```python
import jax
import jax.numpy as jnp
from jax import lax
from jax.sharding import PartitionSpec as P

HD = 128
EXPERTS = 4
TOP = 2
LAYERS = 1


EPS = 1e-06
THETA = 1000000.0
NEGATIVE = -1e30


def for_sending(shard):

    def short(part):
        return part.astype(jnp.bfloat16) if part.dtype == jnp.float32 else part

    return jax.tree.map(short, shard)


def rms_norm(values, gain):
    scale = lax.rsqrt(jnp.mean(values * values, axis=-1, keepdims=True) + EPS)
    return (values * scale * gain, scale)


def norm_back(values, scale, gain, grad):
    scaled = grad * gain
    inner = jnp.mean(scaled * values, axis=-1, keepdims=True)
    grad_values = scale * scaled - values * (scale * scale * scale) * inner
    leading = tuple(range(values.ndim - 1))
    return (grad_values, jnp.sum(grad * values * scale, axis=leading))


def rotate(values, cosine, sine):
    half = values.shape[-1] // 2
    first = values[..., :half]
    second = values[..., half:]
    return jnp.concatenate(
        [first * cosine - second * sine, second * cosine + first * sine], axis=-1
    )


def rope_tables(seq):
    position = lax.iota(jnp.float32, seq)
    freq = THETA ** (-2.0 * lax.iota(jnp.float32, HD // 2) / HD)
    angle = position[:, None] * freq[None, :]
    return (jnp.cos(angle)[:, None, :], jnp.sin(angle)[:, None, :])


def attn_scores(query_block, key_b, start, seq):
    rows = query_block.shape[0]
    scores = jnp.einsum(
        "qkgh,pkh->kgqp", query_block, key_b, preferred_element_type=jnp.float32
    ) * HD ** (-0.5)
    causal = (start + lax.iota(jnp.int32, rows))[:, None] >= lax.iota(jnp.int32, seq)[None, :]
    return jnp.where(causal, scores, NEGATIVE)


def fetch(shards):
    return jax.tree.map(
        lambda part, own: part.astype(own.dtype),
        lax.all_gather(for_sending(shards), "dp", axis=0, tiled=True),
        shards,
    )


def rows_gather(local):
    return lax.all_gather(local, "tensor", axis=0, tiled=True)


def rows_sum(partial_value):
    return lax.psum_scatter(
        partial_value.astype(jnp.bfloat16), "tensor", scatter_dimension=0, tiled=True
    ).astype(jnp.float32)


def grads_gather(local):
    return lax.all_gather(local, "tensor", axis=0, tiled=True)


def grads_sum(partial_value):
    return lax.psum_scatter(
        partial_value.astype(jnp.bfloat16), "tensor", scatter_dimension=0, tiled=True
    ).astype(jnp.float32)


def dispatch(route_rows, weight_rows, seq, capacity):
    flat_route = route_rows.reshape(-1)
    onehot = (flat_route[:, None] == lax.iota(jnp.int32, EXPERTS)[None, :]).astype(jnp.int32)
    place = jnp.sum((jnp.cumsum(onehot, axis=0) - onehot) * onehot, axis=1)
    slot = flat_route * capacity + place
    owner = lax.iota(jnp.int32, seq * TOP) // TOP
    slot_token = jnp.zeros((EXPERTS * capacity,), jnp.int32).at[slot].set(owner)
    slot_gate = jnp.zeros((EXPERTS * capacity,), jnp.float32).at[slot].set(weight_rows.reshape(-1))
    return (slot_token.reshape(EXPERTS, capacity), slot_gate.reshape(EXPERTS, capacity))


def forward_layer(resid, full, gains, route_rows, weight_rows, cosine, sine):
    query_w, key_w, value_w, out_w, gate_w, up_w, down_w = full
    attn_g, ffn_g, query_g, key_g = gains
    width = resid.shape[1]
    normed_one, scale_one = rms_norm(resid, attn_g)
    normed = rows_gather(normed_one.astype(jnp.bfloat16))
    seq = normed.shape[0]
    heads = query_w.shape[1] // HD
    kv_heads = key_w.shape[1] // HD
    query_raw = jnp.dot(normed, query_w, preferred_element_type=jnp.float32).reshape(seq, heads, HD)
    key_raw = jnp.dot(normed, key_w, preferred_element_type=jnp.float32).reshape(seq, kv_heads, HD)
    value_b = (
        jnp.dot(normed, value_w, preferred_element_type=jnp.float32)
        .astype(jnp.bfloat16)
        .reshape(seq, kv_heads, HD)
    )
    query_b = (
        rotate(rms_norm(query_raw, query_g)[0], cosine, sine)
        .astype(jnp.bfloat16)
        .reshape(seq, kv_heads, heads // kv_heads, HD)
    )
    key_b = rotate(rms_norm(key_raw, key_g)[0], cosine, sine).astype(jnp.bfloat16)
    block = min(512, seq)
    lse_parts = []
    context_parts = []
    for start in range(0, seq, block):
        scores = attn_scores(query_b[start : start + block], key_b, start, seq)
        peak = jnp.max(scores, axis=-1, keepdims=True)
        log_total = peak + jnp.log(jnp.sum(jnp.exp(scores - peak), axis=-1, keepdims=True))
        probs_b = jnp.exp(scores - log_total).astype(jnp.bfloat16)
        context_parts.append(
            jnp.einsum("kgqp,pkh->qkgh", probs_b, value_b, preferred_element_type=jnp.float32)
            .reshape(block, heads * HD)
            .astype(jnp.bfloat16)
        )
        lse_parts.append(log_total)
    lse = jnp.concatenate(lse_parts, axis=2)
    context_b = jnp.concatenate(context_parts, axis=0)
    attn_part = jnp.einsum("sc,dc->sd", context_b, out_w, preferred_element_type=jnp.float32)
    resid_two = resid + rows_sum(attn_part)
    normed_two_loc, scale_two = rms_norm(resid_two, ffn_g)
    normed_two = rows_gather(normed_two_loc.astype(jnp.bfloat16))
    capacity = seq * TOP * 9 // (8 * EXPERTS)
    slot_token, slot_gate = dispatch(route_rows, weight_rows, seq, capacity)
    inputs = normed_two[slot_token]
    gate_val = jnp.einsum("esd,def->esf", inputs, gate_w, preferred_element_type=jnp.float32)
    up_val = jnp.einsum("esd,def->esf", inputs, up_w, preferred_element_type=jnp.float32)
    hidden_b = (jax.nn.silu(gate_val) * up_val * slot_gate[..., None]).astype(jnp.bfloat16)
    expert_out = jnp.einsum("esf,def->esd", hidden_b, down_w, preferred_element_type=jnp.float32)
    moe_part = (
        jnp.zeros((seq, width), jnp.float32)
        .at[slot_token.reshape(-1)]
        .add(expert_out.reshape(-1, width))
    )
    output = resid_two + rows_sum(moe_part)
    saved = (
        resid,
        scale_one,
        normed,
        query_raw,
        key_raw,
        query_b,
        key_b,
        value_b,
        lse,
        context_b,
        resid_two,
        scale_two,
        slot_token,
        slot_gate,
        inputs,
        gate_val,
        up_val,
        hidden_b,
    )
    return (output, saved)


def backward_layer(grad, full, gains, saved, cosine, sine):
    query_w, key_w, value_w, out_w, gate_w, up_w, down_w = full
    attn_g, ffn_g, query_g, key_g = gains
    (
        resid,
        scale_one,
        normed,
        query_raw,
        key_raw,
        query_b,
        key_b,
        value_b,
        lse,
        context_b,
        resid_two,
        scale_two,
        slot_token,
        slot_gate,
        inputs,
        gate_val,
        up_val,
        hidden_b,
    ) = saved
    width = resid.shape[1]
    seq = normed.shape[0]
    heads = query_w.shape[1] // HD
    kv_heads = key_w.shape[1] // HD
    group = heads // kv_heads
    own_rows = width // lax.axis_size("dp")
    grad_rows = grads_gather(grad.astype(jnp.bfloat16))
    grad_buf = grad_rows[slot_token]
    grad_hidden = (
        jnp.einsum("esd,def->esf", grad_buf, down_w, preferred_element_type=jnp.float32)
        * slot_gate[..., None]
    )
    sigma = jax.nn.sigmoid(gate_val)
    grad_gate_b = (grad_hidden * up_val * sigma * (1.0 + gate_val * (1.0 - sigma))).astype(
        jnp.bfloat16
    )
    grad_up_b = (grad_hidden * (gate_val * sigma)).astype(jnp.bfloat16)
    grad_inputs = jnp.einsum(
        "esf,def->esd", grad_gate_b, gate_w, preferred_element_type=jnp.float32
    ) + jnp.einsum("esf,def->esd", grad_up_b, up_w, preferred_element_type=jnp.float32)
    grad_normed_two = (
        jnp.zeros((seq, width), jnp.float32)
        .at[slot_token.reshape(-1)]
        .add(grad_inputs.reshape(-1, width))
    )
    grad_two, ffn_gain_part = norm_back(resid_two, scale_two, ffn_g, grads_sum(grad_normed_two))
    grad_two = grad + grad_two
    grad_rows_two = grads_gather(grad_two.astype(jnp.bfloat16))
    grad_context_b = (
        jnp.dot(grad_rows_two, out_w, preferred_element_type=jnp.float32)
        .astype(jnp.bfloat16)
        .reshape(seq, kv_heads, group, HD)
    )
    block = min(512, seq)
    value_total = jnp.zeros((seq, kv_heads, HD), jnp.float32)
    key_total = jnp.zeros((seq, kv_heads, HD), jnp.float32)
    query_parts = []
    for start in range(0, seq, block):
        query_block = query_b[start : start + block]
        context_block = grad_context_b[start : start + block]
        scores = attn_scores(query_block, key_b, start, seq)
        probs = jnp.exp(scores - lse[:, :, start : start + block])
        probs_b = probs.astype(jnp.bfloat16)
        grad_probs = jnp.einsum(
            "qkgh,pkh->kgqp", context_block, value_b, preferred_element_type=jnp.float32
        )
        inner = jnp.sum(probs * grad_probs, axis=-1, keepdims=True)
        grad_scores_b = (probs * (grad_probs - inner)).astype(jnp.bfloat16)
        value_total = value_total + jnp.einsum(
            "kgqp,qkgh->pkh", probs_b, context_block, preferred_element_type=jnp.float32
        )
        query_parts.append(
            jnp.einsum(
                "kgqp,pkh->qkgh", grad_scores_b, key_b, preferred_element_type=jnp.float32
            ).reshape(block, heads, HD)
            * HD ** (-0.5)
        )
        key_total = key_total + jnp.einsum(
            "kgqp,qkgh->pkh", grad_scores_b, query_block, preferred_element_type=jnp.float32
        ) * HD ** (-0.5)
    grad_value_b = value_total.astype(jnp.bfloat16)
    grad_query_rot = jnp.concatenate(query_parts, axis=0)
    query_scale = rms_norm(query_raw, query_g)[1]
    key_scale = rms_norm(key_raw, key_g)[1]
    grad_query_raw, query_gain_part = norm_back(
        query_raw, query_scale, query_g, rotate(grad_query_rot, cosine, -sine)
    )
    grad_key_raw, key_gain_part = norm_back(
        key_raw, key_scale, key_g, rotate(key_total, cosine, -sine)
    )
    grad_query_b = grad_query_raw.reshape(seq, heads * HD).astype(jnp.bfloat16)
    grad_key_b = grad_key_raw.reshape(seq, kv_heads * HD).astype(jnp.bfloat16)
    grad_value_flat = grad_value_b.reshape(seq, kv_heads * HD)
    grad_normed = jnp.einsum("sc,dc->sd", grad_query_b, query_w, preferred_element_type=jnp.float32)
    grad_normed = grad_normed + jnp.einsum(
        "sc,dc->sd", grad_key_b, key_w, preferred_element_type=jnp.float32
    )
    grad_normed = grad_normed + jnp.einsum(
        "sc,dc->sd", grad_value_flat, value_w, preferred_element_type=jnp.float32
    )
    grad_one, attn_gain_part = norm_back(resid, scale_one, attn_g, grads_sum(grad_normed))
    grad_resid = grad_two + grad_one
    parts = [
        jnp.einsum("esd,esf->def", inputs, grad_gate_b, preferred_element_type=jnp.float32).reshape(
            lax.axis_size("dp") * own_rows, -1
        ),
        jnp.einsum("esd,esf->def", inputs, grad_up_b, preferred_element_type=jnp.float32).reshape(
            lax.axis_size("dp") * own_rows, -1
        ),
        jnp.einsum("esd,esf->def", grad_buf, hidden_b, preferred_element_type=jnp.float32).reshape(
            lax.axis_size("dp") * own_rows, -1
        ),
    ]
    attn_parts = [
        jnp.einsum("sd,sc->dc", normed, grad_query_b, preferred_element_type=jnp.float32),
        jnp.einsum("sd,sc->dc", normed, grad_key_b, preferred_element_type=jnp.float32),
        jnp.einsum("sd,sc->dc", normed, grad_value_flat, preferred_element_type=jnp.float32),
        jnp.einsum("sd,sc->dc", grad_rows_two, context_b, preferred_element_type=jnp.float32),
    ]
    summed = lax.psum_scatter(
        jnp.concatenate(
            [jnp.concatenate(attn_parts, axis=1), jnp.concatenate(parts, axis=1)], axis=1
        ),
        "dp",
        scatter_dimension=0,
        tiled=True,
    )
    hidden_cols = gate_w.shape[1] * gate_w.shape[2]
    widths = [
        heads * HD,
        kv_heads * HD,
        kv_heads * HD,
        heads * HD,
        hidden_cols,
        hidden_cols,
        hidden_cols,
    ]
    pieces = []
    offset = 0
    for extent in widths:
        pieces.append(summed[:, offset : offset + extent])
        offset = offset + extent
    expert_shape = (own_rows, gate_w.shape[1], gate_w.shape[2])
    weight_grads = (
        pieces[0],
        pieces[1],
        pieces[2],
        pieces[3],
        pieces[4].reshape(expert_shape),
        pieces[5].reshape(expert_shape),
        pieces[6].reshape(expert_shape),
    )
    gain_grads = (attn_gain_part, ffn_gain_part, query_gain_part, key_gain_part)
    return (grad_resid, weight_grads, gain_grads)


def body(
    tokens,
    cotangent,
    routes,
    route_weights,
    query_weight,
    key_weight,
    value_weight,
    out_weight,
    gate_weight,
    up_weight,
    down_weight,
    attn_gain,
    ffn_gain,
    query_gain,
    key_gain,
):
    weights = (
        query_weight,
        key_weight,
        value_weight,
        out_weight,
        gate_weight,
        up_weight,
        down_weight,
    )
    resid = tokens.astype(jnp.float32)
    seq = tokens.shape[0] * lax.axis_size("tensor")
    cosine, sine = rope_tables(seq)
    layer = 0
    full = fetch(tuple((weight[layer] for weight in weights)))
    gains = (attn_gain[layer], ffn_gain[layer], query_gain[layer], key_gain[layer])
    resid, saved = forward_layer(
        resid, full, gains, routes[layer], route_weights[layer], cosine, sine
    )
    saved_list = [saved]
    output = resid.astype(jnp.bfloat16)
    grad = cotangent.astype(jnp.float32)
    weight_list = [None] * LAYERS
    gain_list = [None] * LAYERS
    for layer in reversed(range(LAYERS)):
        full = fetch(tuple((weight[layer] for weight in weights)))
        gains = (attn_gain[layer], ffn_gain[layer], query_gain[layer], key_gain[layer])
        grad, weight_list[layer], gain_list[layer] = backward_layer(
            grad, full, gains, saved_list[layer], cosine, sine
        )
    stacked = [jnp.stack([weight_list[0][index]]) for index in range(7)]
    attn_stack = jnp.stack([gain_list[0][0]])
    ffn_stack = jnp.stack([gain_list[0][1]])
    query_stack = jnp.stack([gain_list[0][2]])
    key_stack = jnp.stack([gain_list[0][3]])
    attn_total, ffn_total, query_total, key_total = lax.psum(
        (attn_stack, ffn_stack, query_stack, key_stack), ("dp", "tensor")
    )
    return (
        output,
        grad,
        stacked[0],
        stacked[1],
        stacked[2],
        stacked[3],
        stacked[4],
        stacked[5],
        stacked[6],
        attn_total,
        ffn_total,
        query_total,
        key_total,
    )


def solution(mesh):
    return jax.shard_map(
        body,
        mesh=mesh,
        in_specs=(
            P(("dp", "tensor"), None),
            P(("dp", "tensor"), None),
            P(None, "dp", None),
            P(None, "dp", None),
            P(None, "dp", "tensor"),
            P(None, "dp", "tensor"),
            P(None, "dp", "tensor"),
            P(None, "dp", "tensor"),
            P(None, "dp", None, "tensor"),
            P(None, "dp", None, "tensor"),
            P(None, "dp", None, "tensor"),
            P(),
            P(),
            P(),
            P(),
        ),
        out_specs=(
            P(("dp", "tensor"), None),
            P(("dp", "tensor"), None),
            P(None, "dp", "tensor"),
            P(None, "dp", "tensor"),
            P(None, "dp", "tensor"),
            P(None, "dp", "tensor"),
            P(None, "dp", None, "tensor"),
            P(None, "dp", None, "tensor"),
            P(None, "dp", None, "tensor"),
            P(),
            P(),
            P(),
            P(),
        ),
        check_vma=False,
    )
```

profile of v0, /device:TPU:0, one launch (start us, length us, event | category | flops | bytes accessed | tf_op | source)
XLA Modules:
  0.0 2111.9 jit_solution(8257193522748775564)
XLA Ops:
  19.9 30.9 %all-gather.29.cloned.1.call-done = bf16[1,2048,256]{2,1,0:T(8,128)(2,1)} async-done(((bf16[1,128,256]{2,1,0:T(8,128)(2,1)}), bf16[1,2048,256]{2,1,0:T(8,128)(2,1)}) %all-gather.29.cloned.1.call-update) | async-done | bytes 1048592 | tf_op jit(solution)/shard_map/all_gather | solution.py:66
  50.9 57.8 %all-gather.19.cloned.1.call-done = bf16[1024,2048]{1,0:T(8,128)(2,1)} async-done(((bf16[512,2048]{1,0:T(8,128)(2,1)}), bf16[1024,2048]{1,0:T(8,128)(2,1)}) %all-gather.19.cloned.1.call-update) | async-done | bytes 4194320 | tf_op jit(solution)/shard_map/all_gather | solution.py:72
  117.0 31.8 %all-gather.27.cloned.1.call-done = bf16[1,2048,256]{2,1,0:T(8,128)(2,1)} async-done(((bf16[1,128,256]{2,1,0:T(8,128)(2,1)}), bf16[1,2048,256]{2,1,0:T(8,128)(2,1)}) %all-gather.27.cloned.1.call-update) | async-done | bytes 1048592 | tf_op jit(solution)/shard_map/all_gather | solution.py:66
  153.4 71.3 %all-gather.31.cloned.1.call-done = bf16[1,2048,2048]{2,1,0:T(8,128)(2,1)} async-done(((bf16[1,128,2048]{2,1,0:T(8,128)(2,1)}), bf16[1,2048,2048]{2,1,0:T(8,128)(2,1)}) %all-gather.31.cloned.1.call-update) | async-done | bytes 8388624 | tf_op jit(solution)/shard_map/all_gather | solution.py:66
  224.7 12.6 fusion.19
  255.0 14.4 fusion.116
  269.3 13.3 exponential_reduce_fusion
  282.6 13.7 fusion.117
  296.4 13.3 exponential_reduce_fusion.1
  309.7 13.1 fusion.7
  328.6 19.3 fusion.6
  357.3 13.7 fusion.55
  371.9 52.1 %reduce-scatter.6.cloned.1.call-done = bf16[512,2048]{1,0:T(8,128)(2,1)} async-done(((bf16[1024,2048]{1,0:T(8,128)(2,1)}), bf16[512,2048]{1,0:T(8,128)(2,1)}) %reduce-scatter.6.cloned.1.call-update) | async-done | bytes 2097168 | tf_op jit(solution)/shard_map/reduce_scatter | solution.py:76
  451.7 30.7 %all-gather.23.cloned.1.call-done = bf16[1024,2048]{1,0:T(8,128)(2,1)} async-done(((bf16[512,2048]{1,0:T(8,128)(2,1)}), bf16[1024,2048]{1,0:T(8,128)(2,1)}) %all-gather.23.cloned.1.call-update) | async-done | bytes 4194320 | tf_op jit(solution)/shard_map/all_gather | solution.py:82
  482.4 21.2 %gather_fusion.1 = bf16[2304,2048]{1,0:T(8,128)(2,1)} fusion(bf16[1024,2048]{1,0:T(8,128)(2,1)} %all-gather.23.cloned.1.call-done, s32[3072]{0:T(1024)S(1)} %pad_clamp_fusion), kind=kCustom, calls=%fused_computation.1 | custom fusion | bytes 18883584 | tf_op jit(solution)/shard_map/gather | solution.py:210
  503.6 37.8 %all-gather.21.cloned.1.call-done = bf16[1024,2048]{1,0:T(8,128)(2,1)} async-done(((bf16[512,2048]{1,0:T(8,128)(2,1)}), bf16[1024,2048]{1,0:T(8,128)(2,1)}) %all-gather.21.cloned.1.call-update) | async-done | bytes 4194320 | tf_op jit(solution)/shard_map/all_gather | solution.py:72
  541.4 21.0 gather_fusion
  562.4 44.1 %all-gather.35.cloned.1.call-done = bf16[1,2048,4,384]{3,1,2,0:T(8,128)(2,1)} async-done(((bf16[1,128,4,384]{3,1,2,0:T(8,128)(2,1)}), bf16[1,2048,4,384]{3,1,2,0:T(8,128)(2,1)}) %all-gather.35.cloned.1.call-update) | async-done | bytes 6291472 | tf_op jit(solution)/shard_map/all_gather | solution.py:66
  617.1 52.3 %all-gather.37.cloned.1.call-done = bf16[1,2048,4,384]{3,1,2,0:T(8,128)(2,1)} async-done(((bf16[1,128,4,384]{3,1,2,0:T(8,128)(2,1)}), bf16[1,2048,4,384]{3,1,2,0:T(8,128)(2,1)}) %all-gather.37.cloned.1.call-update) | async-done | bytes 6291472 | tf_op jit(solution)/shard_map/all_gather | solution.py:66
  680.1 52.4 %all-gather.39.cloned.1.call-done = bf16[1,2048,4,384]{3,1,2,0:T(8,128)(2,1)} async-done(((bf16[1,128,4,384]{3,1,2,0:T(8,128)(2,1)}), bf16[1,2048,4,384]{3,1,2,0:T(8,128)(2,1)}) %all-gather.39.cloned.1.call-update) | async-done | bytes 6291472 | tf_op jit(solution)/shard_map/all_gather | solution.py:66
  732.5 12.8 multiply_convert_fusion.1
  745.3 12.6 fusion.28
  757.8 15.0 convolution_add_fusion
  772.9 37.3 %scatter_custom_fusion.3 = f32[1024,2048]{1,0:T(8,128)} fusion(s32[2304]{0:T(1024)S(1)} %compare_select_fusion.1, f32[2304,2048]{1,0:T(8,128)} %bitcast.310, f32[]{:T(128)} %constant.24.clone.1), kind=kCustom, calls=%fused_computation.98 | custom fusion | flops 4718592 | bytes 8389120 | tf_op jit(solution)/shard_map/scatter-add | solution.py:226
  816.3 53.0 %reduce-scatter.10.cloned.1.call-done = bf16[512,2048]{1,0:T(8,128)(2,1)} async-done(((bf16[1024,2048]{1,0:T(8,128)(2,1)}), bf16[512,2048]{1,0:T(8,128)(2,1)}) %reduce-scatter.10.cloned.1.call-update) | async-done | bytes 2097168 | tf_op jit(solution)/shard_map/reduce_scatter | solution.py:86
  878.0 24.2 %copy.140 = bf16[2,8,512,1024]{3,1,0,2:T(8,128)(2,1)} copy(bf16[2,8,512,1024]{2,3,1,0:T(8,128)(2,1)} %copy-done) | data formatting | bytes 33554432 | tf_op jit(solution)/shard_map/convert_element_type | solution.py:131
  902.2 23.9 %copy.139 = bf16[2,8,512,1024]{3,1,0,2:T(8,128)(2,1)} copy(bf16[2,8,512,1024]{2,3,1,0:T(8,128)(2,1)} %fusion.6) | data formatting | bytes 33554432 | tf_op jit(solution)/shard_map/convert_element_type | solution.py:131
  933.7 12.5 fusion.58
  948.7 22.3 %fusion = (f32[2,8,512]{2,1,0:T(8,128)S(1)}, f32[2,1024,512,8]{2,1,3,0:T(8,128)}) fusion(f32[2,8,512,1024]{2,3,1,0:T(8,128)} %get-tuple-element.106, f32[2,8,512]{2,1,0:T(8,128)S(1)} %copy-done.37, bf16[1024,2,128,1]{0,2,3,1:T(8,128)(2,1)S(1)} %bitcast.326, bf16[512,2,8,128]{3,2,1,0:T(8,128)(2,1)S(1)} %bitcast.307), kind=kOutput, calls=%fused_computation.8 | convolution fusion | flops 2172641280 | bytes 69795840 | tf_op jit(solution)/shard_map/qkgh,pkh->kgqp/dot_general | solution.py:246
  982.5 22.3 %fusion.3 = (f32[2,8,512]{2,1,0:T(8,128)S(1)}, f32[2,1024,512,8]{2,1,3,0:T(8,128)}) fusion(f32[2,8,512,1024]{2,3,1,0:T(8,128)} %get-tuple-element.108, f32[2,8,512]{2,1,0:T(8,128)S(1)} %copy-done.39, bf16[1024,2,128,1]{0,2,3,1:T(8,128)(2,1)S(1)} %bitcast.327, bf16[512,2,8,128]{3,2,1,0:T(8,128)(2,1)S(1)} %bitcast.300), kind=kOutput, calls=%fused_computation.13 | convolution fusion | flops 2172641280 | bytes 69795840 | tf_op jit(solution)/shard_map/qkgh,pkh->kgqp/dot_general | solution.py:246
  1004.8 28.3 %fusion.5 = bf16[2,8,512,1024]{2,3,1,0:T(8,128)(2,1)} fusion(f32[2,1024,512,8]{2,1,3,0:T(8,128)} %get-tuple-element.110, f32[2,8,512,1024]{2,3,1,0:T(8,128)} %get-tuple-element.108, f32[2,8,512]{2,1,0:T(8,128)S(1)} %get-tuple-element.109, f32[2,8,512]{2,1,0:T(8,128)S(1)} %copy-done.39), kind=kLoop, calls=%fused_computation.15 | loop fusion | flops 33554432 | bytes 83951616 | tf_op jit(solution)/shard_map/convert_element_type | solution.py:250
  1043.6 11.2 fusion.71
  1054.8 28.5 %fusion.2 = bf16[2,8,512,1024]{2,3,1,0:T(8,128)(2,1)} fusion(f32[2,1024,512,8]{2,1,3,0:T(8,128)} %get-tuple-element.112, f32[2,8,512,1024]{2,3,1,0:T(8,128)} %get-tuple-element.106, f32[2,8,512]{2,1,0:T(8,128)S(1)} %get-tuple-element.111, f32[2,8,512]{2,1,0:T(8,128)S(1)} %copy-done.37), kind=kLoop, calls=%fused_computation.10 | loop fusion | flops 33554432 | bytes 83951616 | tf_op jit(solution)/shard_map/convert_element_type | solution.py:250
  1120.3 22.3 %multiply_subtract_fusion = (f32[1024,16,64]{2,1,0:T(8,128)}, f32[1024,16,64]{2,1,0:T(8,128)}) fusion(f32[512,16,128]{2,1,0:T(8,128)} %copy.129, f32[512,16,128]{2,1,0:T(8,128)} %copy.128, f32[1024,64]{1,0:T(8,128)S(1)} %copy-done.23, f32[1024,64]{1,0:T(8,128)S(1)} %copy-done.12), kind=kLoop, calls=%fused_computation.55 | loop fusion | flops 9437184 | bytes 17301504 | tf_op jit(solution)/shard_map/sub | solution.py:43
  1142.7 13.4 multiply_reduce_fusion
  1186.4 22.6 %fusion.12 = (f32[2048]{0:T(1024)S(1)}, bf16[1024,2048]{1,0:T(8,128)(2,1)}) fusion(f32[1024,2048]{1,0:T(8,128)} %copy-done.6, f32[128,8,16,128]{3,2,1,0:T(8,128)} %bitcast.302, f32[128,8,16,128]{3,2,1,0:T(8,128)} %bitcast.304, f32[128,8,16,128]{3,2,1,0:T(8,128)} %bitcast.305, f32[128,8,16,128]{3,2,1,0:T(8,128)} %bitcast.306, f32[2048]{0:T(1024)S(1)} %copy-done.56), kind=kLoop, calls=%fused_computation.40 | loop fusion | flops 18872320 | bytes 46153728 | tf_op jit(solution)/shard_map/reduce_sum | solution.py:35
  1216.3 15.4 add_convert_fusion
  1233.2 12.3 fusion.23
  1245.5 37.5 %scatter_custom_fusion.2 = f32[1024,2048]{1,0:T(8,128)} fusion(s32[2304]{0:T(1024)} %copy-done.61, f32[2304,2048]{1,0:T(8,128)} %bitcast.309, f32[]{:T(128)} %constant.24.clone.1), kind=kCustom, calls=%fused_computation.100 | custom fusion | flops 4718592 | bytes 8389120 | tf_op jit(solution)/shard_map/scatter-add | solution.py:154
  1300.2 11.4 fusion.119
  1311.6 11.5 fusion.120
  1323.2 11.6 convolution_dynamic-update-slice_fusion.1
  1341.8 11.6 convolution_dynamic-update-slice_fusion
  1353.4 11.4 constant_dynamic-update-slice_fusion.2
  1364.8 11.3 constant_dynamic-update-slice_fusion.1
  1376.1 11.3 constant_dynamic-update-slice_fusion
  1392.3 39.8 %all-reduce = (f32[1,2048]{1,0:T(1,128)}, f32[1,2048]{1,0:T(1,128)}, f32[1,128]{1,0:T(1,128)}, f32[1,128]{1,0:T(1,128)}) all-reduce(f32[1,2048]{1,0:T(1,128)S(1)} %bitcast.348, f32[1,2048]{1,0:T(1,128)S(1)} %bitcast.347, f32[1,128]{1,0:T(1,128)S(1)} %bitcast.359, ...), channel_id=1, replica_groups=mesh['dp'=16,'tensor'=2] {'dp','tensor'}, use_global_device_ids=true, to_apply=%region_27.28 | all-reduce | flops 4352 | bytes 34816 | tf_op jit(solution)/shard_map/psum | solution.py:390
  1441.9 651.3 %reduce-scatter.14.cloned.1.call-done = f32[128,9216]{0,1:T(8,128)} async-done(((f32[2048,9216]{0,1:T(8,128)}), f32[128,9216]{0,1:T(8,128)}) %reduce-scatter.14.cloned.1.call-update) | async-done | bytes 4718608 | tf_op jit(solution)/shard_map/reduce_scatter | solution.py:302
  (291 shorter events, 281.5 us)
Async XLA Ops:
  7.2 43.7 %all-gather.29.cloned.1.call-start = ((), (), s32[]{:S(2)}) async-start(), calls=%async_computation.15 | async-start | bytes 1114112 | tf_op jit(solution)/shard_map/all_gather | solution.py:66
  7.9 100.8 %all-gather.19.cloned.1.call-start = ((), (), s32[]{:S(2)}) async-start(), calls=%async_computation.5 | async-start | bytes 6291456 | tf_op jit(solution)/shard_map/all_gather | solution.py:72
  14.7 134.1 %all-gather.27.cloned.1.call-start = ((), (), s32[]{:S(2)}) async-start(), calls=%async_computation.14 | async-start | bytes 1114112 | tf_op jit(solution)/shard_map/all_gather | solution.py:66
  15.4 209.3 %all-gather.31.cloned.1.call-start = ((), (), s32[]{:S(2)}) async-start(), calls=%async_computation.16 | async-start | bytes 8912896 | tf_op jit(solution)/shard_map/all_gather | solution.py:66
  16.0 341.3 %all-gather.33.cloned.1.call-start = ((), (), s32[]{:S(2)}) async-start(), calls=%async_computation.17 | async-start | bytes 8912896 | tf_op jit(solution)/shard_map/all_gather | solution.py:66
  16.6 407.4 %reduce-scatter.6.cloned.1.call-start = ((), (), s32[]{:S(2)}) async-start(), calls=%async_computation.6 | async-start | bytes 6291456 | tf_op jit(solution)/shard_map/reduce_scatter | solution.py:76
  19.5 96.7 %copy-start.24 = (f32[1024,64]{1,0:T(8,128)}, f32[1024,64]{1,0:T(8,128)S(1)}, u32[]{:S(2)}) copy-start(f32[1024,64]{1,0:T(8,128)S(1)} %get-tuple-element.101) | copy-start | bytes 786436
  19.5 228.9 %copy-start.11 = (f32[1024,64]{1,0:T(8,128)}, f32[1024,64]{1,0:T(8,128)S(1)}, u32[]{:S(2)}) copy-start(f32[1024,64]{1,0:T(8,128)S(1)} %get-tuple-element.102) | copy-start | bytes 786436
  19.9 95.8 %copy-start.67 = (f32[1,128]{1,0:T(1,128)S(1)}, f32[1,128]{1,0:T(1,128)}, u32[]{:S(2)}) copy-start(f32[1,128]{1,0:T(1,128)} %param.29) | copy-start | bytes 1540
  115.0 38.4 %copy-start.13 = (f32[1024,2,128]{2,0,1:T(8,128)}, f32[1024,2,128]{2,0,1:T(8,128)S(1)}, u32[]{:S(2)}) copy-start(f32[1024,2,128]{2,0,1:T(8,128)S(1)} %copy.108) | copy-start | bytes 3145732
  117.0 165.6 %copy-start.9 = (bf16[1024,2,128,1]{2,0,3,1:T(8,128)(2,1)}, bf16[1024,2,128,1]{2,0,3,1:T(8,128)(2,1)S(1)}, u32[]{:S(2)}) copy-start(bf16[1024,2,128,1]{2,0,3,1:T(8,128)(2,1)S(1)} %maximum_bitcast_fusion) | copy-start | bytes 1572868
  253.8 15.5 copy-start.17
  253.9 15.5 copy-start.19
  282.6 27.0 %copy-start.36 = (f32[2,8,512]{2,1,0:T(8,128)}, f32[2,8,512]{2,1,0:T(8,128)S(1)}, u32[]{:S(2)}) copy-start(f32[2,8,512]{2,1,0:T(8,128)S(1)} %log_add_fusion) | copy-start | bytes 98308
  309.7 15.5 copy-start.38
  309.7 13.1 copy-start.15
  328.6 28.7 %copy-start.28 = (bf16[2,128,8,512]{3,1,2,0:T(8,128)(2,1)}, bf16[2,128,8,512]{3,1,2,0:T(8,128)(2,1)S(1)}, u32[]{:S(2)}) copy-start(bf16[2,128,8,512]{3,1,2,0:T(8,128)(2,1)S(1)} %convolution_convert_fusion) | copy-start | bytes 6291460
  371.0 52.9 %copy-start.2 = (bf16[512,2048]{1,0:T(8,128)(2,1)S(1)}, bf16[512,2048]{1,0:T(8,128)(2,1)}, u32[]{:S(2)}) copy-start(bf16[512,2048]{1,0:T(8,128)(2,1)} %param.15) | copy-start | bytes 6291460
  371.0 55.4 %copy-start.44 = (f32[1,2048]{1,0:T(1,128)S(1)}, f32[1,2048]{1,0:T(1,128)}, u32[]{:S(2)}) copy-start(f32[1,2048]{1,0:T(1,128)} %param.27) | copy-start | bytes 24580
  371.1 111.3 %all-gather.23.cloned.1.call-start = ((), (), s32[]{:S(2)}) async-start(), calls=%async_computation.9 | async-start | bytes 6291456 | tf_op jit(solution)/shard_map/all_gather | solution.py:82
  371.8 169.5 %all-gather.21.cloned.1.call-start = ((), (), s32[]{:S(2)}) async-start(), calls=%async_computation.7 | async-start | bytes 6291456 | tf_op jit(solution)/shard_map/all_gather | solution.py:72
  426.5 447.3 %copy-start.49 = (f32[512]{0:T(512)}, f32[512]{0:T(512)S(1)}, u32[]{:S(2)}) copy-start(f32[512]{0:T(512)S(1)} %get-tuple-element.99) | copy-start | bytes 6148
  426.5 447.3 %copy-start.57 = (f32[512]{0:T(512)}, f32[512]{0:T(512)S(1)}, u32[]{:S(2)}) copy-start(f32[512]{0:T(512)S(1)} %get-tuple-element.98) | copy-start | bytes 6148
  428.9 177.5 %all-gather.35.cloned.1.call-start = ((), (), s32[]{:S(2)}) async-start(), calls=%async_computation.18 | async-start | bytes 6684672 | tf_op jit(solution)/shard_map/all_gather | solution.py:66
  429.8 239.6 %all-gather.37.cloned.1.call-start = ((), (), s32[]{:S(2)}) async-start(), calls=%async_computation.19 | async-start | bytes 6684672 | tf_op jit(solution)/shard_map/all_gather | solution.py:66
  430.7 301.8 %all-gather.39.cloned.1.call-start = ((), (), s32[]{:S(2)}) async-start(), calls=%async_computation.20 | async-start | bytes 6684672 | tf_op jit(solution)/shard_map/all_gather | solution.py:66
  431.6 437.7 %reduce-scatter.10.cloned.1.call-start = ((), (), s32[]{:S(2)}) async-start(), calls=%async_computation.10 | async-start | bytes 6291456 | tf_op jit(solution)/shard_map/reduce_scatter | solution.py:86
  451.6 321.2 %copy-start.61 = (s32[2304]{0:T(1024)}, s32[2304]{0:T(1024)S(1)}, u32[]{:S(2)}) copy-start(s32[2304]{0:T(1024)S(1)} %compare_select_fusion.1) | copy-start | bytes 27652
  745.3 12.6 copy-start.34
  816.2 117.5 %all-gather.25.cloned.1.call-start = ((), (), s32[]{:S(2)}) async-start(), calls=%async_computation.11 | async-start | bytes 6291456 | tf_op jit(solution)/shard_map/all_gather | solution.py:82
  876.8 511.4 %reduce-scatter.12.cloned.1.call-start = ((), (), s32[]{:S(2)}) async-start(), calls=%async_computation.12 | async-start | bytes 6291456 | tf_op jit(solution)/shard_map/reduce_scatter | solution.py:86
  971.1 11.4 copy-start.39
  1004.8 28.3 %copy-start.10 = (bf16[1024,2,128,1]{2,0,3,1:T(8,128)(2,1)S(1)}, bf16[1024,2,128,1]{2,0,3,1:T(8,128)(2,1)}, u32[]{:S(2)}) copy-start(bf16[1024,2,128,1]{2,0,3,1:T(8,128)(2,1)} %copy-done.9) | copy-start | bytes 1572868
  1033.1 10.4 copy-start.20
  1093.7 10.5 copy-start.12
  1093.7 10.5 copy-start.23
  1120.3 22.3 %copy-start.66 = (f32[1,128]{1,0:T(1,128)S(1)}, f32[1,128]{1,0:T(1,128)}, u32[]{:S(2)}) copy-start(f32[1,128]{1,0:T(1,128)} %param.28) | copy-start | bytes 1540
  1156.9 11.8 copy-start.22
  1231.8 200.3 %reduce-scatter.8.cloned.1.call-start = ((), (), s32[]{:S(2)}) async-start(), calls=%async_computation.8 | async-start | bytes 6291456 | tf_op jit(solution)/shard_map/reduce_scatter | solution.py:76
  1289.1 11.1 copy-start.35
  1311.5 781.6 %reduce-scatter.14.cloned.1.call-start = ((), (), s32[]{:S(2)}) async-start(), calls=%async_computation.13 | async-start | bytes 80216064 | tf_op jit(solution)/shard_map/reduce_scatter | solution.py:302
  1311.6 11.6 copy-start.26
  1311.6 11.6 copy-start.72
  1387.5 44.6 %copy-start.45 = (f32[1,2048]{1,0:T(1,128)S(1)}, f32[1,2048]{1,0:T(1,128)}, u32[]{:S(2)}) copy-start(f32[1,2048]{1,0:T(1,128)} %param.27) | copy-start | bytes 24580
  1387.5 44.6 %copy-start.50 = (f32[512]{0:T(512)S(1)}, f32[512]{0:T(512)}, u32[]{:S(2)}) copy-start(f32[512]{0:T(512)} %copy-done.49) | copy-start | bytes 6148
  1387.5 44.6 %copy-start.58 = (f32[512]{0:T(512)S(1)}, f32[512]{0:T(512)}, u32[]{:S(2)}) copy-start(f32[512]{0:T(512)} %copy-done.57) | copy-start | bytes 6148
  1387.5 44.6 %copy-start.60 = (f32[512]{0:T(512)S(1)}, f32[512]{0:T(512)}, u32[]{:S(2)}) copy-start(f32[512]{0:T(512)} %copy-done.59) | copy-start | bytes 6148
  1387.5 44.6 %copy-start.63 = (f32[512]{0:T(512)S(1)}, f32[512]{0:T(512)}, u32[]{:S(2)}) copy-start(f32[512]{0:T(512)} %get-tuple-element.96) | copy-start | bytes 6148
  (43 other events, 171.1 us)
Sparse Core Ops, SparseCore 0:
  10.2 40.6 all-gather.28
  53.0 55.6 all-gather.18
  110.8 37.9 all-gather.26
  150.8 73.7 all-gather.30
  226.7 73.1 all-gather.32
  371.2 52.7 reduce-scatter.5
  425.6 56.7 all-gather.22
  484.6 56.7 all-gather.20
  544.5 61.9 all-gather.34
  608.8 60.5 all-gather.36
  672.0 60.5 all-gather.38
  816.4 52.8 reduce-scatter.9
  876.9 56.7 all-gather.24
  1231.9 54.2 reduce-scatter.11
  1311.7 54.2 reduce-scatter.7
  1387.7 705.4 reduce-scatter.13
where the time goes:
time: 2120 us; the launch traced here: 2110 us
  waiting for transfers between devices  1180 us (56%)
  matrix products  352 us (17%)
  other arithmetic  318 us (15%)
  local copies, waits for them, and re-layouts  210 us (10%)
  blocking collectives  39.8 us (2%)
    reduce_scatter x1, waiting for transfers between devices, backward_layer(): lax.psum_scatter(jnp.concatenate([jnp.concatenate(attn_parts, axis=1), jn...  651 us
    all_gather x7, waiting for transfers between devices, fetch(): lax.all_gather(for_sending(shards), 'dp', axis=0, tiled=True)  283 us
    all_gather x2, waiting for transfers between devices, rows_gather(): return lax.all_gather(local, 'tensor', axis=0, tiled=True)  95.6 us
    convert_element_type x2, other arithmetic, backward_layer(): grad_scores_b = (probs * (grad_probs - inner)).astype(jnp.bfloat16)  56.8 us
    reduce_scatter x2, waiting for transfers between devices, grads_sum(): lax.psum_scatter(partial_value.astype(jnp.bfloat16), 'tensor', scatter_di...  53 us
    reduce_scatter x2, waiting for transfers between devices, rows_sum(): lax.psum_scatter(partial_value.astype(jnp.bfloat16), 'tensor', scatter_di...  52.1 us
    unnamed x168, local copies, waits for them, and re-layouts  51.3 us
    convert_element_type x2, local copies, waits for them, and re-layouts, forward_layer(): probs_b = jnp.exp(scores - log_total).astype(jnp.bfloat16)  48.1 us
  transfers between devices with their start and end apart: 16, of which 13 were waited for; matrix products, arithmetic and copies ran while one was open for 22% of the time, Pallas kernels for 0%

commit v1 on v0

v1 whole, which is shorter than its diff:
```python
import functools
import math

import jax
import jax.numpy as jnp
import numpy as np
from jax import lax
from jax.experimental import pallas as pl
from jax.experimental.pallas import tpu as pltpu
from jax.sharding import PartitionSpec as P

HD = 128
EPS = 1e-06
SCALE = HD ** -0.5
LOG2E = math.log2(math.e)
NT = (((1,), (1,)), ((), ()))


def head_norm(values, gain, cosine, sine):
    scale = lax.rsqrt(jnp.mean(values * values, axis=-1, keepdims=True) + EPS)
    normed = values * scale * gain
    return normed * cosine + pltpu.roll(normed, HD // 2, 1) * sine, scale


def head_norm_back(values, scale, gain, cosine, sine, grad_rot):
    grad = grad_rot * cosine - pltpu.roll(grad_rot, HD // 2, 1) * sine
    scaled = grad * gain
    inner = jnp.mean(scaled * values, axis=-1, keepdims=True)
    grad_values = scale * scaled - values * (scale * scale * scale) * inner
    return grad_values, jnp.sum(grad * values * scale, axis=0, keepdims=True)


def causal_mask(block):
    key = lax.broadcasted_iota(jnp.int32, (block, block), 0)
    query = lax.broadcasted_iota(jnp.int32, (block, block), 1)
    return key <= query


def attn_fwd_kernel(block, q_ref, k_ref, v_ref, qg_ref, kg_ref, cos_ref, sin_ref, out_ref, lse_ref, qs, ks, vt, ps):
    seq = q_ref.shape[0]

    @pl.when(pl.program_id(1) == 0)
    def _():
        ks[...] = head_norm(k_ref[...], kg_ref[...], cos_ref[...], sin_ref[...])[0].astype(jnp.bfloat16)
        vt[...] = v_ref[...].astype(jnp.bfloat16).T

    qs[...] = head_norm(q_ref[...], qg_ref[...], cos_ref[...], sin_ref[...])[0].astype(jnp.bfloat16)
    mask = causal_mask(block)
    for i in range(seq // block):
        cols = slice(i * block, (i + 1) * block)
        total = jnp.zeros((1, block), jnp.float32)
        for j in range(i + 1):
            rows = slice(j * block, (j + 1) * block)
            scores = lax.dot_general(ks[rows], qs[cols], NT, preferred_element_type=jnp.float32)
            probs = jnp.exp2(scores * (SCALE * LOG2E))
            if j == i:
                probs = jnp.where(mask, probs, 0.0)
            total = total + jnp.sum(probs, axis=0, keepdims=True)
            ps[rows, cols] = probs.astype(jnp.bfloat16)
        lse_ref[0, :, cols] = jnp.log2(total)
        end = (i + 1) * block
        mixed = jnp.dot(vt[:, :end], ps[:end, cols], preferred_element_type=jnp.float32)
        out_ref[cols, :] = (mixed * (1.0 / total)).T.astype(jnp.bfloat16)


def attention_fwd(raw, q_cols, kv_cols, query_g, key_g, cosine, sine):
    seq = raw.shape[0]
    heads, kv = q_cols // HD, kv_cols // HD
    group = heads // kv
    block = min(256, seq)
    head = pl.BlockSpec((seq, HD), lambda k, g: (0, k * group + g))
    key = pl.BlockSpec((seq, HD), lambda k, g: (0, k))
    key_in = pl.BlockSpec((seq, HD), lambda k, g: (0, heads + k))
    value_in = pl.BlockSpec((seq, HD), lambda k, g: (0, heads + kv + k))
    gain = pl.BlockSpec((1, HD), lambda k, g: (0, 0))
    table = pl.BlockSpec((seq, HD), lambda k, g: (0, 0))
    return pl.pallas_call(
        functools.partial(attn_fwd_kernel, block),
        grid=(kv, group),
        in_specs=[head, key_in, value_in, gain, gain, table, table],
        out_specs=[head, pl.BlockSpec((1, 1, seq), lambda k, g: (k * group + g, 0, 0))],
        out_shape=[
            jax.ShapeDtypeStruct((seq, heads * HD), jnp.bfloat16),
            jax.ShapeDtypeStruct((heads, 1, seq), jnp.float32),
        ],
        scratch_shapes=[
            pltpu.VMEM((seq, HD), jnp.bfloat16),
            pltpu.VMEM((seq, HD), jnp.bfloat16),
            pltpu.VMEM((HD, seq), jnp.bfloat16),
            pltpu.VMEM((seq, seq), jnp.bfloat16),
        ],
        compiler_params=pltpu.CompilerParams(vmem_limit_bytes=40 * 2**20),
    )(raw, raw, raw, query_g, key_g, cosine, sine)


def attn_bwd_kernel(
    block, q_ref, k_ref, v_ref, ctx_ref, grad_ref, lse_ref, qg_ref, kg_ref, cos_ref, sin_ref,
    dq_ref, dk_ref, dv_ref, dqg_ref, dkg_ref,
    qs, ks, kt, vs, ps, ds, dks, dvs,
):
    seq = q_ref.shape[0]
    kv_id, g_id = pl.program_id(0), pl.program_id(1)

    @pl.when(g_id == 0)
    def _():
        rotated = head_norm(k_ref[...], kg_ref[...], cos_ref[...], sin_ref[...])[0].astype(jnp.bfloat16)
        ks[...] = rotated
        kt[...] = rotated.T
        vs[...] = v_ref[...].astype(jnp.bfloat16)
        dks[...] = jnp.zeros_like(dks)
        dvs[...] = jnp.zeros_like(dvs)

    @pl.when((g_id == 0) & (kv_id == 0))
    def _():
        dqg_ref[...] = jnp.zeros_like(dqg_ref)
        dkg_ref[...] = jnp.zeros_like(dkg_ref)

    qs[...] = head_norm(q_ref[...], qg_ref[...], cos_ref[...], sin_ref[...])[0].astype(jnp.bfloat16)
    mask = causal_mask(block)
    count = seq // block
    for i in range(count):
        cols = slice(i * block, (i + 1) * block)
        product = grad_ref[cols].astype(jnp.float32) * ctx_ref[cols].astype(jnp.float32)
        delta = jnp.sum(product.T, axis=0, keepdims=True)
        lse = lse_ref[0, :, cols]
        for j in range(i + 1):
            rows = slice(j * block, (j + 1) * block)
            scores = lax.dot_general(ks[rows], qs[cols], NT, preferred_element_type=jnp.float32)
            probs = jnp.exp2(scores * (SCALE * LOG2E) - lse)
            if j == i:
                probs = jnp.where(mask, probs, 0.0)
            grad_probs = lax.dot_general(vs[rows], grad_ref[cols], NT, preferred_element_type=jnp.float32)
            ps[rows, cols] = probs.astype(jnp.bfloat16)
            ds[rows, cols] = (probs * (grad_probs - delta)).astype(jnp.bfloat16)
    for j in range(count):
        rows = slice(j * block, (j + 1) * block)
        dvs[rows] += jnp.dot(ps[rows, j * block :], grad_ref[j * block :], preferred_element_type=jnp.float32)
        dks[rows] += jnp.dot(ds[rows, j * block :], qs[j * block :], preferred_element_type=jnp.float32)
    gain_sum = jnp.zeros((1, HD), jnp.float32)
    for i in range(count):
        cols = slice(i * block, (i + 1) * block)
        end = (i + 1) * block
        grad_t = jnp.dot(kt[:, :end], ds[:end, cols], preferred_element_type=jnp.float32)
        raw = q_ref[cols]
        scale = lax.rsqrt(jnp.mean(raw * raw, axis=-1, keepdims=True) + EPS)
        grad_raw, part = head_norm_back(raw, scale, qg_ref[...], cos_ref[cols], sin_ref[cols], grad_t.T * SCALE)
        dq_ref[cols] = grad_raw.astype(jnp.bfloat16)
        gain_sum = gain_sum + part
    dqg_ref[...] += gain_sum

    @pl.when(g_id == pl.num_programs(1) - 1)
    def _():
        raw = k_ref[...]
        scale = lax.rsqrt(jnp.mean(raw * raw, axis=-1, keepdims=True) + EPS)
        grad_raw, part = head_norm_back(raw, scale, kg_ref[...], cos_ref[...], sin_ref[...], dks[...] * SCALE)
        dk_ref[...] = grad_raw.astype(jnp.bfloat16)
        dv_ref[...] = dvs[...].astype(jnp.bfloat16)
        dkg_ref[...] += part


def attention_bwd(raw, q_cols, kv_cols, context, grad_context, lse, query_g, key_g, cosine, sine):
    seq = raw.shape[0]
    heads, kv = q_cols // HD, kv_cols // HD
    group = heads // kv
    block = min(256, seq)
    head = pl.BlockSpec((seq, HD), lambda k, g: (0, k * group + g))
    key = pl.BlockSpec((seq, HD), lambda k, g: (0, k))
    key_in = pl.BlockSpec((seq, HD), lambda k, g: (0, heads + k))
    value_in = pl.BlockSpec((seq, HD), lambda k, g: (0, heads + kv + k))
    gain = pl.BlockSpec((1, HD), lambda k, g: (0, 0))
    table = pl.BlockSpec((seq, HD), lambda k, g: (0, 0))
    return pl.pallas_call(
        functools.partial(attn_bwd_kernel, block),
        grid=(kv, group),
        in_specs=[head, key_in, value_in, head, head, pl.BlockSpec((1, 1, seq), lambda k, g: (k * group + g, 0, 0)),
                  gain, gain, table, table],
        out_specs=[head, key, key, gain, gain],
        out_shape=[
            jax.ShapeDtypeStruct((seq, heads * HD), jnp.bfloat16),
            jax.ShapeDtypeStruct((seq, kv * HD), jnp.bfloat16),
            jax.ShapeDtypeStruct((seq, kv * HD), jnp.bfloat16),
            jax.ShapeDtypeStruct((1, HD), jnp.float32),
            jax.ShapeDtypeStruct((1, HD), jnp.float32),
        ],
        scratch_shapes=[
            pltpu.VMEM((seq, HD), jnp.bfloat16),
            pltpu.VMEM((seq, HD), jnp.bfloat16),
            pltpu.VMEM((HD, seq), jnp.bfloat16),
            pltpu.VMEM((seq, HD), jnp.bfloat16),
            pltpu.VMEM((seq, seq), jnp.bfloat16),
            pltpu.VMEM((seq, seq), jnp.bfloat16),
            pltpu.VMEM((seq, HD), jnp.float32),
            pltpu.VMEM((seq, HD), jnp.float32),
        ],
        compiler_params=pltpu.CompilerParams(vmem_limit_bytes=48 * 2**20),
    )(raw, raw, raw, context, grad_context, lse, query_g, key_g, cosine, sine)


def rope_tables(seq):
    position = lax.iota(jnp.float32, seq)
    freq = 1000000.0 ** (-2.0 * lax.iota(jnp.float32, HD // 2) / HD)
    angle = position[:, None] * freq[None, :]
    cosine, sine = jnp.cos(angle), jnp.sin(angle)
    return jnp.concatenate([cosine, cosine], axis=1), jnp.concatenate([-sine, sine], axis=1)

BF = jnp.bfloat16
F32 = jnp.float32


def dot(left, right):
    return jnp.dot(left, right, preferred_element_type=F32)


def dot_nt(left, right):
    return lax.dot_general(left, right, (((1,), (1,)), ((), ())), preferred_element_type=F32)


def dot_tn(left, right):
    return lax.dot_general(left, right, (((0,), (0,)), ((), ())), preferred_element_type=F32)


def bits_of(count):
    return count.bit_length() - 1


def swap(value, bit):
    count = lax.axis_size("dp")
    return lax.ppermute(value, "dp", [(i, i ^ (1 << bit)) for i in range(count)])


def swap_pair(value):
    return lax.ppermute(value, "tensor", [(0, 1), (1, 0)])


def block_order():
    count = lax.axis_size("dp")
    bits = bits_of(count)
    reverse = np.array([int(format(i, "b").zfill(bits)[::-1], 2) if bits else 0 for i in range(count)], np.int32)
    me = lax.axis_index("dp").astype(jnp.int32)
    return jnp.asarray(reverse) ^ me, jnp.asarray(reverse)[lax.iota(jnp.int32, count) ^ me]


def copy_kernel(order_ref, in_ref, out_ref):
    out_ref[...] = in_ref[...]


def reorder(values, order):
    rows, width = values.shape
    count = order.shape[0]
    block = width // count
    if block % 128 or rows % 16:
        return jnp.take(values.reshape(rows, count, block), order, axis=1).reshape(rows, width)
    return pl.pallas_call(
        copy_kernel,
        grid_spec=pltpu.PrefetchScalarGridSpec(
            num_scalar_prefetch=1,
            grid=(count,),
            in_specs=[pl.BlockSpec((rows, block), lambda i, order_ref: (0, order_ref[i]))],
            out_specs=pl.BlockSpec((rows, block), lambda i, order_ref: (0, i)),
        ),
        out_shape=jax.ShapeDtypeStruct(values.shape, values.dtype),
    )(order, values)


def gather_rows(shard):
    block = shard
    for bit in reversed(range(bits_of(lax.axis_size("dp")))):
        block = jnp.concatenate([block, swap(block, bit)], axis=0)
    return block


def reduce_rows(left, right):
    bits = bits_of(lax.axis_size("dp"))
    half = left.shape[1] // 2
    received = swap(dot_tn(left[:, half:], right).astype(BF), 0)
    keep = dot_tn(left[:, :half], right) + received.astype(F32)
    for bit in range(1, bits):
        half = keep.shape[0] // 2
        received = swap(keep[half:].astype(BF), bit)
        keep = keep[:half] + received.astype(F32)
        if bit < bits - 1:
            keep = keep.astype(BF).astype(F32)
    return keep


def sum_all(value):
    for bit in range(bits_of(lax.axis_size("dp"))):
        value = value + swap(value, bit)
    return value + swap_pair(value)


def both_rows(own, turn):
    other = swap_pair(own)
    return jnp.where(turn == 0, jnp.concatenate([own, other], axis=0), jnp.concatenate([other, own], axis=0))


def rms_scale(values):
    return lax.rsqrt(jnp.mean(values * values, axis=-1, keepdims=True) + EPS)


def norm_back(values, scale, gain, grad):
    scaled = grad * gain
    inner = jnp.mean(scaled * values, axis=-1, keepdims=True)
    grad_values = scale * scaled - values * (scale * scale * scale) * inner
    return (grad_values, jnp.sum(grad * values * scale, axis=0, keepdims=True))


def body(
    tokens, cotangent, routes, route_weights, query_weight, key_weight, value_weight, out_weight,
    gate_weight, up_weight, down_weight, attn_gain, ffn_gain, query_gain, key_gain,
):
    turn = lax.axis_index("tensor")
    own = tokens.shape[0]
    seq = 2 * own
    width = tokens.shape[1]
    order, inverse = block_order()
    cosine, sine = rope_tables(seq)
    experts, hidden_cols = gate_weight.shape[2], gate_weight.shape[3]
    flat = experts * hidden_cols
    q_cols, kv_cols = query_weight.shape[2], key_weight.shape[2]

    def mine(values):
        return lax.dynamic_slice_in_dim(values, turn * own, own, axis=0)

    def theirs(values):
        return lax.dynamic_slice_in_dim(values, (1 - turn) * own, own, axis=0)

    qkv_w = gather_rows(jnp.concatenate([query_weight[0], key_weight[0], value_weight[0]], axis=1))
    out_w = gather_rows(out_weight[0])
    down_w = gather_rows(down_weight[0].reshape(-1, flat))
    gate_up_w = gather_rows(
        jnp.concatenate([gate_weight[0].reshape(-1, flat), up_weight[0].reshape(-1, flat)], axis=1)
    )

    tokens_all = reorder(both_rows(tokens, turn), order)
    grad_b = reorder(both_rows(cotangent, turn), order)
    attn_g = reorder(attn_gain, order)
    ffn_g = reorder(ffn_gain, order)

    resid = tokens_all.astype(F32)
    scale_one = rms_scale(resid)
    normed = (resid * scale_one * attn_g).astype(BF)
    raw = dot(normed, qkv_w)
    context, lse = attention_fwd(raw, q_cols, kv_cols, query_gain, key_gain, cosine, sine)

    share = jnp.sum(
        route_weights[0][:, :, None] * (routes[0][:, :, None] == lax.iota(jnp.int32, experts)).astype(F32), axis=1
    )
    share = jnp.broadcast_to(share[:, :, None], (seq, experts, hidden_cols)).reshape(seq, flat)
    grad_hidden = dot(grad_b, down_w)

    chunk = seq // 2
    mids = []
    for start in range(0, seq, chunk):
        part = dot_nt(context[start : start + chunk], out_w)
        mids.append(resid[start : start + chunk] + part + swap_pair(part.astype(BF)).astype(F32))
    mid = jnp.concatenate(mids, axis=0)
    scale_two = rms_scale(mid)
    normed_f = (mid * scale_two * ffn_g).astype(BF)
    gate_up = dot(normed_f, gate_up_w)
    gate, up = gate_up[:, :flat], gate_up[:, flat:]
    sigma = jax.nn.sigmoid(gate)
    hidden = (gate * sigma * up * share).astype(BF)
    shared = grad_hidden * share
    grad_gate = (shared * up * sigma * (1.0 + gate * (1.0 - sigma))).astype(BF)
    grad_up = (shared * (gate * sigma)).astype(BF)
    grad_gate_up = jnp.concatenate([grad_gate, grad_up], axis=1)

    grads_mid = []
    ffn_part = jnp.zeros((1, width), F32)
    for start in range(0, seq, chunk):
        rows = slice(start, start + chunk)
        part = dot_nt(grad_gate_up[rows], gate_up_w)
        total = part + swap_pair(part.astype(BF)).astype(F32)
        back, gain_part = norm_back(mid[rows], scale_two[rows], ffn_g, total)
        ffn_part = ffn_part + gain_part
        grads_mid.append(grad_b[rows].astype(F32) + back)
    grad_mid = jnp.concatenate(grads_mid, axis=0)
    grad_mid_b = grad_mid.astype(BF)

    gate_up_grad = reduce_rows(normed_f, grad_gate_up)
    down_grad = reduce_rows(grad_b, hidden)
    out_theirs = swap_pair(dot_nt(theirs(hidden), down_w).astype(BF)).astype(F32)
    output = (mine(mid) + dot_nt(mine(hidden), down_w) + out_theirs).astype(BF)

    out_grad = reduce_rows(grad_mid_b, context)
    grad_context = dot(grad_mid_b, out_w).astype(BF)
    dq, dk, dv, query_part, key_part = attention_bwd(
        raw, q_cols, kv_cols, context, grad_context, lse, query_gain, key_gain, cosine, sine
    )
    grad_qkv = jnp.concatenate([dq, dk, dv], axis=1)
    qkv_grad = reduce_rows(normed, grad_qkv)
    normed_theirs = swap_pair(dot_nt(theirs(grad_qkv), qkv_w).astype(BF)).astype(F32)
    grad_normed = dot_nt(mine(grad_qkv), qkv_w) + normed_theirs
    grad_one, attn_part = norm_back(mine(resid), mine(scale_one), attn_g, grad_normed)
    tokens_grad = reorder(mine(grad_mid) + grad_one, inverse)

    small = jnp.concatenate(
        [reorder(attn_part, inverse), reorder(ffn_part * 0.5, inverse), query_part, key_part], axis=1
    )
    small = sum_all(small)
    attn_total, ffn_total = small[:, :width], small[:, width : 2 * width]
    query_total, key_total = small[:, 2 * width : 2 * width + HD], small[:, 2 * width + HD :]

    def expert(values):
        return values.reshape(1, -1, experts, hidden_cols)

    return (
        reorder(output, inverse),
        tokens_grad,
        qkv_grad[None, :, :q_cols],
        qkv_grad[None, :, q_cols : q_cols + kv_cols],
        qkv_grad[None, :, q_cols + kv_cols :],
        out_grad[None],
        expert(gate_up_grad[:, :flat]),
        expert(gate_up_grad[:, flat:]),
        expert(down_grad),
        attn_total,
        ffn_total,
        query_total,
        key_total,
    )


def solution(mesh):
    return jax.shard_map(
        body,
        mesh=mesh,
        in_specs=(
            P(("dp", "tensor"), None),
            P(("dp", "tensor"), None),
            P(None, "dp", None),
            P(None, "dp", None),
            P(None, "dp", "tensor"),
            P(None, "dp", "tensor"),
            P(None, "dp", "tensor"),
            P(None, "dp", "tensor"),
            P(None, "dp", None, "tensor"),
            P(None, "dp", None, "tensor"),
            P(None, "dp", None, "tensor"),
            P(),
            P(),
            P(),
            P(),
        ),
        out_specs=(
            P(("dp", "tensor"), None),
            P(("dp", "tensor"), None),
            P(None, "dp", "tensor"),
            P(None, "dp", "tensor"),
            P(None, "dp", "tensor"),
            P(None, "dp", "tensor"),
            P(None, "dp", None, "tensor"),
            P(None, "dp", None, "tensor"),
            P(None, "dp", None, "tensor"),
            P(),
            P(),
            P(),
            P(),
        ),
        check_vma=False,
    )
```

time: 2120 us -> 1210 us (0.57)
  waiting for transfers between devices: 1180 us -> 602 us
  other arithmetic: 318 us -> 125 us
  matrix products: 352 us -> 217 us
  local copies, waits for them, and re-layouts: 210 us -> 87.4 us
  Pallas kernels: 0 us -> 119 us
  starting transfers between devices: 0.65 us -> 46.2 us
  blocking collectives: 39.8 us -> 0 us
    reduce_scatter x5 -> x0, waiting for transfers between devices: 756 us -> none  [the longest x1 651 us: backward_layer(): lax.psum_scatter(jnp.concatenate([jnp.concatenate(attn_parts, axis=1), jn...]
    ppermute x0 -> x45, waiting for transfers between devices: none -> 602 us  [the longest x36 429 us: swap(): return lax.ppermute(value, 'dp', [(i, i ^ 1 << bit) for i in range(count)])]
    all_gather x11 -> x0, waiting for transfers between devices: 417 us -> none  [the longest x7 283 us: fetch(): lax.all_gather(for_sending(shards), 'dp', axis=0, tiled=True)]
    dot_general x33 -> x20, matrix products: 352 us -> 217 us  [the longest x8 82.6 us: dot_nt(): lax.dot_general(left, right, (((1,), (1,)), ((), ())), preferred_element_...]
    pallas_call x0 -> x6, Pallas kernels: none -> 119 us  [the longest x1 48.8 us: attention_bwd(): pl.pallas_call(functools.partial(attn_bwd_kernel, block), grid=(kv, group...]
    convert_element_type x10 -> x12, other arithmetic: 110 us -> 31.5 us  [the longest x8 18.7 us: reduce_rows(): keep = keep.astype(BF).astype(F32)]
    scatter-add x2 -> x0, other arithmetic: 74.8 us -> none  [the longest x1 37.5 us: forward_layer(): moe_part = jnp.zeros((seq, width), jnp.float32).at[slot_token.reshape(-1)...]
    reduce_sum x14 -> x4, other arithmetic: 81.9 us -> 10.6 us  [the longest x2 7.18 us: rms_scale(): return lax.rsqrt(jnp.mean(values * values, axis=-1, keepdims=True) + EPS)]
  transfers between devices with their start and end apart: 16 -> 45, of which waited for: 13 -> 21; matrix products, arithmetic and copies ran while one was open for 22% -> 25% of each run, Pallas kernels for 0% -> 6%
where the time goes in v1:
time: 1210 us; the launch traced here: 1200 us
  waiting for transfers between devices  602 us (50%)
  matrix products  217 us (18%)
  other arithmetic  125 us (10%)
  Pallas kernels  119 us (10%)
  local copies, waits for them, and re-layouts  87.4 us (7%)
  starting transfers between devices  46.2 us (4%)
    ppermute x36, waiting for transfers between devices, swap(): return lax.ppermute(value, 'dp', [(i, i ^ 1 << bit) for i in range(count)])  429 us
    ppermute x9, waiting for transfers between devices, swap_pair(): return lax.ppermute(value, 'tensor', [(0, 1), (1, 0)])  173 us
    dot_general x8, matrix products, dot_nt(): lax.dot_general(left, right, (((1,), (1,)), ((), ())), preferred_element_...  82.6 us
    dot_general x8, matrix products, dot_tn(): lax.dot_general(left, right, (((0,), (0,)), ((), ())), preferred_element_...  71.1 us
    dot_general x4, matrix products, dot(): return jnp.dot(left, right, preferred_element_type=F32)  63.7 us
    pallas_call x1, Pallas kernels, attention_bwd(): pl.pallas_call(functools.partial(attn_bwd_kernel, block), grid=(kv, group...  48.8 us
    unnamed x151, local copies, waits for them, and re-layouts  43.5 us
    pallas_call x4, Pallas kernels, reorder(): pl.pallas_call(copy_kernel, grid_spec=pltpu.PrefetchScalarGridSpec(num_sc...  43.1 us
  transfers between devices with their start and end apart: 45, of which 21 were waited for; matrix products, arithmetic and copies ran while one was open for 25% of the time, Pallas kernels for 6%

profile of v1, /device:TPU:0, one launch (start us, length us, event | category | flops | bytes accessed | tf_op | source)
XLA Modules:
  0.0 1198.6 jit_solution(5969496988051793786)
XLA Ops:
  22.3 51.1 %collective-permute-done.1 = bf16[128,2560]{1,0:T(8,128)(2,1)S(1)} collective-permute-done((bf16[128,2560]{1,0:T(8,128)(2,1)}, bf16[128,2560]{1,0:T(8,128)(2,1)S(1)}, u32[]{:S(2)}, u32[]{:S(2)}) %collective-permute-start.1) | collective-permute-done | bytes 655392 | tf_op jit(solution)/shard_map/ppermute | solution.py:228
  91.4 45.9 %collective-permute-done.2 = bf16[256,2560]{1,0:T(8,128)(2,1)S(1)} collective-permute-done((bf16[256,2560]{1,0:T(8,128)(2,1)}, bf16[256,2560]{1,0:T(8,128)(2,1)S(1)}, u32[]{:S(2)}, u32[]{:S(2)}) %collective-permute-start.2) | collective-permute-done | bytes 1310752 | tf_op jit(solution)/shard_map/ppermute | solution.py:228
  148.4 13.9 %collective-permute-done.6 = bf16[256,2048]{1,0:T(8,128)(2,1)S(1)} collective-permute-done((bf16[256,2048]{1,0:T(8,128)(2,1)S(1)}, bf16[256,2048]{1,0:T(8,128)(2,1)S(1)}, u32[]{:S(2)}, u32[]{:S(2)}) %collective-permute-start.6) | collective-permute-done | bytes 1048608 | tf_op jit(solution)/shard_map/ppermute | solution.py:228
  167.8 13.1 %collective-permute-done.16 = bf16[256,1536]{1,0:T(8,128)(2,1)S(1)} collective-permute-done((bf16[256,1536]{1,0:T(8,128)(2,1)S(1)}, bf16[256,1536]{1,0:T(8,128)(2,1)S(1)}, u32[]{:S(2)}, u32[]{:S(2)}) %collective-permute-start.16) | collective-permute-done | bytes 786464 | tf_op jit(solution)/shard_map/ppermute | solution.py:228
  185.9 14.9 %collective-permute-done.3 = bf16[512,2560]{1,0:T(8,128)(2,1)S(1)} collective-permute-done((bf16[512,2560]{1,0:T(8,128)(2,1)S(1)}, bf16[512,2560]{1,0:T(8,128)(2,1)S(1)}, u32[]{:S(2)}, u32[]{:S(2)}) %collective-permute-start.3) | collective-permute-done | bytes 2621472 | tf_op jit(solution)/shard_map/ppermute | solution.py:228
  205.9 39.0 %collective-permute-done.7 = bf16[512,2048]{1,0:T(8,128)(2,1)S(1)} collective-permute-done((bf16[512,2048]{1,0:T(8,128)(2,1)S(1)}, bf16[512,2048]{1,0:T(8,128)(2,1)S(1)}, u32[]{:S(2)}, u32[]{:S(2)}) %collective-permute-start.7) | collective-permute-done | bytes 2097184 | tf_op jit(solution)/shard_map/ppermute | solution.py:228
  259.7 11.1 shard_map.255
  270.8 6.7 convert_element_type.174
  281.8 10.9 shard_map.258
  305.3 48.6 %collective-permute-done.13 = bf16[512,3072]{1,0:T(8,128)(2,1)} collective-permute-done((bf16[512,3072]{1,0:T(8,128)(2,1)}, bf16[512,3072]{1,0:T(8,128)(2,1)}, u32[]{:S(2)}, u32[]{:S(2)}) %collective-permute-start.13) | collective-permute-done | bytes 3145760 | tf_op jit(solution)/shard_map/ppermute | solution.py:228
  366.9 16.1 %fusion.71.q_ref.k_ref.v_ref = f32[1024,2560]{1,0:T(8,128)} fusion(bf16[1024,2048]{1,0:T(8,128)(2,1)S(1)} %multiply_convert_fusion.1, bf16[2048,2560]{1,0:T(8,128)(2,1)} %constant_dynamic-update-slice_fusion), kind=kOutput, calls=%fused_computation.199 | convolution fusion | flops 10737418240 | bytes 25165824 | tf_op jit(solution)/shard_map/dot_general | solution.py:211
  383.0 27.0 %shard_map.256 = (bf16[1024,2048]{1,0:T(8,128)(2,1)S(1)}, f32[16,1,1024]{2,1,0:T(1,128)S(1)}) custom-call(f32[1024,2560]{1,0:T(8,128)} %fusion.71.q_ref.k_ref.v_ref, f32[1024,2560]{1,0:T(8,128)} %fusion.71.q_ref.k_ref.v_ref, f32[1024,2560]{1,0:T(8,128)} %fusion.71.q_ref.k_ref.v_ref, f32[1,128]{1,0:T(1,128)S(1)} %copy-done.4, f32[1,128]{1,0:T(1,128)S(1)} %copy-done.5, ...), custom_call_target="tpu_custom_call" | custom-call | tf_op jit(solution)/shard_map/pallas_call | solution.py:77
  410.0 11.3 fusion.68
  422.9 10.2 fusion.67
  448.7 21.4 %collective-permute-done.9 = bf16[512,2048]{1,0:T(8,128)(2,1)} collective-permute-done((bf16[512,2048]{1,0:T(8,128)(2,1)}, bf16[512,2048]{1,0:T(8,128)(2,1)}, u32[]{:S(2)}, u32[]{:S(2)}) %collective-permute-start.9) | collective-permute-done | bytes 2097184 | tf_op jit(solution)/shard_map/ppermute | solution.py:232
  470.1 44.5 %collective-permute-done.10 = bf16[512,2048]{1,0:T(8,128)(2,1)} collective-permute-done((bf16[512,2048]{1,0:T(8,128)(2,1)}, bf16[512,2048]{1,0:T(8,128)(2,1)}, u32[]{:S(2)}, u32[]{:S(2)}) %collective-permute-start.10) | collective-permute-done | bytes 2097184 | tf_op jit(solution)/shard_map/ppermute | solution.py:232
  514.6 13.8 %fusion.11 = (f32[512,2048]{1,0:T(8,128)}, f32[512,2048]{1,0:T(8,128)}) fusion(f32[512,2048]{1,0:T(8,128)} %get-tuple-element.69, f32[1024,2048]{1,0:T(8,128)} %convert_element_type.174, bf16[512,2048]{1,0:T(8,128)(2,1)} %collective-permute-done.10, bf16[512,2048]{1,0:T(8,128)(2,1)} %collective-permute-done.9, f32[512,2048]{1,0:T(8,128)} %get-tuple-element.71), kind=kLoop, calls=%fused_computation.51 | loop fusion | flops 6291456 | bytes 29360128 | tf_op jit(solution)/shard_map/add | solution.py:356
  538.9 15.5 %fusion.72 = f32[1024,3072]{1,0:T(8,128)} fusion(bf16[1024,2048]{1,0:T(8,128)(2,1)S(1)} %multiply_convert_fusion, bf16[2048,3072]{1,0:T(8,128)(2,1)S(1)} %copy-done.53), kind=kOutput, calls=%fused_computation.200 | convolution fusion | flops 12884901888 | bytes 29360128 | tf_op jit(solution)/shard_map/dot_general | solution.py:211
  554.5 17.9 %multiply_convert_fusion.2 = (bf16[1024,1536]{1,0:T(8,128)(2,1)}, bf16[1024,1536]{1,0:T(8,128)(2,1)}, bf16[1024,1536]{1,0:T(8,128)(2,1)}) fusion(f32[1024,3072]{1,0:T(8,128)} %fusion.72, f32[1024,1536]{1,0:T(8,128)} %bitcast.99, bf16[1024,2048]{1,0:T(8,128)(2,1)} %shard_map.258, bf16[2048,1536]{1,0:T(8,128)(2,1)} %constant_dynamic-update-slice_fusion.18), kind=kOutput, calls=%fused_computation.29 | convolution fusion | flops 6469189632 | bytes 38797312 | tf_op jit(solution)/shard_map/dot_general | solution.py:211
  572.4 11.8 fusion.70
  584.2 12.4 %fusion.69 = (bf16[512,2048]{1,0:T(8,128)(2,1)}, f32[512,2048]{1,0:T(8,128)}) fusion(bf16[2048,3072]{1,0:T(8,128)(2,1)} %constant_dynamic-update-slice_fusion.12, bf16[1024,1536]{1,0:T(8,128)(2,1)} %get-tuple-element.37, bf16[1024,1536]{1,0:T(8,128)(2,1)} %get-tuple-element.36), kind=kOutput, calls=%fused_computation.197 | convolution fusion | flops 6449790976 | bytes 25165824 | tf_op jit(solution)/shard_map/dot_general | solution.py:215
  598.6 8.0 convolution_convert_fusion.5
  606.6 11.9 convolution_convert_fusion
  618.5 26.8 %collective-permute-done.21 = bf16[512,2048]{1,0:T(8,128)(2,1)S(1)} collective-permute-done((bf16[512,2048]{1,0:T(8,128)(2,1)}, bf16[512,2048]{1,0:T(8,128)(2,1)S(1)}, u32[]{:S(2)}, u32[]{:S(2)}) %collective-permute-start.21) | collective-permute-done | bytes 2097184 | tf_op jit(solution)/shard_map/ppermute | solution.py:232
  645.3 43.7 %collective-permute-done.22 = bf16[512,2048]{1,0:T(8,128)(2,1)S(1)} collective-permute-done((bf16[512,2048]{1,0:T(8,128)(2,1)}, bf16[512,2048]{1,0:T(8,128)(2,1)S(1)}, u32[]{:S(2)}, u32[]{:S(2)}) %collective-permute-start.22) | collective-permute-done | bytes 2097184 | tf_op jit(solution)/shard_map/ppermute | solution.py:232
  692.3 7.5 subtract_add_fusion
  703.9 14.2 %convolution_convert_fusion.2.grad_ref = bf16[1024,2048]{1,0:T(8,128)(2,1)} fusion(bf16[1024,2048]{1,0:T(8,128)(2,1)S(1)} %fusion, bf16[2048,2048]{1,0:T(8,128)(2,1)} %constant_dynamic-update-slice_fusion.5), kind=kOutput, calls=%fused_computation.69 | convolution fusion | flops 8592031744 | bytes 16777216 | tf_op jit(solution)/shard_map/dot_general | solution.py:211
  718.1 48.8 %shard_map.259 = (bf16[1024,2048]{1,0:T(8,128)(2,1)}, bf16[1024,256]{1,0:T(8,128)(2,1)S(1)}, bf16[1024,256]{1,0:T(8,128)(2,1)S(1)}, f32[1,128]{1,0:T(1,128)S(1)}, f32[1,128]{1,0:T(1,128)S(1)}) custom-call(f32[1024,2560]{1,0:T(8,128)} %fusion.71.q_ref.k_ref.v_ref, f32[1024,2560]{1,0:T(8,128)} %fusion.71.q_ref.k_ref.v_ref, ...), custom_call_target="tpu_custom_call" | custom-call | tf_op jit(solution)/shard_map/pallas_call | solution.py:172
  769.6 7.2 convolution_convert_fusion.6
  778.5 6.8 convolution_convert_fusion.3
  786.9 10.3 convolution_convert_fusion.1
  797.2 28.6 %collective-permute-done.23 = bf16[512,2048]{1,0:T(8,128)(2,1)} collective-permute-done((bf16[512,2048]{1,0:T(8,128)(2,1)}, bf16[512,2048]{1,0:T(8,128)(2,1)}, u32[]{:S(2)}, u32[]{:S(2)}) %collective-permute-start.23) | collective-permute-done | bytes 2097184 | tf_op jit(solution)/shard_map/ppermute | solution.py:232
  825.8 12.6 %multiply_reduce_fusion.4 = (f32[2048]{0:T(1024)S(1)}, f32[512]{0:T(512)S(1)}, f32[512,2048]{1,0:T(8,128)}) fusion(f32[1024,2048]{1,0:T(8,128)} %convert_element_type.174, s32[]{:T(128)S(6)} %select_n.52, f32[512]{0:T(512)S(1)} %copy-done.52, f32[2048]{0:T(1024)S(1)} %copy-done.50, bf16[512,2048]{1,0:T(8,128)(2,1)} %collective-permute-done.23, ...), kind=kOutput, calls=%fused_computation.59 | convolution fusion | flops 5377095168 | bytes 23614464 | tf_op jit(solution)/shard_map/dot_general | solution.py:215
  839.3 9.5 convolution_convert_fusion.4
  860.2 8.4 collective-permute-done.19
  869.8 9.0 fusion.9.in_ref
  878.8 10.3 shard_map.257
  895.4 7.1 fusion.5.in_ref
  902.6 10.8 shard_map.260
  919.6 10.8 convert_add_fusion
  934.0 7.2 convert_add_fusion.2
  945.3 8.4 convert_add_fusion.1
  957.1 91.7 %collective-permute-done.29 = bf16[512,2048]{1,0:T(8,128)(2,1)} collective-permute-done((bf16[512,2048]{1,0:T(8,128)(2,1)}, bf16[512,2048]{1,0:T(8,128)(2,1)}, u32[]{:S(2)}, u32[]{:S(2)}) %collective-permute-start.29) | collective-permute-done | bytes 2097184 | tf_op jit(solution)/shard_map/ppermute | solution.py:228
  1063.1 25.4 %collective-permute-done.30 = bf16[256,2048]{1,0:T(8,128)(2,1)S(1)} collective-permute-done((bf16[256,2048]{1,0:T(8,128)(2,1)S(1)}, bf16[256,2048]{1,0:T(8,128)(2,1)S(1)}, u32[]{:S(2)}, u32[]{:S(2)}) %collective-permute-start.30) | collective-permute-done | bytes 1048608 | tf_op jit(solution)/shard_map/ppermute | solution.py:228
  1091.0 9.2 collective-permute-done.25
  1111.0 19.5 %collective-permute-done.31 = bf16[128,2048]{1,0:T(8,128)(2,1)} collective-permute-done((bf16[128,2048]{1,0:T(8,128)(2,1)}, bf16[128,2048]{1,0:T(8,128)(2,1)}, u32[]{:S(2)}, u32[]{:S(2)}) %collective-permute-start.31) | collective-permute-done | bytes 524320 | tf_op jit(solution)/shard_map/ppermute | solution.py:228
  1139.7 26.8 %collective-permute-done.26 = bf16[256,2560]{1,0:T(8,128)(2,1)} collective-permute-done((bf16[256,2560]{1,0:T(8,128)(2,1)}, bf16[256,2560]{1,0:T(8,128)(2,1)}, u32[]{:S(2)}, u32[]{:S(2)}) %collective-permute-start.26) | collective-permute-done | bytes 1310752 | tf_op jit(solution)/shard_map/ppermute | solution.py:228
  1172.2 24.1 %collective-permute-done.27 = bf16[128,2560]{1,0:T(8,128)(2,1)S(1)} collective-permute-done((bf16[128,2560]{1,0:T(8,128)(2,1)}, bf16[128,2560]{1,0:T(8,128)(2,1)S(1)}, u32[]{:S(2)}, u32[]{:S(2)}) %collective-permute-start.27) | collective-permute-done | bytes 655392 | tf_op jit(solution)/shard_map/ppermute | solution.py:228
  (322 shorter events, 235.0 us)
Async XLA Ops:
  3.1 70.4 %collective-permute-start.1 = (bf16[128,2560]{1,0:T(8,128)(2,1)}, bf16[128,2560]{1,0:T(8,128)(2,1)S(1)}, u32[]{:S(2)}, u32[]{:S(2)}) collective-permute-start(bf16[128,2560]{1,0:T(8,128)(2,1)} %get-tuple-element.47), channel_id=1, source_target_pairs={{0,16},{2,18},{4,20},{6,22},{8,24},{10,26},{12,28},{14,30},{16,0},... | collective-permute-start | bytes 1966088 | tf_op jit(solution)/shard_map/ppermute | solution.py:228
  7.1 246.8 %collective-permute-start = (bf16[512,2048]{1,0:T(8,128)(2,1)}, bf16[512,2048]{1,0:T(8,128)(2,1)}, u32[]{:S(2)}, u32[]{:S(2)}) collective-permute-start(bf16[512,2048]{1,0:T(8,128)(2,1)} %param.18), channel_id=1, source_target_pairs={{0,1},{1,0},{2,3},{3,2},{4,5},{5,4},{6,7},{7,6},{8,9},{9,8},{10,11... | collective-permute-start | bytes 6291464 | tf_op jit(solution)/shard_map/ppermute | solution.py:232
  8.6 79.6 %collective-permute-start.5 = (bf16[128,2048]{1,0:T(8,128)(2,1)}, bf16[128,2048]{1,0:T(8,128)(2,1)}, u32[]{:S(2)}, u32[]{:S(2)}) collective-permute-start(bf16[128,2048]{1,0:T(8,128)(2,1)} %bitcast.95), channel_id=1, source_target_pairs={{0,16},{2,18},{4,20},{6,22},{8,24},{10,26},{12,28},{14,30},{16,0},... | collective-permute-start | bytes 1572872 | tf_op jit(solution)/shard_map/ppermute | solution.py:228
  12.0 151.9 %collective-permute-start.11 = (bf16[128,3072]{1,0:T(8,128)(2,1)}, bf16[128,3072]{1,0:T(8,128)(2,1)S(1)}, u32[]{:S(2)}, u32[]{:S(2)}) collective-permute-start(bf16[128,3072]{1,0:T(8,128)(2,1)} %get-tuple-element.49), channel_id=1, source_target_pairs={{0,16},{2,18},{4,20},{6,22},{8,24},{10,26},{12,28},{14,30},{16,0},... | collective-permute-start | bytes 2359304 | tf_op jit(solution)/shard_map/ppermute | solution.py:228
  15.4 125.6 %collective-permute-start.15 = (bf16[128,1536]{1,0:T(8,128)(2,1)}, bf16[128,1536]{1,0:T(8,128)(2,1)}, u32[]{:S(2)}, u32[]{:S(2)}) collective-permute-start(bf16[128,1536]{1,0:T(8,128)(2,1)} %bitcast.47), channel_id=1, source_target_pairs={{0,16},{2,18},{4,20},{6,22},{8,24},{10,26},{12,28},{14,30},{16,0},... | collective-permute-start | bytes 1179656 | tf_op jit(solution)/shard_map/ppermute | solution.py:228
  75.5 61.8 %collective-permute-start.2 = (bf16[256,2560]{1,0:T(8,128)(2,1)}, bf16[256,2560]{1,0:T(8,128)(2,1)S(1)}, u32[]{:S(2)}, u32[]{:S(2)}) collective-permute-start(bf16[256,2560]{1,0:T(8,128)(2,1)} %pad_maximum_fusion.16), channel_id=1, source_target_pairs={{0,8},{2,10},{4,12},{6,14},{8,0},{10,2},{12,4},{14,6},{16,24},{18,... | collective-permute-start | bytes 3932168 | tf_op jit(solution)/shard_map/ppermute | solution.py:228
  76.8 219.3 %copy-start.49 = (f32[2048]{0:T(1024)}, f32[2048]{0:T(1024)S(1)}, u32[]{:S(2)}) copy-start(f32[2048]{0:T(1024)S(1)} %get-tuple-element.64) | copy-start | bytes 24580
  88.3 189.3 %collective-permute-start.20 = (bf16[512,2048]{1,0:T(8,128)(2,1)}, bf16[512,2048]{1,0:T(8,128)(2,1)}, u32[]{:S(2)}, u32[]{:S(2)}) collective-permute-start(bf16[512,2048]{1,0:T(8,128)(2,1)} %param.19), channel_id=1, source_target_pairs={{0,1},{1,0},{2,3},{3,2},{4,5},{5,4},{6,7},{7,6},{8,9},{9,8},{10,11... | collective-permute-start | bytes 6291464 | tf_op jit(solution)/shard_map/ppermute | solution.py:232
  137.2 25.1 %collective-permute-start.6 = (bf16[256,2048]{1,0:T(8,128)(2,1)S(1)}, bf16[256,2048]{1,0:T(8,128)(2,1)S(1)}, u32[]{:S(2)}, u32[]{:S(2)}) collective-permute-start(bf16[256,2048]{1,0:T(8,128)(2,1)S(1)} %pad_maximum_fusion.17), channel_id=1, source_target_pairs={{0,8},{2,10},{4,12},{6,14},{8,0},{10,2},{12,4},{14,6},{16,24},{18,... | collective-permute-start | bytes 3145736 | tf_op jit(solution)/shard_map/ppermute | solution.py:228
  141.0 59.8 %collective-permute-start.3 = (bf16[512,2560]{1,0:T(8,128)(2,1)S(1)}, bf16[512,2560]{1,0:T(8,128)(2,1)S(1)}, u32[]{:S(2)}, u32[]{:S(2)}) collective-permute-start(bf16[512,2560]{1,0:T(8,128)(2,1)S(1)} %pad_maximum_fusion.12), channel_id=1, source_target_pairs={{0,4},{2,6},{4,0},{6,2},{8,12},{10,14},{12,8},{14,10},{16,20},{18,... | collective-permute-start | bytes 7864328 | tf_op jit(solution)/shard_map/ppermute | solution.py:228
  162.3 18.6 %collective-permute-start.16 = (bf16[256,1536]{1,0:T(8,128)(2,1)S(1)}, bf16[256,1536]{1,0:T(8,128)(2,1)S(1)}, u32[]{:S(2)}, u32[]{:S(2)}) collective-permute-start(bf16[256,1536]{1,0:T(8,128)(2,1)S(1)} %pad_maximum_fusion.18), channel_id=1, source_target_pairs={{0,8},{2,10},{4,12},{6,14},{8,0},{10,2},{12,4},{14,6},{16,24},{18,... | collective-permute-start | bytes 2359304 | tf_op jit(solution)/shard_map/ppermute | solution.py:228
  163.9 80.9 %collective-permute-start.7 = (bf16[512,2048]{1,0:T(8,128)(2,1)S(1)}, bf16[512,2048]{1,0:T(8,128)(2,1)S(1)}, u32[]{:S(2)}, u32[]{:S(2)}) collective-permute-start(bf16[512,2048]{1,0:T(8,128)(2,1)S(1)} %pad_maximum_fusion.13), channel_id=1, source_target_pairs={{0,4},{2,6},{4,0},{6,2},{8,12},{10,14},{12,8},{14,10},{16,20},{18,... | collective-permute-start | bytes 6291464 | tf_op jit(solution)/shard_map/ppermute | solution.py:228
  180.9 68.4 %collective-permute-start.12 = (bf16[256,3072]{1,0:T(8,128)(2,1)S(1)}, bf16[256,3072]{1,0:T(8,128)(2,1)S(1)}, u32[]{:S(2)}, u32[]{:S(2)}) collective-permute-start(bf16[256,3072]{1,0:T(8,128)(2,1)S(1)} %pad_maximum_fusion.14), channel_id=1, source_target_pairs={{0,8},{2,10},{4,12},{6,14},{8,0},{10,2},{12,4},{14,6},{16,24},{18,... | collective-permute-start | bytes 4718600 | tf_op jit(solution)/shard_map/ppermute | solution.py:228
  205.9 156.0 %collective-permute-start.4 = (bf16[1024,2560]{1,0:T(8,128)(2,1)}, bf16[1024,2560]{1,0:T(8,128)(2,1)}, u32[]{:S(2)}, u32[]{:S(2)}) collective-permute-start(bf16[1024,2560]{1,0:T(8,128)(2,1)} %pad_maximum_fusion.4), channel_id=1, source_target_pairs={{0,2},{2,0},{4,6},{6,4},{8,10},{10,8},{12,14},{14,12},{16,18},{18,... | collective-permute-start | bytes 15728648 | tf_op jit(solution)/shard_map/ppermute | solution.py:228
  248.2 108.9 %collective-permute-start.8 = (bf16[1024,2048]{1,0:T(8,128)(2,1)}, bf16[1024,2048]{1,0:T(8,128)(2,1)}, u32[]{:S(2)}, u32[]{:S(2)}) collective-permute-start(bf16[1024,2048]{1,0:T(8,128)(2,1)} %pad_maximum_fusion.5), channel_id=1, source_target_pairs={{0,2},{2,0},{4,6},{6,4},{8,10},{10,8},{12,14},{14,12},{16,18},{18,... | collective-permute-start | bytes 12582920 | tf_op jit(solution)/shard_map/ppermute | solution.py:228
  249.4 47.9 %collective-permute-start.17 = (bf16[512,1536]{1,0:T(8,128)(2,1)}, bf16[512,1536]{1,0:T(8,128)(2,1)}, u32[]{:S(2)}, u32[]{:S(2)}) collective-permute-start(bf16[512,1536]{1,0:T(8,128)(2,1)} %pad_maximum_fusion.15), channel_id=1, source_target_pairs={{0,4},{2,6},{4,0},{6,2},{8,12},{10,14},{12,8},{14,10},{16,20},{18,... | collective-permute-start | bytes 4718600 | tf_op jit(solution)/shard_map/ppermute | solution.py:228
  253.9 100.0 %collective-permute-start.13 = (bf16[512,3072]{1,0:T(8,128)(2,1)}, bf16[512,3072]{1,0:T(8,128)(2,1)}, u32[]{:S(2)}, u32[]{:S(2)}) collective-permute-start(bf16[512,3072]{1,0:T(8,128)(2,1)} %pad_maximum_fusion.10), channel_id=1, source_target_pairs={{0,4},{2,6},{4,0},{6,2},{8,12},{10,14},{12,8},{14,10},{16,20},{18,... | collective-permute-start | bytes 9437192 | tf_op jit(solution)/shard_map/ppermute | solution.py:228
  296.1 137.5 %copy-start.51 = (f32[512]{0:T(512)}, f32[512]{0:T(512)S(1)}, u32[]{:S(2)}) copy-start(f32[512]{0:T(512)S(1)} %dynamic-slice.3) | copy-start | bytes 6148
  302.0 139.8 %collective-permute-start.18 = (bf16[1024,1536]{1,0:T(8,128)(2,1)}, bf16[1024,1536]{1,0:T(8,128)(2,1)}, u32[]{:S(2)}, u32[]{:S(2)}) collective-permute-start(bf16[1024,1536]{1,0:T(8,128)(2,1)} %pad_maximum_fusion.11), channel_id=1, source_target_pairs={{0,2},{2,0},{4,6},{6,4},{8,10},{10,8},{12,14},{14,12},{16,18},{18,... | collective-permute-start | bytes 9437192 | tf_op jit(solution)/shard_map/ppermute | solution.py:228
  357.0 88.6 %collective-permute-start.14 = (bf16[1024,3072]{1,0:T(8,128)(2,1)S(1)}, bf16[1024,3072]{1,0:T(8,128)(2,1)S(1)}, u32[]{:S(2)}, u32[]{:S(2)}) collective-permute-start(bf16[1024,3072]{1,0:T(8,128)(2,1)S(1)} %pad_maximum_fusion.3), channel_id=1, source_target_pairs={{0,2},{2,0},{4,6},{6,4},{8,10},{10,8},{12,14},{14,12},{16,18},{18,... | collective-permute-start | bytes 18874376 | tf_op jit(solution)/shard_map/ppermute | solution.py:228
  421.3 48.7 %collective-permute-start.9 = (bf16[512,2048]{1,0:T(8,128)(2,1)}, bf16[512,2048]{1,0:T(8,128)(2,1)}, u32[]{:S(2)}, u32[]{:S(2)}) collective-permute-start(bf16[512,2048]{1,0:T(8,128)(2,1)} %get-tuple-element.70), channel_id=1, source_target_pairs={{0,1},{1,0},{2,3},{3,2},{4,5},{5,4},{6,7},{7,6},{8,9},{9,8},{10,11... | collective-permute-start | bytes 6291464 | tf_op jit(solution)/shard_map/ppermute | solution.py:232
  433.1 81.5 %collective-permute-start.10 = (bf16[512,2048]{1,0:T(8,128)(2,1)}, bf16[512,2048]{1,0:T(8,128)(2,1)}, u32[]{:S(2)}, u32[]{:S(2)}) collective-permute-start(bf16[512,2048]{1,0:T(8,128)(2,1)} %get-tuple-element.68), channel_id=1, source_target_pairs={{0,1},{1,0},{2,3},{3,2},{4,5},{5,4},{6,7},{7,6},{8,9},{9,8},{10,11... | collective-permute-start | bytes 6291464 | tf_op jit(solution)/shard_map/ppermute | solution.py:232
  596.5 48.7 %collective-permute-start.21 = (bf16[512,2048]{1,0:T(8,128)(2,1)}, bf16[512,2048]{1,0:T(8,128)(2,1)S(1)}, u32[]{:S(2)}, u32[]{:S(2)}) collective-permute-start(bf16[512,2048]{1,0:T(8,128)(2,1)} %get-tuple-element.74), channel_id=1, source_target_pairs={{0,1},{1,0},{2,3},{3,2},{4,5},{5,4},{6,7},{7,6},{8,9},{9,8},{10,11... | collective-permute-start | bytes 6291464 | tf_op jit(solution)/shard_map/ppermute | solution.py:232
  598.1 90.8 %collective-permute-start.22 = (bf16[512,2048]{1,0:T(8,128)(2,1)}, bf16[512,2048]{1,0:T(8,128)(2,1)S(1)}, u32[]{:S(2)}, u32[]{:S(2)}) collective-permute-start(bf16[512,2048]{1,0:T(8,128)(2,1)} %get-tuple-element.72), channel_id=1, source_target_pairs={{0,1},{1,0},{2,3},{3,2},{4,5},{5,4},{6,7},{7,6},{8,9},{9,8},{10,11... | collective-permute-start | bytes 6291464 | tf_op jit(solution)/shard_map/ppermute | solution.py:232
  776.9 48.9 %collective-permute-start.23 = (bf16[512,2048]{1,0:T(8,128)(2,1)}, bf16[512,2048]{1,0:T(8,128)(2,1)}, u32[]{:S(2)}, u32[]{:S(2)}) collective-permute-start(bf16[512,2048]{1,0:T(8,128)(2,1)} %convolution_convert_fusion.6), channel_id=1, source_target_pairs={{0,1},{1,0},{2,3},{3,2},{4,5},{5,4},{6,7},{7,6},{8,9},{9,8},{10,11... | collective-permute-start | bytes 6291464 | tf_op jit(solution)/shard_map/ppermute | solution.py:232
  785.2 64.2 %collective-permute-start.36 = (bf16[1024,1536]{1,0:T(8,128)(2,1)}, bf16[1024,1536]{1,0:T(8,128)(2,1)}, u32[]{:S(2)}, u32[]{:S(2)}) collective-permute-start(bf16[1024,1536]{1,0:T(8,128)(2,1)} %convolution_convert_fusion.3), channel_id=1, source_target_pairs={{0,2},{2,0},{4,6},{6,4},{8,10},{10,8},{12,14},{14,12},{16,18},{18,... | collective-permute-start | bytes 9437192 | tf_op jit(solution)/shard_map/ppermute | solution.py:228
  785.2 134.3 %collective-permute-start.32 = (bf16[1024,3072]{1,0:T(8,128)(2,1)}, bf16[1024,3072]{1,0:T(8,128)(2,1)}, u32[]{:S(2)}, u32[]{:S(2)}) collective-permute-start(bf16[1024,3072]{1,0:T(8,128)(2,1)} %convolution_convert_fusion), channel_id=1, source_target_pairs={{0,2},{2,0},{4,6},{6,4},{8,10},{10,8},{12,14},{14,12},{16,18},{18,... | collective-permute-start | bytes 18874376 | tf_op jit(solution)/shard_map/ppermute | solution.py:228
  785.7 82.8 %collective-permute-start.19 = (bf16[512,2048]{1,0:T(8,128)(2,1)}, bf16[512,2048]{1,0:T(8,128)(2,1)}, u32[]{:S(2)}, u32[]{:S(2)}) collective-permute-start(bf16[512,2048]{1,0:T(8,128)(2,1)} %convolution_convert_fusion.5), channel_id=1, source_target_pairs={{0,1},{1,0},{2,3},{3,2},{4,5},{5,4},{6,7},{7,6},{8,9},{9,8},{10,11... | collective-permute-start | bytes 6291464 | tf_op jit(solution)/shard_map/ppermute | solution.py:232
  839.2 9.9 collective-permute-start.40
  848.8 85.2 %collective-permute-start.28 = (bf16[1024,2048]{1,0:T(8,128)(2,1)}, bf16[1024,2048]{1,0:T(8,128)(2,1)}, u32[]{:S(2)}, u32[]{:S(2)}) collective-permute-start(bf16[1024,2048]{1,0:T(8,128)(2,1)} %convolution_convert_fusion.4), channel_id=1, source_target_pairs={{0,2},{2,0},{4,6},{6,4},{8,10},{10,8},{12,14},{14,12},{16,18},{18,... | collective-permute-start | bytes 12582920 | tf_op jit(solution)/shard_map/ppermute | solution.py:228
  849.1 96.1 %collective-permute-start.24 = (bf16[1024,2560]{1,0:T(8,128)(2,1)}, bf16[1024,2560]{1,0:T(8,128)(2,1)}, u32[]{:S(2)}, u32[]{:S(2)}) collective-permute-start(bf16[1024,2560]{1,0:T(8,128)(2,1)} %convolution_convert_fusion.1), channel_id=1, source_target_pairs={{0,2},{2,0},{4,6},{6,4},{8,10},{10,8},{12,14},{14,12},{16,18},{18,... | collective-permute-start | bytes 15728648 | tf_op jit(solution)/shard_map/ppermute | solution.py:228
  849.4 10.6 collective-permute-start.41
  860.0 54.5 %collective-permute-start.37 = (bf16[512,1536]{1,0:T(8,128)(2,1)S(1)}, bf16[512,1536]{1,0:T(8,128)(2,1)}, u32[]{:S(2)}, u32[]{:S(2)}) collective-permute-start(bf16[512,1536]{1,0:T(8,128)(2,1)S(1)} %slice.421), channel_id=1, source_target_pairs={{0,4},{2,6},{4,0},{6,2},{8,12},{10,14},{12,8},{14,10},{16,20},{18,... | collective-permute-start | bytes 4718600 | tf_op jit(solution)/shard_map/ppermute | solution.py:228
  868.5 20.6 %collective-permute-start.42 = (f32[1,4352]{1,0:T(1,128)S(1)}, f32[1,4352]{1,0:T(1,128)S(1)}, u32[]{:S(2)}, u32[]{:S(2)}) collective-permute-start(f32[1,4352]{1,0:T(1,128)S(1)} %add.206), channel_id=1, source_target_pairs={{0,8},{2,10},{4,12},{6,14},{8,0},{10,2},{12,4},{14,6},{16,24},{18,... | collective-permute-start | bytes 52232 | tf_op jit(solution)/shard_map/ppermute | solution.py:228
  889.1 4.7 collective-permute-start.43
  893.9 19.5 %collective-permute-start.44 = (f32[1,4352]{1,0:T(1,128)S(1)}, f32[1,4352]{1,0:T(1,128)S(1)}, u32[]{:S(2)}, u32[]{:S(2)}) collective-permute-start(f32[1,4352]{1,0:T(1,128)S(1)} %add.208), channel_id=1, source_target_pairs={{0,1},{1,0},{2,3},{3,2},{4,5},{5,4},{6,7},{7,6},{8,9},{9,8},{10,11... | collective-permute-start | bytes 52232 | tf_op jit(solution)/shard_map/ppermute | solution.py:232
  918.4 135.1 %collective-permute-start.38 = (bf16[256,1536]{1,0:T(8,128)(2,1)}, bf16[256,1536]{1,0:T(8,128)(2,1)}, u32[]{:S(2)}, u32[]{:S(2)}) collective-permute-start(bf16[256,1536]{1,0:T(8,128)(2,1)} %slice.318), channel_id=1, source_target_pairs={{0,8},{2,10},{4,12},{6,14},{8,0},{10,2},{12,4},{14,6},{16,24},{18,... | collective-permute-start | bytes 2359304 | tf_op jit(solution)/shard_map/ppermute | solution.py:228
  932.6 125.1 %collective-permute-start.33 = (bf16[512,3072]{1,0:T(8,128)(2,1)}, bf16[512,3072]{1,0:T(8,128)(2,1)}, u32[]{:S(2)}, u32[]{:S(2)}) collective-permute-start(bf16[512,3072]{1,0:T(8,128)(2,1)} %slice.418), channel_id=1, source_target_pairs={{0,4},{2,6},{4,0},{6,2},{8,12},{10,14},{12,8},{14,10},{16,20},{18,... | collective-permute-start | bytes 9437192 | tf_op jit(solution)/shard_map/ppermute | solution.py:228
  943.1 105.7 %collective-permute-start.29 = (bf16[512,2048]{1,0:T(8,128)(2,1)}, bf16[512,2048]{1,0:T(8,128)(2,1)}, u32[]{:S(2)}, u32[]{:S(2)}) collective-permute-start(bf16[512,2048]{1,0:T(8,128)(2,1)} %slice.420), channel_id=1, source_target_pairs={{0,4},{2,6},{4,0},{6,2},{8,12},{10,14},{12,8},{14,10},{16,20},{18,... | collective-permute-start | bytes 6291464 | tf_op jit(solution)/shard_map/ppermute | solution.py:228
  953.7 98.7 %copy-start.12 = (f32[1024,2560]{1,0:T(8,128)}, f32[1024,2560]{1,0:T(8,128)S(1)}, u32[]{:S(2)}) copy-start(f32[1024,2560]{1,0:T(8,128)S(1)} %convert_add_fusion.1) | copy-start | bytes 31457284
  955.6 144.6 %collective-permute-start.25 = (bf16[512,2560]{1,0:T(8,128)(2,1)}, bf16[512,2560]{1,0:T(8,128)(2,1)}, u32[]{:S(2)}, u32[]{:S(2)}) collective-permute-start(bf16[512,2560]{1,0:T(8,128)(2,1)} %slice.419), channel_id=1, source_target_pairs={{0,4},{2,6},{4,0},{6,2},{8,12},{10,14},{12,8},{14,10},{16,20},{18,... | collective-permute-start | bytes 7864328 | tf_op jit(solution)/shard_map/ppermute | solution.py:228
  1052.5 36.0 %collective-permute-start.30 = (bf16[256,2048]{1,0:T(8,128)(2,1)S(1)}, bf16[256,2048]{1,0:T(8,128)(2,1)S(1)}, u32[]{:S(2)}, u32[]{:S(2)}) collective-permute-start(bf16[256,2048]{1,0:T(8,128)(2,1)S(1)} %slice.300), channel_id=1, source_target_pairs={{0,8},{2,10},{4,12},{6,14},{8,0},{10,2},{12,4},{14,6},{16,24},{18,... | collective-permute-start | bytes 3145736 | tf_op jit(solution)/shard_map/ppermute | solution.py:228
  1054.8 53.0 %collective-permute-start.39 = (bf16[128,1536]{1,0:T(8,128)(2,1)S(1)}, bf16[128,1536]{1,0:T(8,128)(2,1)S(1)}, u32[]{:S(2)}, u32[]{:S(2)}) collective-permute-start(bf16[128,1536]{1,0:T(8,128)(2,1)S(1)} %slice.320), channel_id=1, source_target_pairs={{0,16},{2,18},{4,20},{6,22},{8,24},{10,26},{12,28},{14,30},{16,0},... | collective-permute-start | bytes 1179656 | tf_op jit(solution)/shard_map/ppermute | solution.py:228
  1061.8 74.5 %collective-permute-start.34 = (bf16[256,3072]{1,0:T(8,128)(2,1)}, bf16[256,3072]{1,0:T(8,128)(2,1)}, u32[]{:S(2)}, u32[]{:S(2)}) collective-permute-start(bf16[256,3072]{1,0:T(8,128)(2,1)} %slice.308), channel_id=1, source_target_pairs={{0,8},{2,10},{4,12},{6,14},{8,0},{10,2},{12,4},{14,6},{16,24},{18,... | collective-permute-start | bytes 4718600 | tf_op jit(solution)/shard_map/ppermute | solution.py:228
  1089.8 40.7 %collective-permute-start.31 = (bf16[128,2048]{1,0:T(8,128)(2,1)}, bf16[128,2048]{1,0:T(8,128)(2,1)}, u32[]{:S(2)}, u32[]{:S(2)}) collective-permute-start(bf16[128,2048]{1,0:T(8,128)(2,1)} %slice.302), channel_id=1, source_target_pairs={{0,16},{2,18},{4,20},{6,22},{8,24},{10,26},{12,28},{14,30},{16,0},... | collective-permute-start | bytes 1572872 | tf_op jit(solution)/shard_map/ppermute | solution.py:228
  1107.0 59.5 %collective-permute-start.26 = (bf16[256,2560]{1,0:T(8,128)(2,1)}, bf16[256,2560]{1,0:T(8,128)(2,1)}, u32[]{:S(2)}, u32[]{:S(2)}) collective-permute-start(bf16[256,2560]{1,0:T(8,128)(2,1)} %slice.289), channel_id=1, source_target_pairs={{0,8},{2,10},{4,12},{6,14},{8,0},{10,2},{12,4},{14,6},{16,24},{18,... | collective-permute-start | bytes 3932168 | tf_op jit(solution)/shard_map/ppermute | solution.py:228
  1138.4 31.2 %collective-permute-start.35 = (bf16[128,3072]{1,0:T(8,128)(2,1)S(1)}, bf16[128,3072]{1,0:T(8,128)(2,1)S(1)}, u32[]{:S(2)}, u32[]{:S(2)}) collective-permute-start(bf16[128,3072]{1,0:T(8,128)(2,1)S(1)} %slice.310), channel_id=1, source_target_pairs={{0,16},{2,18},{4,20},{6,22},{8,24},{10,26},{12,28},{14,30},{16,0},... | collective-permute-start | bytes 2359304 | tf_op jit(solution)/shard_map/ppermute | solution.py:228
  1169.0 27.3 %collective-permute-start.27 = (bf16[128,2560]{1,0:T(8,128)(2,1)}, bf16[128,2560]{1,0:T(8,128)(2,1)S(1)}, u32[]{:S(2)}, u32[]{:S(2)}) collective-permute-start(bf16[128,2560]{1,0:T(8,128)(2,1)} %slice.291), channel_id=1, source_target_pairs={{0,16},{2,18},{4,20},{6,22},{8,24},{10,26},{12,28},{14,30},{16,0},... | collective-permute-start | bytes 1966088 | tf_op jit(solution)/shard_map/ppermute | solution.py:228
  (62 other events, 1591.1 us)

commit v2 on v1

v2 whole, which is shorter than its diff:
```python
import functools
import math

import jax
import jax.numpy as jnp
import numpy as np
from jax import lax
from jax.experimental import pallas as pl
from jax.experimental.pallas import tpu as pltpu
from jax.sharding import PartitionSpec as P

HD = 128
EPS = 1e-06
THETA = 1000000.0
SCALE = HD ** -0.5
LOG2E = math.log2(math.e)
NT = (((1,), (1,)), ((), ()))
BF = jnp.bfloat16
F32 = jnp.float32


def params(mib):
    return pltpu.CompilerParams(vmem_limit_bytes=mib * 2**20)


def dot(left, right):
    return jnp.dot(left, right, preferred_element_type=F32)


def dot_nt(left, right):
    return lax.dot_general(left, right, NT, preferred_element_type=F32)


def dot_tn(left, right):
    return lax.dot_general(left, right, (((0,), (0,)), ((), ())), preferred_element_type=F32)


def head_norm(values, gain, cosine, sine):
    scale = lax.rsqrt(jnp.mean(values * values, axis=-1, keepdims=True) + EPS)
    normed = values * scale * gain
    return normed * cosine + pltpu.roll(normed, HD // 2, 1) * sine


def head_norm_back(values, gain, cosine, sine, grad_rot):
    scale = lax.rsqrt(jnp.mean(values * values, axis=-1, keepdims=True) + EPS)
    grad = grad_rot * cosine - pltpu.roll(grad_rot, HD // 2, 1) * sine
    scaled = grad * gain
    inner = jnp.mean(scaled * values, axis=-1, keepdims=True)
    grad_values = scale * scaled - values * (scale * scale * scale) * inner
    return grad_values, jnp.sum(grad * values * scale, axis=0, keepdims=True)


def causal_mask(block):
    key = lax.broadcasted_iota(jnp.int32, (block, block), 0)
    query = lax.broadcasted_iota(jnp.int32, (block, block), 1)
    return key <= query


def attn_fwd_kernel(
    block, q_ref, k_ref, v_ref, qg_ref, kg_ref, qcos_ref, qsin_ref, kcos_ref, ksin_ref, out_ref, lse_ref, qs, ks, vt, ps
):
    base = (k_ref.shape[0] - q_ref.shape[0]) // block

    @pl.when(pl.program_id(1) == 0)
    def _():
        ks[...] = head_norm(k_ref[...], kg_ref[...], kcos_ref[...], ksin_ref[...]).astype(BF)
        vt[...] = v_ref[...].astype(BF).T

    qs[...] = head_norm(q_ref[...], qg_ref[...], qcos_ref[...], qsin_ref[...]).astype(BF)
    mask = causal_mask(block)
    for i in range(q_ref.shape[0] // block):
        cols = slice(i * block, (i + 1) * block)
        total = jnp.zeros((1, block), F32)
        for j in range(base + i + 1):
            rows = slice(j * block, (j + 1) * block)
            probs = jnp.exp2(dot_nt(ks[rows], qs[cols]) * (SCALE * LOG2E))
            if j == base + i:
                probs = jnp.where(mask, probs, 0.0)
            total = total + jnp.sum(probs, axis=0, keepdims=True)
            ps[rows, cols] = probs.astype(BF)
        lse_ref[0, :, cols] = jnp.log2(total)
        end = (base + i + 1) * block
        mixed = dot(vt[:, :end], ps[:end, cols])
        out_ref[cols, :] = (mixed * (1.0 / total)).T.astype(BF)


def attn_specs(raw, q_cols, kv_cols, chunk, index):
    heads, kv = q_cols // HD, kv_cols // HD
    group = heads // kv
    keys = (index + 1) * chunk
    head_in = pl.BlockSpec((chunk, HD), lambda k, g: (index, k * group + g))
    head = pl.BlockSpec((chunk, HD), lambda k, g: (0, k * group + g))
    lse = pl.BlockSpec((1, 1, chunk), lambda k, g: (k * group + g, 0, 0))
    gain = pl.BlockSpec((1, HD), lambda k, g: (0, 0))
    query_table = pl.BlockSpec((chunk, HD), lambda k, g: (index, 0))

    def of_keys(rows):
        return (
            pl.BlockSpec((rows, HD), lambda k, g: (0, heads + k)),
            pl.BlockSpec((rows, HD), lambda k, g: (0, heads + kv + k)),
            pl.BlockSpec((rows, HD), lambda k, g: (0, 0)),
            pl.BlockSpec((rows, HD), lambda k, g: (0, k)),
        )

    return heads, kv, group, keys, head_in, head, lse, gain, query_table, of_keys


def attention_fwd(raw, q_cols, kv_cols, chunk, index, query_g, key_g, cosine, sine):
    heads, kv, group, keys, head_in, head, lse, gain, query_table, of_keys = attn_specs(
        raw, q_cols, kv_cols, chunk, index
    )
    key_in, value_in, key_table, _ = of_keys(keys)
    return pl.pallas_call(
        functools.partial(attn_fwd_kernel, min(256, chunk)),
        grid=(kv, group),
        in_specs=[head_in, key_in, value_in, gain, gain, query_table, query_table, key_table, key_table],
        out_specs=[head, lse],
        out_shape=[
            jax.ShapeDtypeStruct((chunk, heads * HD), BF),
            jax.ShapeDtypeStruct((heads, 1, chunk), F32),
        ],
        scratch_shapes=[
            pltpu.VMEM((chunk, HD), BF),
            pltpu.VMEM((keys, HD), BF),
            pltpu.VMEM((HD, keys), BF),
            pltpu.VMEM((keys, chunk), BF),
        ],
        compiler_params=params(40),
    )(raw, raw, raw, query_g, key_g, cosine, sine, cosine, sine)


def attn_bwd_kernel(
    block, keys, first, last, q_ref, k_ref, v_ref, ctx_ref, grad_ref, lse_ref, qg_ref, kg_ref,
    qcos_ref, qsin_ref, kcos_ref, ksin_ref, *rest,
):
    if first:
        dq_ref, dk_ref, dv_ref, dqg_ref, dkg_ref, qs, ks, kt, vs, ps, ds, dks, dvs = rest
    else:
        (dk_in, dv_in, dqg_in, dq_ref, dk_ref, dv_ref, dqg_ref, dkg_ref,
         qs, ks, kt, vs, ps, ds, dks, dvs) = rest
    chunk = q_ref.shape[0]
    base = (keys - chunk) // block
    kv_id, g_id = pl.program_id(0), pl.program_id(1)

    @pl.when(g_id == 0)
    def _():
        rotated = head_norm(k_ref[:keys], kg_ref[...], kcos_ref[:keys], ksin_ref[:keys]).astype(BF)
        ks[...] = rotated
        kt[...] = rotated.T
        vs[...] = v_ref[:keys].astype(BF)
        dks[...] = jnp.zeros_like(dks) if first else dk_in[...]
        dvs[...] = jnp.zeros_like(dvs) if first else dv_in[...]

    @pl.when((g_id == 0) & (kv_id == 0))
    def _():
        dqg_ref[...] = jnp.zeros_like(dqg_ref) if first else dqg_in[...]
        dkg_ref[...] = jnp.zeros_like(dkg_ref)

    qs[...] = head_norm(q_ref[...], qg_ref[...], qcos_ref[...], qsin_ref[...]).astype(BF)
    mask = causal_mask(block)
    for i in range(chunk // block):
        cols = slice(i * block, (i + 1) * block)
        product = grad_ref[cols].astype(F32) * ctx_ref[cols].astype(F32)
        delta = jnp.sum(product.T, axis=0, keepdims=True)
        lse = lse_ref[0, :, cols]
        for j in range(base + i + 1):
            rows = slice(j * block, (j + 1) * block)
            probs = jnp.exp2(dot_nt(ks[rows], qs[cols]) * (SCALE * LOG2E) - lse)
            if j == base + i:
                probs = jnp.where(mask, probs, 0.0)
            grad_probs = dot_nt(vs[rows], grad_ref[cols])
            ps[rows, cols] = probs.astype(BF)
            ds[rows, cols] = (probs * (grad_probs - delta)).astype(BF)
    for j in range(keys // block):
        rows = slice(j * block, (j + 1) * block)
        start = max(0, j - base) * block
        dvs[rows] += dot(ps[rows, start:], grad_ref[start:])
        dks[rows] += dot(ds[rows, start:], qs[start:])
    gain_sum = jnp.zeros((1, HD), F32)
    for i in range(chunk // block):
        cols = slice(i * block, (i + 1) * block)
        end = (base + i + 1) * block
        grad_t = dot(kt[:, :end], ds[:end, cols])
        grad_raw, part = head_norm_back(q_ref[cols], qg_ref[...], qcos_ref[cols], qsin_ref[cols], grad_t.T * SCALE)
        dq_ref[cols] = grad_raw.astype(BF)
        gain_sum = gain_sum + part
    dqg_ref[...] += gain_sum

    @pl.when(g_id == pl.num_programs(1) - 1)
    def _():
        if last:
            grad_raw, part = head_norm_back(k_ref[...], kg_ref[...], kcos_ref[...], ksin_ref[...], dks[...] * SCALE)
            dk_ref[...] = grad_raw.astype(BF)
            dv_ref[...] = dvs[...].astype(BF)
            dkg_ref[...] += part
        else:
            dk_ref[...] = dks[...]
            dv_ref[...] = dvs[...]


def attention_bwd(
    raw, q_cols, kv_cols, chunk, index, context, grad_context, lse_rows, query_g, key_g, cosine, sine, earlier, last
):
    seq = raw.shape[0]
    heads, kv, group, keys, head_in, head, lse, gain, query_table, of_keys = attn_specs(
        raw, q_cols, kv_cols, chunk, index
    )
    key_in, value_in, key_table, key_out = of_keys(seq)
    first = earlier is None
    more = [] if first else list(earlier)
    kind = BF if last else F32
    return pl.pallas_call(
        functools.partial(attn_bwd_kernel, min(256, chunk), keys, first, last),
        grid=(kv, group),
        in_specs=[head_in, key_in, value_in, head, head, lse, gain, gain, query_table, query_table, key_table, key_table]
        + ([] if first else [key_out, key_out, gain]),
        out_specs=[head, key_out, key_out, gain, gain],
        out_shape=[
            jax.ShapeDtypeStruct((chunk, heads * HD), BF),
            jax.ShapeDtypeStruct((seq, kv * HD), kind),
            jax.ShapeDtypeStruct((seq, kv * HD), kind),
            jax.ShapeDtypeStruct((1, HD), F32),
            jax.ShapeDtypeStruct((1, HD), F32),
        ],
        scratch_shapes=[
            pltpu.VMEM((chunk, HD), BF),
            pltpu.VMEM((keys, HD), BF),
            pltpu.VMEM((HD, keys), BF),
            pltpu.VMEM((keys, HD), BF),
            pltpu.VMEM((keys, chunk), BF),
            pltpu.VMEM((keys, chunk), BF),
            pltpu.VMEM((seq, HD), F32),
            pltpu.VMEM((seq, HD), F32),
        ],
        compiler_params=params(48),
    )(raw, raw, raw, context, grad_context, lse_rows, query_g, key_g, cosine, sine, cosine, sine, *more)


def rope_tables(seq):
    position = lax.iota(F32, seq)
    freq = THETA ** (-2.0 * lax.iota(F32, HD // 2) / HD)
    angle = position[:, None] * freq[None, :]
    cosine, sine = jnp.cos(angle), jnp.sin(angle)
    return jnp.concatenate([cosine, cosine], axis=1), jnp.concatenate([-sine, sine], axis=1)


def bits_of(count):
    return count.bit_length() - 1


def swap(value, bit):
    count = lax.axis_size("dp")
    return lax.ppermute(value, "dp", [(i, i ^ (1 << bit)) for i in range(count)])


def swap_pair(value):
    return lax.ppermute(value, "tensor", [(0, 1), (1, 0)])


def after(value, *needed):
    return lax.optimization_barrier((value, needed))[0]


def block_order():
    count = lax.axis_size("dp")
    bits = bits_of(count)
    reverse = np.array([int(format(i, "b").zfill(bits)[::-1], 2) if bits else 0 for i in range(count)], np.int32)
    return jnp.asarray(reverse) ^ lax.axis_index("dp").astype(jnp.int32)


def join_kernel(count, turn_ref, order_ref, one_ref, two_ref, out_ref):
    block = out_ref.shape[1] // count

    def fill(ref):
        for i in range(count):
            column = pl.multiple_of(order_ref[i] * block, block)
            out_ref[:, i * block : (i + 1) * block] = ref[:, pl.ds(column, block)]

    @pl.when(pl.program_id(0) == turn_ref[0])
    def _():
        fill(one_ref)

    @pl.when(pl.program_id(0) != turn_ref[0])
    def _():
        fill(two_ref)


def join(one, two, turn, order):
    rows, width = one.shape
    count = order.shape[0]
    tile = min(256, rows)
    turn = jnp.asarray(turn, jnp.int32)
    if (width // count) % 128:
        both = jnp.where(turn == 0, jnp.concatenate([one, two], axis=0), jnp.concatenate([two, one], axis=0))
        return jnp.take(both.reshape(2 * rows, count, -1), order, axis=1).reshape(2 * rows, width)
    steps = rows // tile
    half = pl.BlockSpec((tile, width), lambda h, r: (r, 0))
    return pl.pallas_call(
        functools.partial(join_kernel, count),
        grid=(2, steps),
        in_specs=[pl.BlockSpec(memory_space=pltpu.SMEM), pl.BlockSpec(memory_space=pltpu.SMEM), half, half],
        out_specs=pl.BlockSpec((tile, width), lambda h, r: (h * steps + r, 0)),
        out_shape=jax.ShapeDtypeStruct((2 * rows, width), one.dtype),
        compiler_params=params(32),
    )(turn.reshape(1), order, one, two)


def pick(turn_ref, index, own_ref, other_ref):
    return jnp.where(turn_ref[0] == index, own_ref[...].astype(F32), other_ref[...].astype(F32))


def mean_square(values):
    return lax.rsqrt(jnp.mean(values * values, axis=-1, keepdims=True) + EPS)


def mid_kernel(index, turn_ref, own_ref, other_ref, part_ref, got_ref, gain_ref, mid_ref, normed_ref):
    mid = pick(turn_ref, index, own_ref, other_ref) + (part_ref[...].astype(F32) + got_ref[...].astype(F32))
    mid_ref[...] = mid
    normed_ref[...] = (mid * mean_square(mid) * gain_ref[...]).astype(BF)


def middle(own, other, part, got, gain, turn, index):
    rows, width = own.shape
    tile = min(128, rows)
    block = pl.BlockSpec((tile, width), lambda r: (r, 0))
    return pl.pallas_call(
        functools.partial(mid_kernel, index),
        grid=(rows // tile,),
        in_specs=[pl.BlockSpec(memory_space=pltpu.SMEM)] + [block] * 4 + [pl.BlockSpec((1, width), lambda r: (0, 0))],
        out_specs=[block, block],
        out_shape=[jax.ShapeDtypeStruct((rows, width), F32), jax.ShapeDtypeStruct((rows, width), BF)],
        compiler_params=params(32),
    )(turn.reshape(1), own, other, part, got, gain)


def norm_back(values, gain, grad):
    scale = mean_square(values)
    scaled = grad * gain
    inner = jnp.mean(scaled * values, axis=-1, keepdims=True)
    grad_values = scale * scaled - values * (scale * scale * scale) * inner
    return grad_values, jnp.sum(grad * values * scale, axis=0, keepdims=True)


def mid_back_kernel(index, turn_ref, own_ref, other_ref, part_ref, got_ref, mid_ref, gain_ref, out_ref, low_ref, sum_ref):
    grad = part_ref[...].astype(F32) + got_ref[...].astype(F32)
    back, part = norm_back(mid_ref[...], gain_ref[...], grad)
    total = pick(turn_ref, index, own_ref, other_ref) + back
    out_ref[...] = total
    low_ref[...] = total.astype(BF)

    @pl.when(pl.program_id(0) == 0)
    def _():
        sum_ref[...] = jnp.zeros_like(sum_ref)

    sum_ref[...] += part


def middle_back(own, other, part, got, mid, gain, turn, index):
    rows, width = own.shape
    tile = min(128, rows)
    block = pl.BlockSpec((tile, width), lambda r: (r, 0))
    line = pl.BlockSpec((1, width), lambda r: (0, 0))
    return pl.pallas_call(
        functools.partial(mid_back_kernel, index),
        grid=(rows // tile,),
        in_specs=[pl.BlockSpec(memory_space=pltpu.SMEM)] + [block] * 5 + [line],
        out_specs=[block, block, line],
        out_shape=[
            jax.ShapeDtypeStruct((rows, width), F32),
            jax.ShapeDtypeStruct((rows, width), BF),
            jax.ShapeDtypeStruct((1, width), F32),
        ],
        compiler_params=params(32),
    )(turn.reshape(1), own, other, part, got, mid, gain)


def expert_kernel(x_ref, own_ref, other_ref, turn_ref, gate_ref, up_ref, down_ref, route_ref, weight_ref, *rest, index):
    hidden_ref, gg_ref, gu_ref = rest[-3:]
    expert = pl.program_id(0)
    share = jnp.sum(jnp.where(route_ref[...] == expert, weight_ref[...], 0.0), axis=-1, keepdims=True)
    gate = dot(x_ref[...], gate_ref[...])
    up = dot(x_ref[...], up_ref[...])
    cot = jnp.where(turn_ref[0] == index, own_ref[...], other_ref[...])
    grad_hidden = dot(cot, down_ref[...]) * share
    sigma = 1.0 / (1.0 + jnp.exp(-gate))
    silu = gate * sigma
    hidden_ref[...] = (silu * up * share).astype(BF)
    gg_ref[...] = (grad_hidden * up * sigma * (1.0 + gate * (1.0 - sigma))).astype(BF)
    gu_ref[...] = (grad_hidden * silu).astype(BF)


def expert_part(normed, own, other, weights, routes, route_weights, turn, index, experts, earlier):
    rows, width = normed.shape
    cols = weights.shape[1] // (3 * experts)
    seq = routes.shape[0]
    full = pl.BlockSpec((rows, width), lambda e: (0, 0))
    scalar = pl.BlockSpec(memory_space=pltpu.SMEM)
    pair = pl.BlockSpec((rows, routes.shape[1]), lambda e: (index, 0))
    out = pl.BlockSpec((rows, cols), lambda e: (index, e))
    more = [] if earlier is None else list(earlier)
    return pl.pallas_call(
        functools.partial(expert_kernel, index=index),
        grid=(experts,),
        in_specs=[full, full, full, scalar]
        + [pl.BlockSpec((width, cols), lambda e, k=k: (0, k * experts + e)) for k in range(3)]
        + [pair, pair]
        + [pl.BlockSpec(memory_space=pl.ANY)] * len(more),
        out_specs=[out, out, out],
        out_shape=[jax.ShapeDtypeStruct((seq, experts * cols), BF)] * 3,
        input_output_aliases={9 + i: i for i in range(len(more))},
        compiler_params=params(56),
    )(normed, own, other, turn.reshape(1), weights, weights, weights, routes, route_weights, *more)


def fold(keep, received):
    return (keep.astype(F32) + received.astype(F32)).astype(BF)


def sum_all(value):
    for bit in range(bits_of(lax.axis_size("dp"))):
        value = value + swap(value, bit)
    return value + swap_pair(value)


class Reduction:
    def __init__(self, left, right, order, *needed):
        self.order = list(order)
        self.block = left.shape[1] // lax.axis_size("dp")
        half = left.shape[1] // 2
        self.left, self.right = left[:, :half], right
        self.sent = dot_tn(after(left[:, half:], *needed), right).astype(BF)
        self.got = swap(self.sent, 0)

    def keep(self, *needed):
        total = dot_tn(after(self.left, *needed), self.right) + self.got.astype(F32)
        self.axes = list(range(1, bits_of(lax.axis_size("dp"))))
        shape = (2,) * len(self.axes) + (self.block, total.shape[1])
        self.held = total.astype(BF).reshape(shape)
        self.send()
        return self.held

    def send(self):
        axis = self.axes.index(self.order[0])
        self.mine = lax.index_in_dim(self.held, 0, axis, keepdims=False)
        self.got = swap(lax.index_in_dim(self.held, 1, axis, keepdims=False), self.order[0])

    def step(self, *needed):
        self.axes.remove(self.order.pop(0))
        mine = after(self.mine, *needed) if needed else self.mine
        if not self.order:
            return mine.astype(F32) + self.got.astype(F32)
        self.held = fold(mine, self.got)
        self.send()
        return self.held

    def finish(self, *needed):
        while True:
            result = self.step(*needed)
            if not self.order:
                return result


def body(
    tokens, cotangent, routes, route_weights, query_weight, key_weight, value_weight, out_weight,
    gate_weight, up_weight, down_weight, attn_gain, ffn_gain, query_gain, key_gain,
):
    turn = lax.axis_index("tensor").astype(jnp.int32)
    chunk = tokens.shape[0]
    seq = 2 * chunk
    width = tokens.shape[1]
    order = block_order()
    cosine, sine = rope_tables(seq)
    experts, hidden_cols = gate_weight.shape[2], gate_weight.shape[3]
    flat = experts * hidden_cols
    q_cols, kv_cols = query_weight.shape[2], key_weight.shape[2]
    qkv_cols = q_cols + 2 * kv_cols
    bits = bits_of(lax.axis_size("dp"))
    straight = list(range(1, bits))
    crossed = straight if bits < 3 else [2, 1] + straight[2:]
    row_routes, row_weights = routes[0], route_weights[0]

    def select(zero, one):
        return jnp.where(turn == 0, zero, one)

    attn_w = lax.all_gather(
        jnp.concatenate([query_weight[0], key_weight[0], value_weight[0], out_weight[0]], axis=1),
        "dp", axis=0, tiled=True,
    )
    ffn_w = lax.all_gather(
        jnp.concatenate([w[0].reshape(-1, flat) for w in (gate_weight, up_weight, down_weight)], axis=1),
        "dp", axis=0, tiled=True,
    )
    qkv_w, out_w = attn_w[:, :qkv_cols], attn_w[:, qkv_cols:]
    gate_up_w, down_w = ffn_w[:, : 2 * flat], ffn_w[:, 2 * flat :]

    tokens_other = swap_pair(tokens)
    cot_other = swap_pair(cotangent)
    resid = select(
        jnp.concatenate([tokens, tokens_other], axis=0), jnp.concatenate([tokens_other, tokens], axis=0)
    ).astype(F32)
    normed = (resid * mean_square(resid) * attn_gain).astype(BF)
    normed_rel = join(normed[:chunk], normed[chunk:], 0, order)
    cot_rel = join(cotangent, cot_other, turn, order)

    raw = dot(after(normed, normed_rel, cot_rel), qkv_w)
    context, lse, part, got = {}, {}, {}, {}
    last = raw
    for index in (1, 0):
        context[index], lse[index] = attention_fwd(
            after(raw, last), q_cols, kv_cols, chunk, index, query_gain, key_gain, cosine, sine
        )
        part[index] = dot_nt(context[index], out_w).astype(BF)
        got[index] = swap_pair(part[index])
        last = part[index]

    mid, normed_f, back_part, back_got = {}, {}, {}, {}
    done = None
    for index in (1, 0):
        mid[index], normed_f[index] = middle(
            tokens, tokens_other, after(part[index], last), got[index], ffn_gain, turn, index
        )
        done = expert_part(
            normed_f[index], cotangent, cot_other, ffn_w, row_routes, row_weights, turn, index, experts, done
        )
        rows = slice(index * chunk, (index + 1) * chunk)
        grad_gate_up = jnp.concatenate([done[1][rows], done[2][rows]], axis=1)
        back_part[index] = dot_nt(grad_gate_up, gate_up_w).astype(BF)
        back_got[index] = swap_pair(back_part[index])
        last = back_part[index]
        done = [after(value, last) for value in done]
    hidden, grad_gate, grad_up = done
    normed_f_rel = join(after(normed_f[0], last), normed_f[1], 0, order)

    down_sum = Reduction(cot_rel, hidden, straight, normed_f_rel)
    gate_sum = Reduction(normed_f_rel, grad_gate, straight, down_sum.sent)
    up_sum = Reduction(normed_f_rel, grad_up, crossed, gate_sum.sent)
    last = down_sum.keep(up_sum.sent)
    last = up_sum.keep(last)
    last = gate_sum.keep(last)

    grad_mid, grad_mid_b, ffn_parts, grad_context, dq = {}, {}, {}, {}, {}
    earlier = None
    for index in (1, 0):
        grad_mid[index], grad_mid_b[index], ffn_parts[index] = middle_back(
            cotangent, cot_other, after(back_part[index], last), back_got[index], mid[index], ffn_gain, turn, index
        )
        grad_context[index] = dot(grad_mid_b[index], out_w).astype(BF)
        if index == 0:
            grad_mid_rel = join(after(grad_mid_b[0], grad_context[0]), grad_mid_b[1], 0, order)
            all_context = jnp.concatenate([context[0], context[1]], axis=0)
            out_sum = Reduction(grad_mid_rel, all_context, straight)
            last = out_sum.sent
            last = out_sum.keep(last)
            last = down_sum.step(last)
            last = up_sum.step(last)
        dq[index], dk, dv, query_part, key_part = attention_bwd(
            raw, q_cols, kv_cols, chunk, index, context[index], after(grad_context[index], last), lse[index],
            query_gain, key_gain, cosine, sine, earlier, index == 0,
        )
        earlier = (dk, dv, query_part)
        last = dq[index]
        if index == 1:
            hidden_theirs = select(hidden[chunk:], hidden[:chunk])
            out_theirs = dot_nt(after(hidden_theirs, last), down_w).astype(BF)
            hidden_mine = select(hidden[:chunk], hidden[chunk:])
            out_mine = dot_nt(after(hidden_mine, out_theirs), down_w).astype(BF)
            last = out_mine

    last = gate_sum.step(last)
    last = down_sum.step(last)
    theirs = jnp.concatenate([select(dq[1], dq[0]), select(dk[chunk:], dk[:chunk]), select(dv[chunk:], dv[:chunk])], axis=1)
    grad_theirs = dot_nt(after(theirs, last), qkv_w).astype(BF)
    grad_qkv = jnp.concatenate([jnp.concatenate([dq[0], dq[1]], axis=0), dk, dv], axis=1)
    grad_got = swap_pair(grad_theirs)
    middle_col = qkv_cols // 2
    one_sum = Reduction(normed_rel, grad_qkv[:, :middle_col], crossed, grad_theirs)
    two_sum = Reduction(normed_rel, grad_qkv[:, middle_col:], straight, one_sum.sent)
    last = up_sum.step(two_sum.sent)
    last = out_sum.step(last)
    last = one_sum.keep(last)
    last = two_sum.keep(last)
    mine = select(grad_qkv[:chunk], grad_qkv[chunk:])
    grad_mine = dot_nt(after(mine, last), qkv_w)
    down_grad = down_sum.finish(grad_mine)
    last = gate_sum.step(down_grad)
    last = one_sum.step(last)
    last = out_sum.step(last)
    output = select(mid[0], mid[1]) + (out_mine.astype(F32) + swap_pair(after(out_theirs, grad_theirs)).astype(F32))
    output = after(output, last).astype(BF)
    last = two_sum.step(output)
    up_grad = up_sum.finish(last)
    gate_grad = gate_sum.finish(up_grad)
    last = one_sum.step(gate_grad)
    last = two_sum.step(last)

    grad_normed = after(grad_mine, last) + grad_got.astype(F32)
    grad_one, attn_part = norm_back(tokens.astype(F32), attn_gain, grad_normed)
    tokens_grad = select(grad_mid[0], grad_mid[1]) + grad_one
    out_grad = out_sum.finish(tokens_grad)
    ffn_part = (ffn_parts[0] + ffn_parts[1]) * 0.5
    small = sum_all(jnp.concatenate([attn_part, ffn_part, query_part, key_part], axis=1))
    one_grad = one_sum.finish(out_grad)
    two_grad = two_sum.finish(one_grad)
    qkv_grad = jnp.concatenate([one_grad, two_grad], axis=1)

    def expert(values):
        return values.reshape(1, -1, experts, hidden_cols)

    return (
        output,
        tokens_grad,
        qkv_grad[None, :, :q_cols],
        qkv_grad[None, :, q_cols : q_cols + kv_cols],
        qkv_grad[None, :, q_cols + kv_cols :],
        out_grad[None],
        expert(gate_grad),
        expert(up_grad),
        expert(down_grad),
        small[:, :width],
        small[:, width : 2 * width],
        small[:, 2 * width : 2 * width + HD],
        small[:, 2 * width + HD :],
    )


def solution(mesh):
    return jax.shard_map(
        body,
        mesh=mesh,
        in_specs=(
            P(("dp", "tensor"), None),
            P(("dp", "tensor"), None),
            P(None, "dp", None),
            P(None, "dp", None),
            P(None, "dp", "tensor"),
            P(None, "dp", "tensor"),
            P(None, "dp", "tensor"),
            P(None, "dp", "tensor"),
            P(None, "dp", None, "tensor"),
            P(None, "dp", None, "tensor"),
            P(None, "dp", None, "tensor"),
            P(),
            P(),
            P(),
            P(),
        ),
        out_specs=(
            P(("dp", "tensor"), None),
            P(("dp", "tensor"), None),
            P(None, "dp", "tensor"),
            P(None, "dp", "tensor"),
            P(None, "dp", "tensor"),
            P(None, "dp", "tensor"),
            P(None, "dp", None, "tensor"),
            P(None, "dp", None, "tensor"),
            P(None, "dp", None, "tensor"),
            P(),
            P(),
            P(),
            P(),
        ),
        check_vma=False,
    )
```

time: 1210 us -> 773 us (0.64)
  waiting for transfers between devices: 602 us -> 251 us
  other arithmetic: 125 us -> 51.4 us
  Pallas kernels: 119 us -> 167 us
  matrix products: 217 us -> 179 us
  local copies, waits for them, and re-layouts: 87.4 us -> 66.1 us
  between operations: 2.07 us -> 15.4 us
    ppermute x36 -> x28, waiting for transfers between devices: 429 us -> 112 us  [swap(): return lax.ppermute(value, 'dp', [(i, i ^ 1 << bit) for i in range(count)])]
    pallas_call x6 -> x14, Pallas kernels: 119 us -> 167 us  [the longest x2 60.2 us: attention_bwd(): pl.pallas_call(functools.partial(attn_bwd_kernel, min(256, chunk), keys,...]
    ppermute x9, waiting for transfers between devices: 173 us -> 139 us  [swap_pair(): return lax.ppermute(value, 'tensor', [(0, 1), (1, 0)])]
    concatenate x14 -> x7, other arithmetic: 33.9 us -> 5.79 us  [the longest x1 2.41 us: body(): jnp.concatenate([query_weight[0], key_weight[0], value_weight[0], out_wei...]
    dot_general x4 -> x3, matrix products: 63.7 us -> 36.9 us  [dot(): return jnp.dot(left, right, preferred_element_type=F32)]
    add x6 -> x7, other arithmetic: 29.7 us -> 12.1 us  [the longest x1 5.64 us: body(): select(mid[0], mid[1])]
    concatenate x6 -> x1, local copies, waits for them, and re-layouts: 17.6 us -> 0.24 us  [body(): all_context = jnp.concatenate([context[0], context[1]], axis=0)]
    convert_element_type x12 -> x13, other arithmetic: 31.5 us -> 17.7 us  [the longest x12 14.6 us: fold(): return (keep.astype(F32) + received.astype(F32)).astype(BF)]
  transfers between devices with their start and end apart: 45 -> 39, of which waited for: 21 -> 20; matrix products, arithmetic and copies ran while one was open for 25% -> 32% of each run, Pallas kernels for 6% -> 18%
where the time goes in v2:
time: 773 us; the launch traced here: 769 us
  waiting for transfers between devices  251 us (32%)
  matrix products  179 us (23%)
  Pallas kernels  167 us (22%)
  local copies, waits for them, and re-layouts  66.1 us (9%)
  other arithmetic  51.4 us (7%)
  starting transfers between devices  38.7 us (5%)
  between operations  15.4 us (2%)
    ppermute x9, waiting for transfers between devices, swap_pair(): return lax.ppermute(value, 'tensor', [(0, 1), (1, 0)])  139 us
    ppermute x28, waiting for transfers between devices, swap(): return lax.ppermute(value, 'dp', [(i, i ^ 1 << bit) for i in range(count)])  112 us
    dot_general x8, matrix products, dot_nt(): return lax.dot_general(left, right, NT, preferred_element_type=F32)  78.6 us
    dot_general x12, matrix products, dot_tn(): lax.dot_general(left, right, (((0,), (0,)), ((), ())), preferred_element_...  63.7 us
    pallas_call x2, Pallas kernels, attention_bwd(): pl.pallas_call(functools.partial(attn_bwd_kernel, min(256, chunk), keys,...  60.2 us
    pallas_call x2, Pallas kernels, expert_part(): pl.pallas_call(functools.partial(expert_kernel, index=index), grid=(exper...  40.1 us
    dot_general x3, matrix products, dot(): return jnp.dot(left, right, preferred_element_type=F32)  36.9 us
    pallas_call x2, Pallas kernels, attention_fwd(): pl.pallas_call(functools.partial(attn_fwd_kernel, min(256, chunk)), grid=...  36.2 us
  transfers between devices with their start and end apart: 39, of which 20 were waited for; matrix products, arithmetic and copies ran while one was open for 32% of the time, Pallas kernels for 18%

profile of v2, /device:TPU:0, one launch (start us, length us, event | category | flops | bytes accessed | tf_op | source)
XLA Modules:
  0.0 768.8 jit_solution(10148780747595050704)
XLA Ops:
  17.3 44.1 %collective-permute-done.other_ref = bf16[512,2048]{1,0:T(8,128)(2,1)} collective-permute-done((bf16[512,2048]{1,0:T(8,128)(2,1)S(1)}, bf16[512,2048]{1,0:T(8,128)(2,1)}, u32[]{:S(2)}, u32[]{:S(2)}) %collective-permute-start) | collective-permute-done | bytes 2097184 | tf_op jit(solution)/shard_map/ppermute | solution.py:257
  74.0 31.5 %collective-permute-done.1.two_ref.other_ref = bf16[512,2048]{1,0:T(8,128)(2,1)} collective-permute-done((bf16[512,2048]{1,0:T(8,128)(2,1)}, bf16[512,2048]{1,0:T(8,128)(2,1)}, u32[]{:S(2)}, u32[]{:S(2)}) %collective-permute-start.1) | collective-permute-done | bytes 2097184 | tf_op jit(solution)/shard_map/ppermute | solution.py:257
  111.9 15.0 %fusion.11.q_ref.k_ref.v_ref = f32[1024,2560]{1,0:T(8,128)S(1)} fusion(bf16[1024,2048]{1,0:T(8,128)(2,1)} %copy-done.41, bf16[2048,4608]{1,0:T(8,128)(2,1)} %all-gather.3.cloned.1.call-done), kind=kOutput, calls=%fused_computation.14 | convolution fusion | flops 10737418240 | bytes 25165824 | tf_op jit(solution)/shard_map/dot_general | solution.py:27
  126.9 19.8 %shard_map.257 = (bf16[512,2048]{1,0:T(8,128)(2,1)S(1)}, f32[16,1,512]{2,1,0:T(1,128)S(1)}) custom-call(f32[1024,2560]{1,0:T(8,128)S(1)} %fusion.11.q_ref.k_ref.v_ref, f32[1024,2560]{1,0:T(8,128)S(1)} %fusion.11.q_ref.k_ref.v_ref, f32[1024,2560]{1,0:T(8,128)S(1)} %fusion.11.q_ref.k_ref.v_ref, f32[1,128]{1,0:T(1,128)S(1)} %copy-done.36, ...), custom_call_target="tpu_custom_call" | custom-call | tf_op jit(solution)/shard_map/pallas_call | solution.py:113
  146.8 10.1 %fusion.41.part_ref = bf16[512,2048]{1,0:T(8,128)(2,1)} fusion(bf16[512,2048]{1,0:T(8,128)(2,1)S(1)} %get-tuple-element.94.ctx_ref, bf16[2048,4608]{1,0:T(8,128)(2,1)} %all-gather.3.cloned.1.call-done), kind=kOutput, calls=%fused_computation.65 | convolution fusion | flops 4296015872 | bytes 12582912 | tf_op jit(solution)/shard_map/dot_general | solution.py:31
  164.5 16.4 %shard_map.258 = (bf16[512,2048]{1,0:T(8,128)(2,1)S(1)}, f32[16,1,512]{2,1,0:T(1,128)S(1)}) custom-call(f32[1024,2560]{1,0:T(8,128)S(1)} %copy-done.1, f32[1024,2560]{1,0:T(8,128)S(1)} %copy-done.1, f32[1024,2560]{1,0:T(8,128)S(1)} %copy-done.1, f32[1,128]{1,0:T(1,128)S(1)} %copy-done.36, f32[1,128]{1,0:T(1,128)S(1)} %copy-done.38, ...), custom_call_target="tpu_custom_call" | custom-call | tf_op jit(solution)/shard_map/pallas_call | solution.py:113
  180.9 10.3 %fusion.44.part_ref = bf16[512,2048]{1,0:T(8,128)(2,1)} fusion(bf16[512,2048]{1,0:T(8,128)(2,1)S(1)} %get-tuple-element.96.ctx_ref, bf16[2048,4608]{1,0:T(8,128)(2,1)} %all-gather.3.cloned.1.call-done), kind=kOutput, calls=%fused_computation.66 | convolution fusion | flops 4296015872 | bytes 12582912 | tf_op jit(solution)/shard_map/dot_general | solution.py:31
  194.8 10.8 %collective-permute-done.2.got_ref = bf16[512,2048]{1,0:T(8,128)(2,1)} collective-permute-done((bf16[512,2048]{1,0:T(8,128)(2,1)}, bf16[512,2048]{1,0:T(8,128)(2,1)}, u32[]{:S(2)}, u32[]{:S(2)}) %collective-permute-start.2) | collective-permute-done | bytes 2097184 | tf_op jit(solution)/shard_map/ppermute | solution.py:257
  205.6 4.5 shard_map.259
  213.6 20.0 %shard_map.260 = (bf16[1024,1536]{1,0:T(8,128)(2,1)}, bf16[1024,1536]{1,0:T(8,128)(2,1)}, bf16[1024,1536]{1,0:T(8,128)(2,1)}) custom-call(bf16[512,2048]{1,0:T(8,128)(2,1)} %copy-done.13, bf16[512,2048]{1,0:T(8,128)(2,1)} %own_ref.11, bf16[512,2048]{1,0:T(8,128)(2,1)} %collective-permute-done.1.two_ref.other_ref, s32[1]{0:T(128)} %bitcast.turn_ref, ...), custom_call_target="tpu_custom_call" | custom-call | tf_op jit(solution)/shard_map/pallas_call | solution.py:401
  236.1 9.7 %fusion.59.part_ref = bf16[512,2048]{1,0:T(8,128)(2,1)S(1)} fusion(bf16[2048,4608]{1,0:T(8,128)(2,1)} %all-gather.5.cloned.1.call-done.gate_ref.up_ref.down_ref, bf16[512,1536]{1,0:T(8,128)(2,1)S(1)} %slice.232, bf16[512,1536]{1,0:T(8,128)(2,1)S(1)} %slice.231), kind=kOutput, calls=%fused_computation.71 | convolution fusion | flops 6449790976 | bytes 17825792 | tf_op jit(solution)/shard_map/dot_general | solution.py:31
  249.8 4.5 shard_map.261
  257.6 20.1 %shard_map.262 = (bf16[1024,1536]{1,0:T(8,128)(2,1)}, bf16[1024,1536]{1,0:T(8,128)(2,1)}, bf16[1024,1536]{1,0:T(8,128)(2,1)}) custom-call(bf16[512,2048]{1,0:T(8,128)(2,1)} %copy-done.15, bf16[512,2048]{1,0:T(8,128)(2,1)} %own_ref.11, ...), custom_call_target="tpu_custom_call", output_to_operand_aliasing={{0}: (9, {}), {1}: (10, {}), {2}: (11, {})} | custom-call | tf_op jit(solution)/shard_map/pallas_call | solution.py:401
  280.2 10.9 %fusion.64.part_ref = bf16[512,2048]{1,0:T(8,128)(2,1)} fusion(bf16[2048,4608]{1,0:T(8,128)(2,1)} %all-gather.5.cloned.1.call-done.gate_ref.up_ref.down_ref, bf16[512,1536]{1,0:T(8,128)(2,1)S(1)} %slice.235, bf16[512,1536]{1,0:T(8,128)(2,1)S(1)} %slice.234), kind=kOutput, calls=%fused_computation.72 | convolution fusion | flops 6449790976 | bytes 17825792 | tf_op jit(solution)/shard_map/dot_general | solution.py:31
  295.5 5.0 convolution_convert_fusion.4
  300.5 5.1 convolution_convert_fusion.3
  305.6 5.1 convolution_convert_fusion.2
  320.7 5.6 add_convert_fusion.1
  329.5 5.3 add_convert_fusion.3
  338.1 6.7 add_convert_fusion.2
  344.8 19.9 %collective-permute-done.6.got_ref = bf16[512,2048]{1,0:T(8,128)(2,1)S(1)} collective-permute-done((bf16[512,2048]{1,0:T(8,128)(2,1)S(1)}, bf16[512,2048]{1,0:T(8,128)(2,1)S(1)}, u32[]{:S(2)}, u32[]{:S(2)}) %collective-permute-start.6) | collective-permute-done | bytes 2097184 | tf_op jit(solution)/shard_map/ppermute | solution.py:257
  364.7 5.6 shard_map.264
  370.4 11.2 %fusion.47.grad_ref = bf16[512,2048]{1,0:T(8,128)(2,1)} fusion(bf16[512,2048]{1,0:T(8,128)(2,1)S(1)} %get-tuple-element.121.two_ref, bf16[2048,4608]{1,0:T(8,128)(2,1)} %all-gather.3.cloned.1.call-done), kind=kOutput, calls=%fused_computation.67 | convolution fusion | flops 4296015872 | bytes 12582912 | tf_op jit(solution)/shard_map/dot_general | solution.py:27
  381.6 34.1 %shard_map.265 = (bf16[512,2048]{1,0:T(8,128)(2,1)S(1)}, f32[1024,256]{1,0:T(8,128)S(1)}, f32[1024,256]{1,0:T(8,128)S(1)}, f32[1,128]{1,0:T(1,128)S(1)}, f32[1,128]{1,0:T(1,128)}) custom-call(f32[1024,2560]{1,0:T(8,128)} %copy-done, f32[1024,2560]{1,0:T(8,128)} %copy-done, f32[1024,2560]{1,0:T(8,128)} %copy-done, bf16[512,2048]{1,0:T(8,128)(2,1)} %copy-done.17, ...), custom_call_target="tpu_custom_call" | custom-call | tf_op jit(solution)/shard_map/pallas_call | solution.py:212
  415.8 9.3 %fusion.53 = bf16[512,2048]{1,0:T(8,128)(2,1)} fusion(bf16[512,1536]{1,0:T(8,128)(2,1)S(1)} %copy-done.65, bf16[2048,4608]{1,0:T(8,128)(2,1)} %all-gather.5.cloned.1.call-done.gate_ref.up_ref.down_ref), kind=kOutput, calls=%fused_computation.69 | convolution fusion | flops 3222274048 | bytes 9961472 | tf_op jit(solution)/shard_map/dot_general | solution.py:31
  425.1 7.7 %fusion.56 = bf16[512,2048]{1,0:T(8,128)(2,1)} fusion(bf16[512,1536]{1,0:T(8,128)(2,1)S(1)} %copy-done.64, bf16[2048,4608]{1,0:T(8,128)(2,1)} %all-gather.5.cloned.1.call-done.gate_ref.up_ref.down_ref), kind=kOutput, calls=%fused_computation.70 | convolution fusion | flops 3222274048 | bytes 9961472 | tf_op jit(solution)/shard_map/dot_general | solution.py:31
  436.1 6.3 shard_map.266
  442.5 10.7 %fusion.50.grad_ref = bf16[512,2048]{1,0:T(8,128)(2,1)} fusion(bf16[512,2048]{1,0:T(8,128)(2,1)S(1)} %get-tuple-element.143.one_ref, bf16[2048,4608]{1,0:T(8,128)(2,1)} %all-gather.3.cloned.1.call-done), kind=kOutput, calls=%fused_computation.68 | convolution fusion | flops 4296015872 | bytes 12582912 | tf_op jit(solution)/shard_map/dot_general | solution.py:27
  458.0 6.2 convolution_convert_fusion.5
  471.0 26.1 %shard_map.267 = (bf16[512,2048]{1,0:T(8,128)(2,1)}, bf16[1024,256]{1,0:T(8,128)(2,1)S(1)}, bf16[1024,256]{1,0:T(8,128)(2,1)S(1)}, f32[1,128]{1,0:T(1,128)S(1)}, f32[1,128]{1,0:T(1,128)S(1)}) custom-call(f32[1024,2560]{1,0:T(8,128)} %copy-done, f32[1024,2560]{1,0:T(8,128)} %copy-done, f32[1024,2560]{1,0:T(8,128)} %copy-done, bf16[512,2048]{1,0:T(8,128)(2,1)} %copy-done.19, ...), custom_call_target="tpu_custom_call" | custom-call | tf_op jit(solution)/shard_map/pallas_call | solution.py:212
  510.9 9.6 %fusion.7 = f32[512,2048]{1,0:T(8,128)} fusion(bf16[512,2560]{1,0:T(8,128)(2,1)S(1)} %slice_select_fusion, bf16[2048,4608]{1,0:T(8,128)(2,1)} %all-gather.3.cloned.1.call-done), kind=kOutput, calls=%fused_computation.10 | convolution fusion | flops 5368709120 | bytes 17301504 | tf_op jit(solution)/shard_map/dot_general | solution.py:31
  522.2 11.0 %fusion.38 = bf16[512,2048]{1,0:T(8,128)(2,1)} fusion(bf16[512,2560]{1,0:T(8,128)(2,1)S(1)} %pad_maximum_fusion.1, bf16[2048,4608]{1,0:T(8,128)(2,1)} %all-gather.3.cloned.1.call-done), kind=kOutput, calls=%fused_computation.64 | convolution fusion | flops 5369757696 | bytes 15204352 | tf_op jit(solution)/shard_map/dot_general | solution.py:31
  537.6 4.7 convolution_convert_fusion
  547.9 6.5 add_convert_fusion
  556.8 6.6 collective-permute-done.18
  569.0 26.3 %collective-permute-done.13 = bf16[512,2048]{1,0:T(8,128)(2,1)} collective-permute-done((bf16[512,2048]{1,0:T(8,128)(2,1)}, bf16[512,2048]{1,0:T(8,128)(2,1)}, u32[]{:S(2)}, u32[]{:S(2)}) %collective-permute-start.13) | collective-permute-done | bytes 2097184 | tf_op jit(solution)/shard_map/ppermute | solution.py:257
  595.9 5.6 add_add_fusion
  601.5 8.9 %collective-permute-done.16 = bf16[2,2,128,2048]{3,2,1,0:T(8,128)(2,1)} collective-permute-done((bf16[2,2,128,2048]{3,2,1,0:T(8,128)(2,1)}, bf16[2,2,128,2048]{3,2,1,0:T(8,128)(2,1)}, u32[]{:S(2)}, u32[]{:S(2)}) %collective-permute-start.16) | collective-permute-done | bytes 2097184 | tf_op jit(solution)/shard_map/ppermute | solution.py:253
  613.9 4.5 add_convert_fusion.5
  622.6 4.7 add_convert_fusion.4
  627.4 31.1 %collective-permute-done.20 = bf16[2,2,128,1280]{3,2,1,0:T(8,128)(2,1)S(1)} collective-permute-done((bf16[2,2,128,1280]{3,2,1,0:T(8,128)(2,1)S(1)}, bf16[2,2,128,1280]{3,2,1,0:T(8,128)(2,1)S(1)}, u32[]{:S(2)}, u32[]{:S(2)}) %collective-permute-start.20) | collective-permute-done | bytes 1310752 | tf_op jit(solution)/shard_map/ppermute | solution.py:253
  660.2 19.6 %collective-permute-done.21 = bf16[2,128,2048]{2,1,0:T(8,128)(2,1)S(1)} collective-permute-done((bf16[2,128,2048]{2,1,0:T(8,128)(2,1)S(1)}, bf16[2,128,2048]{2,1,0:T(8,128)(2,1)S(1)}, u32[]{:S(2)}, u32[]{:S(2)}) %collective-permute-start.21) | collective-permute-done | bytes 1048608 | tf_op jit(solution)/shard_map/ppermute | solution.py:253
  681.1 5.8 collective-permute-done.23
  703.6 8.1 %collective-permute-done.27 = bf16[2,128,1280]{2,1,0:T(8,128)(2,1)} collective-permute-done((bf16[2,128,1280]{2,1,0:T(8,128)(2,1)}, bf16[2,128,1280]{2,1,0:T(8,128)(2,1)}, u32[]{:S(2)}, u32[]{:S(2)}) %collective-permute-start.27) | collective-permute-done | bytes 655392 | tf_op jit(solution)/shard_map/ppermute | solution.py:253
  713.0 4.5 fusion.31
  719.6 5.2 fusion.28
  731.0 12.1 %collective-permute-done.35 = f32[1,4352]{1,0:T(1,128)S(1)} collective-permute-done((f32[1,4352]{1,0:T(1,128)S(1)}, f32[1,4352]{1,0:T(1,128)S(1)}, u32[]{:S(2)}, u32[]{:S(2)}) %collective-permute-start.35) | collective-permute-done | bytes 17440 | tf_op jit(solution)/shard_map/ppermute | solution.py:253
  748.2 11.7 %collective-permute-done.31 = bf16[128,1280]{1,0:T(8,128)(2,1)S(1)} collective-permute-done((bf16[128,1280]{1,0:T(8,128)(2,1)S(1)}, bf16[128,1280]{1,0:T(8,128)(2,1)S(1)}, u32[]{:S(2)}, u32[]{:S(2)}) %collective-permute-start.31) | collective-permute-done | bytes 327712 | tf_op jit(solution)/shard_map/ppermute | solution.py:253
  (323 shorter events, 169.2 us)
Async XLA Ops:
  7.2 104.7 %all-gather.3.cloned.1.call-start = ((), (), s32[]{:S(2)}) async-start(), calls=%async_computation | async-start | bytes 20054016 | tf_op jit(solution)/shard_map/all_gather | solution.py:485
  9.7 203.9 %all-gather.5.cloned.1.call-start = ((), (), s32[]{:S(2)}) async-start(), calls=%async_computation.1 | async-start | bytes 20054016 | tf_op jit(solution)/shard_map/all_gather | solution.py:489
  11.8 49.5 %collective-permute-start = (bf16[512,2048]{1,0:T(8,128)(2,1)S(1)}, bf16[512,2048]{1,0:T(8,128)(2,1)}, u32[]{:S(2)}, u32[]{:S(2)}) collective-permute-start(bf16[512,2048]{1,0:T(8,128)(2,1)S(1)} %copy-done.2), channel_id=1, source_target_pairs={{0,1},{1,0},{2,3},{3,2},{4,5},{5,4},{6,7},{7,6},{8,9},{9,8},{10,11... | collective-permute-start | bytes 6291464 | tf_op jit(solution)/shard_map/ppermute | solution.py:257
  14.8 90.7 %collective-permute-start.1 = (bf16[512,2048]{1,0:T(8,128)(2,1)}, bf16[512,2048]{1,0:T(8,128)(2,1)}, u32[]{:S(2)}, u32[]{:S(2)}) collective-permute-start(bf16[512,2048]{1,0:T(8,128)(2,1)} %own_ref.11), channel_id=1, source_target_pairs={{0,1},{1,0},{2,3},{3,2},{4,5},{5,4},{6,7},{7,6},{8,9},{9,8},{10,11... | collective-permute-start | bytes 6291464 | tf_op jit(solution)/shard_map/ppermute | solution.py:257
  17.0 47.9 %copy-start.73 = (f32[1,2048]{1,0:T(1,128)S(1)}, f32[1,2048]{1,0:T(1,128)}, u32[]{:S(2)}) copy-start(f32[1,2048]{1,0:T(1,128)} %param.27) | copy-start | bytes 24580
  70.1 35.4 %copy-start.3 = (bf16[512,2048]{1,0:T(8,128)(2,1)S(1)}, bf16[512,2048]{1,0:T(8,128)(2,1)}, u32[]{:S(2)}) copy-start(bf16[512,2048]{1,0:T(8,128)(2,1)} %own_ref.11) | copy-start | bytes 6291460
  156.8 48.8 %collective-permute-start.2 = (bf16[512,2048]{1,0:T(8,128)(2,1)}, bf16[512,2048]{1,0:T(8,128)(2,1)}, u32[]{:S(2)}, u32[]{:S(2)}) collective-permute-start(bf16[512,2048]{1,0:T(8,128)(2,1)} %fusion.41.part_ref), channel_id=1, source_target_pairs={{0,1},{1,0},{2,3},{3,2},{4,5},{5,4},{6,7},{7,6},{8,9},{9,8},{10,11... | collective-permute-start | bytes 6291464 | tf_op jit(solution)/shard_map/ppermute | solution.py:257
  191.3 58.5 %collective-permute-start.3 = (bf16[512,2048]{1,0:T(8,128)(2,1)}, bf16[512,2048]{1,0:T(8,128)(2,1)}, u32[]{:S(2)}, u32[]{:S(2)}) collective-permute-start(bf16[512,2048]{1,0:T(8,128)(2,1)} %fusion.44.part_ref), channel_id=1, source_target_pairs={{0,1},{1,0},{2,3},{3,2},{4,5},{5,4},{6,7},{7,6},{8,9},{9,8},{10,11... | collective-permute-start | bytes 6291464 | tf_op jit(solution)/shard_map/ppermute | solution.py:257
  245.8 70.4 %copy-start.27 = (bf16[512,2048]{1,0:T(8,128)(2,1)}, bf16[512,2048]{1,0:T(8,128)(2,1)S(1)}, u32[]{:S(2)}) copy-start(bf16[512,2048]{1,0:T(8,128)(2,1)S(1)} %fusion.59.part_ref) | copy-start | bytes 6291460
  300.5 20.2 %collective-permute-start.8 = (bf16[1024,1536]{1,0:T(8,128)(2,1)}, bf16[1024,1536]{1,0:T(8,128)(2,1)}, u32[]{:S(2)}, u32[]{:S(2)}) collective-permute-start(bf16[1024,1536]{1,0:T(8,128)(2,1)} %convolution_convert_fusion.4), channel_id=1, source_target_pairs={{0,2},{2,0},{4,6},{6,4},{8,10},{10,8},{12,14},{14,12},{16,18},{18,... | collective-permute-start | bytes 9437192 | tf_op jit(solution)/shard_map/ppermute | solution.py:253
  310.6 18.8 %collective-permute-start.4 = (bf16[1024,1536]{1,0:T(8,128)(2,1)}, bf16[1024,1536]{1,0:T(8,128)(2,1)}, u32[]{:S(2)}, u32[]{:S(2)}) collective-permute-start(bf16[1024,1536]{1,0:T(8,128)(2,1)} %convolution_convert_fusion.2), channel_id=1, source_target_pairs={{0,2},{2,0},{4,6},{6,4},{8,10},{10,8},{12,14},{14,12},{16,18},{18,... | collective-permute-start | bytes 9437192 | tf_op jit(solution)/shard_map/ppermute | solution.py:253
  316.1 22.0 %collective-permute-start.5 = (bf16[1024,1536]{1,0:T(8,128)(2,1)}, bf16[1024,1536]{1,0:T(8,128)(2,1)}, u32[]{:S(2)}, u32[]{:S(2)}) collective-permute-start(bf16[1024,1536]{1,0:T(8,128)(2,1)} %convolution_convert_fusion.3), channel_id=1, source_target_pairs={{0,2},{2,0},{4,6},{6,4},{8,10},{10,8},{12,14},{14,12},{16,18},{18,... | collective-permute-start | bytes 9437192 | tf_op jit(solution)/shard_map/ppermute | solution.py:253
  316.2 48.5 %collective-permute-start.6 = (bf16[512,2048]{1,0:T(8,128)(2,1)S(1)}, bf16[512,2048]{1,0:T(8,128)(2,1)S(1)}, u32[]{:S(2)}, u32[]{:S(2)}) collective-permute-start(bf16[512,2048]{1,0:T(8,128)(2,1)S(1)} %fusion.59.part_ref), channel_id=1, source_target_pairs={{0,1},{1,0},{2,3},{3,2},{4,5},{5,4},{6,7},{7,6},{8,9},{9,8},{10,11... | collective-permute-start | bytes 6291464 | tf_op jit(solution)/shard_map/ppermute | solution.py:257
  319.6 116.4 %collective-permute-start.7 = (bf16[512,2048]{1,0:T(8,128)(2,1)}, bf16[512,2048]{1,0:T(8,128)(2,1)}, u32[]{:S(2)}, u32[]{:S(2)}) collective-permute-start(bf16[512,2048]{1,0:T(8,128)(2,1)} %fusion.64.part_ref), channel_id=1, source_target_pairs={{0,1},{1,0},{2,3},{3,2},{4,5},{5,4},{6,7},{7,6},{8,9},{9,8},{10,11... | collective-permute-start | bytes 6291464 | tf_op jit(solution)/shard_map/ppermute | solution.py:257
  328.2 136.0 %collective-permute-start.9 = (bf16[2,2,128,1536]{3,2,1,0:T(8,128)(2,1)}, bf16[2,2,128,1536]{3,2,1,0:T(8,128)(2,1)}, u32[]{:S(2)}, u32[]{:S(2)}) collective-permute-start(bf16[2,2,128,1536]{3,2,1,0:T(8,128)(2,1)} %bitcast.12), channel_id=1, source_target_pairs={{0,4},{2,6},{4,0},{6,2},{8,12},{10,14},{12,8},{14,10},{16,20},{18,... | collective-permute-start | bytes 4718600 | tf_op jit(solution)/shard_map/ppermute | solution.py:253
  336.6 28.1 %copy-start.4 = (bf16[512,2048]{1,0:T(8,128)(2,1)S(1)}, bf16[512,2048]{1,0:T(8,128)(2,1)}, u32[]{:S(2)}) copy-start(bf16[512,2048]{1,0:T(8,128)(2,1)} %own_ref.11) | copy-start | bytes 6291460
  336.6 28.1 %copy-start.28 = (bf16[512,2048]{1,0:T(8,128)(2,1)S(1)}, bf16[512,2048]{1,0:T(8,128)(2,1)}, u32[]{:S(2)}) copy-start(bf16[512,2048]{1,0:T(8,128)(2,1)} %copy-done.27) | copy-start | bytes 6291460
  336.6 130.8 %collective-permute-start.10 = (bf16[2,2,128,1536]{3,2,1,0:T(8,128)(2,1)}, bf16[2,2,128,1536]{3,2,1,0:T(8,128)(2,1)}, u32[]{:S(2)}, u32[]{:S(2)}) collective-permute-start(bf16[2,2,128,1536]{3,2,1,0:T(8,128)(2,1)} %get-tuple-element.190), channel_id=1, source_target_pairs={{0,8},{2,10},{4,12},{6,14},{8,0},{10,2},{12,4},{14,6},{16,24},{18,... | collective-permute-start | bytes 4718600 | tf_op jit(solution)/shard_map/ppermute | solution.py:253
  381.6 34.1 %copy-start.65 = (bf16[512,1536]{1,0:T(8,128)(2,1)S(1)}, bf16[512,1536]{1,0:T(8,128)(2,1)}, u32[]{:S(2)}) copy-start(bf16[512,1536]{1,0:T(8,128)(2,1)} %get-tuple-element.125) | copy-start | bytes 4718596
  434.7 70.5 %collective-permute-start.11 = (bf16[2,2,128,1536]{3,2,1,0:T(8,128)(2,1)}, bf16[2,2,128,1536]{3,2,1,0:T(8,128)(2,1)}, u32[]{:S(2)}, u32[]{:S(2)}) collective-permute-start(bf16[2,2,128,1536]{3,2,1,0:T(8,128)(2,1)} %bitcast.16), channel_id=1, source_target_pairs={{0,4},{2,6},{4,0},{6,2},{8,12},{10,14},{12,8},{14,10},{16,20},{18,... | collective-permute-start | bytes 4718600 | tf_op jit(solution)/shard_map/ppermute | solution.py:253
  464.2 82.2 %collective-permute-start.14 = (bf16[1024,2048]{1,0:T(8,128)(2,1)}, bf16[1024,2048]{1,0:T(8,128)(2,1)}, u32[]{:S(2)}, u32[]{:S(2)}) collective-permute-start(bf16[1024,2048]{1,0:T(8,128)(2,1)} %convolution_convert_fusion.5), channel_id=1, source_target_pairs={{0,2},{2,0},{4,6},{6,4},{8,10},{10,8},{12,14},{14,12},{16,18},{18,... | collective-permute-start | bytes 12582920 | tf_op jit(solution)/shard_map/ppermute | solution.py:253
  501.3 32.0 %copy-start.46 = (bf16[1024,2048]{1,0:T(8,128)(2,1)}, bf16[1024,2048]{1,0:T(8,128)(2,1)S(1)}, u32[]{:S(2)}) copy-start(bf16[1024,2048]{1,0:T(8,128)(2,1)S(1)} %get-tuple-element.199) | copy-start | bytes 12582916
  501.4 20.6 %collective-permute-start.12 = (bf16[2,128,1536]{2,1,0:T(8,128)(2,1)}, bf16[2,128,1536]{2,1,0:T(8,128)(2,1)S(1)}, u32[]{:S(2)}, u32[]{:S(2)}) collective-permute-start(bf16[2,128,1536]{2,1,0:T(8,128)(2,1)} %get-tuple-element.206), channel_id=1, source_target_pairs={{0,8},{2,10},{4,12},{6,14},{8,0},{10,2},{12,4},{14,6},{16,24},{18,... | collective-permute-start | bytes 2359304 | tf_op jit(solution)/shard_map/ppermute | solution.py:253
  502.9 40.0 %collective-permute-start.15 = (bf16[2,128,1536]{2,1,0:T(8,128)(2,1)S(1)}, bf16[2,128,1536]{2,1,0:T(8,128)(2,1)S(1)}, u32[]{:S(2)}, u32[]{:S(2)}) collective-permute-start(bf16[2,128,1536]{2,1,0:T(8,128)(2,1)S(1)} %get-tuple-element.204), channel_id=1, source_target_pairs={{0,4},{2,6},{4,0},{6,2},{8,12},{10,14},{12,8},{14,10},{16,20},{18,... | collective-permute-start | bytes 2359304 | tf_op jit(solution)/shard_map/ppermute | solution.py:253
  504.8 32.8 %copy-start.40 = (bf16[1024,2560]{1,0:T(8,128)(2,1)}, bf16[1024,2560]{1,0:T(8,128)(2,1)S(1)}, u32[]{:S(2)}) copy-start(bf16[1024,2560]{1,0:T(8,128)(2,1)S(1)} %pad_maximum_fusion) | copy-start | bytes 15728644
  510.5 55.4 %collective-permute-start.19 = (bf16[2,128,1536]{2,1,0:T(8,128)(2,1)}, bf16[2,128,1536]{2,1,0:T(8,128)(2,1)}, u32[]{:S(2)}, u32[]{:S(2)}) collective-permute-start(bf16[2,128,1536]{2,1,0:T(8,128)(2,1)} %get-tuple-element.202), channel_id=1, source_target_pairs={{0,8},{2,10},{4,12},{6,14},{8,0},{10,2},{12,4},{14,6},{16,24},{18,... | collective-permute-start | bytes 2359304 | tf_op jit(solution)/shard_map/ppermute | solution.py:253
  537.6 75.4 %collective-permute-start.17 = (bf16[1024,1280]{1,0:T(8,128)(2,1)}, bf16[1024,1280]{1,0:T(8,128)(2,1)}, u32[]{:S(2)}, u32[]{:S(2)}) collective-permute-start(bf16[1024,1280]{1,0:T(8,128)(2,1)} %convolution_convert_fusion.1), channel_id=1, source_target_pairs={{0,2},{2,0},{4,6},{6,4},{8,10},{10,8},{12,14},{14,12},{16,18},{18,... | collective-permute-start | bytes 7864328 | tf_op jit(solution)/shard_map/ppermute | solution.py:253
  542.3 80.1 %collective-permute-start.22 = (bf16[1024,1280]{1,0:T(8,128)(2,1)}, bf16[1024,1280]{1,0:T(8,128)(2,1)}, u32[]{:S(2)}, u32[]{:S(2)}) collective-permute-start(bf16[1024,1280]{1,0:T(8,128)(2,1)} %convolution_convert_fusion), channel_id=1, source_target_pairs={{0,2},{2,0},{4,6},{6,4},{8,10},{10,8},{12,14},{14,12},{16,18},{18,... | collective-permute-start | bytes 7864328 | tf_op jit(solution)/shard_map/ppermute | solution.py:253
  542.9 20.4 %collective-permute-start.18 = (bf16[128,1536]{1,0:T(8,128)(2,1)S(1)}, bf16[128,1536]{1,0:T(8,128)(2,1)S(1)}, u32[]{:S(2)}, u32[]{:S(2)}) collective-permute-start(bf16[128,1536]{1,0:T(8,128)(2,1)S(1)} %get-tuple-element.218), channel_id=1, source_target_pairs={{0,16},{2,18},{4,20},{6,22},{8,24},{10,26},{12,28},{14,30},{16,0},... | collective-permute-start | bytes 1179656 | tf_op jit(solution)/shard_map/ppermute | solution.py:253
  546.4 48.8 %collective-permute-start.13 = (bf16[512,2048]{1,0:T(8,128)(2,1)}, bf16[512,2048]{1,0:T(8,128)(2,1)}, u32[]{:S(2)}, u32[]{:S(2)}) collective-permute-start(bf16[512,2048]{1,0:T(8,128)(2,1)} %fusion.53), channel_id=1, source_target_pairs={{0,1},{1,0},{2,3},{3,2},{4,5},{5,4},{6,7},{7,6},{8,9},{9,8},{10,11... | collective-permute-start | bytes 6291464 | tf_op jit(solution)/shard_map/ppermute | solution.py:257
  563.4 47.0 %collective-permute-start.16 = (bf16[2,2,128,2048]{3,2,1,0:T(8,128)(2,1)}, bf16[2,2,128,2048]{3,2,1,0:T(8,128)(2,1)}, u32[]{:S(2)}, u32[]{:S(2)}) collective-permute-start(bf16[2,2,128,2048]{3,2,1,0:T(8,128)(2,1)} %bitcast.21), channel_id=1, source_target_pairs={{0,4},{2,6},{4,0},{6,2},{8,12},{10,14},{12,8},{14,10},{16,20},{18,... | collective-permute-start | bytes 6291464 | tf_op jit(solution)/shard_map/ppermute | solution.py:253
  565.9 30.0 %copy-start.59 = (bf16[512,2048]{1,0:T(8,128)(2,1)S(1)}, bf16[512,2048]{1,0:T(8,128)(2,1)}, u32[]{:S(2)}) copy-start(bf16[512,2048]{1,0:T(8,128)(2,1)} %fusion.56) | copy-start | bytes 6291460
  565.9 147.1 %collective-permute-start.28 = (bf16[512,2048]{1,0:T(8,128)(2,1)}, bf16[512,2048]{1,0:T(8,128)(2,1)}, u32[]{:S(2)}, u32[]{:S(2)}) collective-permute-start(bf16[512,2048]{1,0:T(8,128)(2,1)} %fusion.38), channel_id=1, source_target_pairs={{0,1},{1,0},{2,3},{3,2},{4,5},{5,4},{6,7},{7,6},{8,9},{9,8},{10,11... | collective-permute-start | bytes 6291464 | tf_op jit(solution)/shard_map/ppermute | solution.py:257
  595.2 93.1 %collective-permute-start.24 = (bf16[128,1536]{1,0:T(8,128)(2,1)}, bf16[128,1536]{1,0:T(8,128)(2,1)S(1)}, u32[]{:S(2)}, u32[]{:S(2)}) collective-permute-start(bf16[128,1536]{1,0:T(8,128)(2,1)} %get-tuple-element.214), channel_id=1, source_target_pairs={{0,16},{2,18},{4,20},{6,22},{8,24},{10,26},{12,28},{14,30},{16,0},... | collective-permute-start | bytes 1179656 | tf_op jit(solution)/shard_map/ppermute | solution.py:253
  610.4 79.5 %collective-permute-start.25 = (bf16[128,1536]{1,0:T(8,128)(2,1)S(1)}, bf16[128,1536]{1,0:T(8,128)(2,1)S(1)}, u32[]{:S(2)}, u32[]{:S(2)}) collective-permute-start(bf16[128,1536]{1,0:T(8,128)(2,1)S(1)} %get-tuple-element.216), channel_id=1, source_target_pairs={{0,16},{2,18},{4,20},{6,22},{8,24},{10,26},{12,28},{14,30},{16,0},... | collective-permute-start | bytes 1179656 | tf_op jit(solution)/shard_map/ppermute | solution.py:253
  618.6 39.9 %collective-permute-start.20 = (bf16[2,2,128,1280]{3,2,1,0:T(8,128)(2,1)S(1)}, bf16[2,2,128,1280]{3,2,1,0:T(8,128)(2,1)S(1)}, u32[]{:S(2)}, u32[]{:S(2)}) collective-permute-start(bf16[2,2,128,1280]{3,2,1,0:T(8,128)(2,1)S(1)} %get-tuple-element.196), channel_id=1, source_target_pairs={{0,8},{2,10},{4,12},{6,14},{8,0},{10,2},{12,4},{14,6},{16,24},{18,... | collective-permute-start | bytes 3932168 | tf_op jit(solution)/shard_map/ppermute | solution.py:253
  622.5 57.3 %collective-permute-start.21 = (bf16[2,128,2048]{2,1,0:T(8,128)(2,1)S(1)}, bf16[2,128,2048]{2,1,0:T(8,128)(2,1)S(1)}, u32[]{:S(2)}, u32[]{:S(2)}) collective-permute-start(bf16[2,128,2048]{2,1,0:T(8,128)(2,1)S(1)} %get-tuple-element.198), channel_id=1, source_target_pairs={{0,8},{2,10},{4,12},{6,14},{8,0},{10,2},{12,4},{14,6},{16,24},{18,... | collective-permute-start | bytes 3145736 | tf_op jit(solution)/shard_map/ppermute | solution.py:253
  658.5 28.4 %collective-permute-start.23 = (bf16[2,2,128,1280]{3,2,1,0:T(8,128)(2,1)S(1)}, bf16[2,2,128,1280]{3,2,1,0:T(8,128)(2,1)S(1)}, u32[]{:S(2)}, u32[]{:S(2)}) collective-permute-start(bf16[2,2,128,1280]{3,2,1,0:T(8,128)(2,1)S(1)} %bitcast.143), channel_id=1, source_target_pairs={{0,4},{2,6},{4,0},{6,2},{8,12},{10,14},{12,8},{14,10},{16,20},{18,... | collective-permute-start | bytes 3932168 | tf_op jit(solution)/shard_map/ppermute | solution.py:253
  688.5 13.8 %collective-permute-start.26 = (bf16[2,128,1280]{2,1,0:T(8,128)(2,1)}, bf16[2,128,1280]{2,1,0:T(8,128)(2,1)}, u32[]{:S(2)}, u32[]{:S(2)}) collective-permute-start(bf16[2,128,1280]{2,1,0:T(8,128)(2,1)} %get-tuple-element.208), channel_id=1, source_target_pairs={{0,4},{2,6},{4,0},{6,2},{8,12},{10,14},{12,8},{14,10},{16,20},{18,... | collective-permute-start | bytes 1966088 | tf_op jit(solution)/shard_map/ppermute | solution.py:253
  689.9 21.8 %collective-permute-start.27 = (bf16[2,128,1280]{2,1,0:T(8,128)(2,1)}, bf16[2,128,1280]{2,1,0:T(8,128)(2,1)}, u32[]{:S(2)}, u32[]{:S(2)}) collective-permute-start(bf16[2,128,1280]{2,1,0:T(8,128)(2,1)} %get-tuple-element.210), channel_id=1, source_target_pairs={{0,8},{2,10},{4,12},{6,14},{8,0},{10,2},{12,4},{14,6},{16,24},{18,... | collective-permute-start | bytes 1966088 | tf_op jit(solution)/shard_map/ppermute | solution.py:253
  695.5 34.4 %collective-permute-start.29 = (bf16[128,2048]{1,0:T(8,128)(2,1)}, bf16[128,2048]{1,0:T(8,128)(2,1)S(1)}, u32[]{:S(2)}, u32[]{:S(2)}) collective-permute-start(bf16[128,2048]{1,0:T(8,128)(2,1)} %get-tuple-element.212), channel_id=1, source_target_pairs={{0,16},{2,18},{4,20},{6,22},{8,24},{10,26},{12,28},{14,30},{16,0},... | collective-permute-start | bytes 1572872 | tf_op jit(solution)/shard_map/ppermute | solution.py:253
  717.6 1.3 collective-permute-start.32
  718.8 5.9 collective-permute-start.33
  724.8 5.0 collective-permute-start.34
  724.9 23.2 %collective-permute-start.30 = (bf16[128,1280]{1,0:T(8,128)(2,1)S(1)}, bf16[128,1280]{1,0:T(8,128)(2,1)S(1)}, u32[]{:S(2)}, u32[]{:S(2)}) collective-permute-start(bf16[128,1280]{1,0:T(8,128)(2,1)S(1)} %get-tuple-element.222), channel_id=1, source_target_pairs={{0,16},{2,18},{4,20},{6,22},{8,24},{10,26},{12,28},{14,30},{16,0},... | collective-permute-start | bytes 983048 | tf_op jit(solution)/shard_map/ppermute | solution.py:253
  729.8 13.3 %collective-permute-start.35 = (f32[1,4352]{1,0:T(1,128)S(1)}, f32[1,4352]{1,0:T(1,128)S(1)}, u32[]{:S(2)}, u32[]{:S(2)}) collective-permute-start(f32[1,4352]{1,0:T(1,128)S(1)} %add.162), channel_id=1, source_target_pairs={{0,16},{2,18},{4,20},{6,22},{8,24},{10,26},{12,28},{14,30},{16,0},... | collective-permute-start | bytes 52232 | tf_op jit(solution)/shard_map/ppermute | solution.py:253
  743.2 3.8 collective-permute-start.36
  744.7 15.2 %collective-permute-start.31 = (bf16[128,1280]{1,0:T(8,128)(2,1)S(1)}, bf16[128,1280]{1,0:T(8,128)(2,1)S(1)}, u32[]{:S(2)}, u32[]{:S(2)}) collective-permute-start(bf16[128,1280]{1,0:T(8,128)(2,1)S(1)} %get-tuple-element.224), channel_id=1, source_target_pairs={{0,16},{2,18},{4,20},{6,22},{8,24},{10,26},{12,28},{14,30},{16,0},... | collective-permute-start | bytes 983048 | tf_op jit(solution)/shard_map/ppermute | solution.py:253
  (73 other events, 531.0 us)
Sparse Core Ops, SparseCore 0:
  10.2 101.6 all-gather.2
  113.5 98.9 all-gather.4

commit v3 on v2

v3 whole, which is shorter than its diff:
```python
import functools
import math

import jax
import jax.numpy as jnp
import numpy as np
from jax import lax
from jax.experimental import pallas as pl
from jax.experimental.pallas import tpu as pltpu
from jax.sharding import PartitionSpec as P

HD = 128
EPS = 1e-06
THETA = 1000000.0
SCALE = HD ** -0.5
LOG2E = math.log2(math.e)
NT = (((1,), (1,)), ((), ()))
BF = jnp.bfloat16
F32 = jnp.float32


def params(mib):
    return pltpu.CompilerParams(vmem_limit_bytes=mib * 2**20)


def dot(left, right):
    return jnp.dot(left, right, preferred_element_type=F32)


def dot_nt(left, right):
    return lax.dot_general(left, right, NT, preferred_element_type=F32)


def dot_tn(left, right):
    return lax.dot_general(left, right, (((0,), (0,)), ((), ())), preferred_element_type=F32)


def head_norm(values, gain, cosine, sine):
    scale = lax.rsqrt(jnp.mean(values * values, axis=-1, keepdims=True) + EPS)
    normed = values * scale * gain
    return normed * cosine + pltpu.roll(normed, HD // 2, 1) * sine


def head_norm_back(values, gain, cosine, sine, grad_rot):
    scale = lax.rsqrt(jnp.mean(values * values, axis=-1, keepdims=True) + EPS)
    grad = grad_rot * cosine - pltpu.roll(grad_rot, HD // 2, 1) * sine
    scaled = grad * gain
    inner = jnp.mean(scaled * values, axis=-1, keepdims=True)
    grad_values = scale * scaled - values * (scale * scale * scale) * inner
    return grad_values, jnp.sum(grad * values * scale, axis=0, keepdims=True)


def causal(offset, rows, columns):
    key = lax.broadcasted_iota(jnp.int32, (rows, columns), 0) + offset
    return key <= lax.broadcasted_iota(jnp.int32, (rows, columns), 1)


def attn_fwd_kernel(block, q_ref, k_ref, v_ref, qg_ref, kg_ref, qcos_ref, qsin_ref, kcos_ref, ksin_ref, *rest):
    out_ref, lse_ref, qs, ks, vt, ps, ss, mix, sums = rest[-9:]
    chunk, per = q_ref.shape[0], q_ref.shape[1] // HD
    base = k_ref.shape[0] - chunk
    tile = min(64, block)

    @pl.when(pl.program_id(1) == 0)
    def _():
        ks[...] = head_norm(k_ref[...], kg_ref[...], kcos_ref[...], ksin_ref[...]).astype(BF)
        vt[...] = v_ref[...].astype(BF).T

    for h in range(per):
        lanes = slice(h * HD, (h + 1) * HD)
        qs[h] = head_norm(q_ref[:, lanes], qg_ref[...], qcos_ref[...], qsin_ref[...]).astype(BF)
    pairs = [(h, i) for h in range(per) for i in range(chunk // block)]

    def place(h, i):
        start = base + i * block
        return slice(h * HD, (h + 1) * HD), slice(i * block, (i + 1) * block), start, start + block

    for h, i in pairs:
        lanes, cols, start, end = place(h, i)
        ss[h, :end, cols] = dot_nt(ks[:end], qs[h, cols])
    for h, i in pairs:
        lanes, cols, start, end = place(h, i)
        total = jnp.zeros((8, block), F32)
        for r in range(0, end, tile):
            probs = jnp.exp2(ss[h, r : r + tile, cols] * (SCALE * LOG2E))
            if r >= start:
                probs = jnp.where(causal(r - start, tile, block), probs, 0.0)
            total = total + jnp.sum(probs.reshape(tile // 8, 8, block), axis=0)
            ps[h, r : r + tile, cols] = probs.astype(BF)
        sums[h, :, cols] = jnp.sum(total, axis=0, keepdims=True)
    for h, i in pairs:
        lanes, cols, start, end = place(h, i)
        mix[h, :, cols] = dot(vt[:, :end], ps[h, :end, cols])
    for h, i in pairs:
        lanes, cols, start, end = place(h, i)
        out_ref[cols, lanes] = (mix[h, :, cols] * (1.0 / sums[h, :, cols])).T.astype(BF)
    lse_ref[...] = jnp.log2(sums[...])


def attn_specs(raw, q_cols, kv_cols, chunk, index, per):
    heads, kv = q_cols // HD, kv_cols // HD
    steps = heads // kv // per
    keys = (index + 1) * chunk
    head_in = pl.BlockSpec((chunk, per * HD), lambda k, g: (index, k * steps + g))
    head = pl.BlockSpec((chunk, per * HD), lambda k, g: (0, k * steps + g))
    lse = pl.BlockSpec((per, 1, chunk), lambda k, g: (k * steps + g, 0, 0))
    gain = pl.BlockSpec((1, HD), lambda k, g: (0, 0))
    query_table = pl.BlockSpec((chunk, HD), lambda k, g: (index, 0))

    def of_keys(rows):
        return (
            pl.BlockSpec((rows, HD), lambda k, g: (0, heads + k)),
            pl.BlockSpec((rows, HD), lambda k, g: (0, heads + kv + k)),
            pl.BlockSpec((rows, HD), lambda k, g: (0, 0)),
            pl.BlockSpec((rows, HD), lambda k, g: (0, k)),
        )

    return heads, kv, steps, keys, head_in, head, lse, gain, query_table, of_keys


def attention_fwd(raw, q_cols, kv_cols, chunk, index, query_g, key_g, cosine, sine, earlier):
    seq = raw.shape[0]
    more = [] if earlier is None else [earlier]
    per = min(4, q_cols // kv_cols)
    heads, kv, steps, keys, head_in, head, lse, gain, query_table, of_keys = attn_specs(
        raw, q_cols, kv_cols, chunk, index, per
    )
    key_in, value_in, key_table, _ = of_keys(keys)
    return pl.pallas_call(
        functools.partial(attn_fwd_kernel, min(256, chunk)),
        grid=(kv, steps),
        in_specs=[head_in, key_in, value_in, gain, gain, query_table, query_table, key_table, key_table]
        + [pl.BlockSpec(memory_space=pl.ANY)] * len(more),
        out_specs=[head_in, lse],
        out_shape=[
            pltpu.HBM((seq, heads * HD), BF),
            jax.ShapeDtypeStruct((heads, 1, chunk), F32),
        ],
        scratch_shapes=[
            pltpu.VMEM((per, chunk, HD), BF),
            pltpu.VMEM((keys, HD), BF),
            pltpu.VMEM((HD, keys), BF),
            pltpu.VMEM((per, keys, chunk), BF),
            pltpu.VMEM((per, keys, chunk), F32),
            pltpu.VMEM((per, HD, chunk), F32),
            pltpu.VMEM((per, 1, chunk), F32),
        ],
        input_output_aliases={9: 0} if more else {},
        compiler_params=params(48),
    )(raw, raw, raw, query_g, key_g, cosine, sine, cosine, sine, *more)


def attn_bwd_kernel(
    block, keys, first, last, q_ref, k_ref, v_ref, ctx_ref, grad_ref, lse_ref, qg_ref, kg_ref,
    qcos_ref, qsin_ref, kcos_ref, ksin_ref, *rest,
):
    if first:
        dq_ref, dk_ref, dv_ref, dqg_ref, dkg_ref, qs, ks, kt, vs, ps, ds, dks, dvs, ss, gs, deltas, dqs = rest
    else:
        (dk_in, dv_in, dqg_in, dq_in, dq_ref, dk_ref, dv_ref, dqg_ref, dkg_ref,
         qs, ks, kt, vs, ps, ds, dks, dvs, ss, gs, deltas, dqs) = rest
    chunk, per = q_ref.shape[0], q_ref.shape[1] // HD
    base = (keys - chunk) // block
    kv_id, g_id = pl.program_id(0), pl.program_id(1)

    @pl.when(g_id == 0)
    def _():
        rotated = head_norm(k_ref[:keys], kg_ref[...], kcos_ref[:keys], ksin_ref[:keys]).astype(BF)
        ks[...] = rotated
        kt[...] = rotated.T
        vs[...] = v_ref[:keys].astype(BF)
        dks[...] = jnp.zeros_like(dks) if first else dk_in[...]
        dvs[...] = jnp.zeros_like(dvs) if first else dv_in[...]

    @pl.when((g_id == 0) & (kv_id == 0))
    def _():
        dqg_ref[...] = jnp.zeros_like(dqg_ref) if first else dqg_in[...]
        dkg_ref[...] = jnp.zeros_like(dkg_ref)

    tile = min(64, block)
    for h in range(per):
        lanes = slice(h * HD, (h + 1) * HD)
        qs[h] = head_norm(q_ref[:, lanes], qg_ref[...], qcos_ref[...], qsin_ref[...]).astype(BF)
    pairs = [(h, i) for h in range(per) for i in range(chunk // block)]

    def place(h, i):
        start = (base + i) * block
        return slice(h * HD, (h + 1) * HD), slice(i * block, (i + 1) * block), start, start + block

    def first_products(h):
        for i in range(chunk // block):
            lanes, cols, start, end = place(h, i)
            product = grad_ref[cols, lanes].astype(F32) * ctx_ref[cols, lanes].astype(F32)
            deltas[h, :, cols] = jnp.sum(product.T, axis=0, keepdims=True)
            ss[h % 2, :end, cols] = dot_nt(ks[:end], qs[h, cols])
            gs[h % 2, :end, cols] = dot_nt(vs[:end], grad_ref[cols, lanes])

    def weights(h):
        for i in range(chunk // block):
            lanes, cols, start, end = place(h, i)
            delta, lse = deltas[h, :, cols], lse_ref[h, :, cols]
            for r in range(0, end, tile):
                rows = slice(r, r + tile)
                probs = jnp.exp2(ss[h % 2, rows, cols] * (SCALE * LOG2E) - lse)
                if r >= start:
                    probs = jnp.where(causal(r - start, tile, block), probs, 0.0)
                ps[h % 2, rows, cols] = probs.astype(BF)
                ds[h % 2, rows, cols] = (probs * (gs[h % 2, rows, cols] - delta)).astype(BF)

    def second_products(h):
        lanes = slice(h * HD, (h + 1) * HD)
        for j in range(keys // block):
            rows = slice(j * block, (j + 1) * block)
            start = max(0, j - base) * block
            dvs[rows] += dot(ps[h % 2, rows, start:], grad_ref[start:, lanes])
            dks[rows] += dot(ds[h % 2, rows, start:], qs[h, start:])
        for i in range(chunk // block):
            lanes, cols, start, end = place(h, i)
            dqs[h % 2, :, cols] = dot(kt[:, :end], ds[h % 2, :end, cols])

    def last_part(h):
        total = jnp.zeros((1, HD), F32)
        for i in range(chunk // block):
            lanes, cols, start, end = place(h, i)
            grad_raw, part = head_norm_back(
                q_ref[cols, lanes], qg_ref[...], qcos_ref[cols], qsin_ref[cols], dqs[h % 2, :, cols].T * SCALE
            )
            dq_ref[cols, lanes] = grad_raw.astype(BF)
            total = total + part
        return total

    gain_sum = jnp.zeros((1, HD), F32)
    first_products(0)
    for h in range(per):
        if h + 1 < per:
            first_products(h + 1)
        weights(h)
        if h:
            gain_sum = gain_sum + last_part(h - 1)
        second_products(h)
    gain_sum = gain_sum + last_part(per - 1)
    dqg_ref[...] += gain_sum

    @pl.when(g_id == pl.num_programs(1) - 1)
    def _():
        if last:
            grad_raw, part = head_norm_back(k_ref[...], kg_ref[...], kcos_ref[...], ksin_ref[...], dks[...] * SCALE)
            dk_ref[...] = grad_raw.astype(BF)
            dv_ref[...] = dvs[...].astype(BF)
            dkg_ref[...] += part
        else:
            dk_ref[...] = dks[...]
            dv_ref[...] = dvs[...]


def attention_bwd(
    raw, q_cols, kv_cols, chunk, index, context, grad_context, lse_rows, query_g, key_g, cosine, sine, earlier, last
):
    seq = raw.shape[0]
    per = min(4, q_cols // kv_cols)
    heads, kv, steps, keys, head_in, head, lse, gain, query_table, of_keys = attn_specs(
        raw, q_cols, kv_cols, chunk, index, per
    )
    key_in, value_in, key_table, key_out = of_keys(seq)
    first = earlier is None
    more = [] if first else list(earlier)
    kind = BF if last else F32
    return pl.pallas_call(
        functools.partial(attn_bwd_kernel, min(256, chunk), keys, first, last),
        grid=(kv, steps),
        in_specs=[head_in, key_in, value_in, head_in, head, lse, gain, gain, query_table, query_table, key_table, key_table]
        + ([] if first else [key_out, key_out, gain, pl.BlockSpec(memory_space=pl.ANY)]),
        out_specs=[head_in, key_out, key_out, gain, gain],
        out_shape=[
            jax.ShapeDtypeStruct((seq, heads * HD), BF),
            jax.ShapeDtypeStruct((seq, kv * HD), kind),
            jax.ShapeDtypeStruct((seq, kv * HD), kind),
            jax.ShapeDtypeStruct((1, HD), F32),
            jax.ShapeDtypeStruct((1, HD), F32),
        ],
        scratch_shapes=[
            pltpu.VMEM((per, chunk, HD), BF),
            pltpu.VMEM((keys, HD), BF),
            pltpu.VMEM((HD, keys), BF),
            pltpu.VMEM((keys, HD), BF),
            pltpu.VMEM((2, keys, chunk), BF),
            pltpu.VMEM((2, keys, chunk), BF),
            pltpu.VMEM((seq, HD), F32),
            pltpu.VMEM((seq, HD), F32),
            pltpu.VMEM((2, keys, chunk), F32),
            pltpu.VMEM((2, keys, chunk), F32),
            pltpu.VMEM((per, 1, chunk), F32),
            pltpu.VMEM((2, HD, chunk), F32),
        ],
        input_output_aliases={} if first else {15: 0},
        compiler_params=params(58),
    )(raw, raw, raw, in_hbm(context), grad_context, lse_rows, query_g, key_g, cosine, sine, cosine, sine, *more)


def rope_tables(seq):
    position = lax.iota(F32, seq)
    freq = THETA ** (-2.0 * lax.iota(F32, HD // 2) / HD)
    angle = position[:, None] * freq[None, :]
    cosine, sine = jnp.cos(angle), jnp.sin(angle)
    return jnp.concatenate([cosine, cosine], axis=1), jnp.concatenate([-sine, sine], axis=1)


def bits_of(count):
    return count.bit_length() - 1


def swap(value, bit):
    count = lax.axis_size("dp")
    return lax.ppermute(value, "dp", [(i, i ^ (1 << bit)) for i in range(count)])


def swap_pair(value):
    return lax.ppermute(value, "tensor", [(0, 1), (1, 0)])


def after(value, *needed):
    return lax.optimization_barrier((value, needed))[0]


def in_hbm(value):
    return pltpu.with_memory_space_constraint(value, pltpu.HBM)


def tie_kernel(*refs):
    pass


def tie(value, *needed):
    anywhere = pl.BlockSpec(memory_space=pl.ANY)
    return pl.pallas_call(
        tie_kernel,
        in_specs=[anywhere] * (1 + len(needed)),
        out_specs=anywhere,
        out_shape=jax.ShapeDtypeStruct(value.shape, value.dtype),
        input_output_aliases={0: 0},
    )(value, *needed)


def block_order():
    count = lax.axis_size("dp")
    bits = bits_of(count)
    reverse = np.array([int(format(i, "b").zfill(bits)[::-1], 2) if bits else 0 for i in range(count)], np.int32)
    return jnp.asarray(reverse) ^ lax.axis_index("dp").astype(jnp.int32)


def join_kernel(count, parts, turn_ref, order_ref, one_ref, two_ref, *out_refs):
    block = one_ref.shape[1] // count

    def fill(ref):
        for i in range(count):
            column = pl.multiple_of(order_ref[i] * block, block)
            out_ref, at = out_refs[i // (count // parts)], i % (count // parts)
            out_ref[:, at * block : (at + 1) * block] = ref[:, pl.ds(column, block)]

    @pl.when(pl.program_id(0) == turn_ref[0])
    def _():
        fill(one_ref)

    @pl.when(pl.program_id(0) != turn_ref[0])
    def _():
        fill(two_ref)


def join(one, two, turn, order, parts):
    rows, width = one.shape
    count = order.shape[0]
    tile = min(256, rows)
    turn = jnp.asarray(turn, jnp.int32)
    if (width // count) % 128:
        both = jnp.where(turn == 0, jnp.concatenate([one, two], axis=0), jnp.concatenate([two, one], axis=0))
        both = jnp.take(both.reshape(2 * rows, count, -1), order, axis=1).reshape(2 * rows, width)
        return jnp.split(both, parts, axis=1)
    steps = rows // tile
    half = pl.BlockSpec((tile, width), lambda h, r: (r, 0))
    scalar = pl.BlockSpec(memory_space=pltpu.SMEM)
    return pl.pallas_call(
        functools.partial(join_kernel, count, parts),
        grid=(2, steps),
        in_specs=[scalar, scalar, half, half],
        out_specs=[pl.BlockSpec((tile, width // parts), lambda h, r: (h * steps + r, 0))] * parts,
        out_shape=[jax.ShapeDtypeStruct((2 * rows, width // parts), one.dtype)] * parts,
        compiler_params=params(32),
    )(turn.reshape(1), order, one, two)


def mean_square(values):
    return lax.rsqrt(jnp.mean(values * values, axis=-1, keepdims=True) + EPS)


def mid_kernel(base_ref, part_ref, got_ref, gain_ref, *rest):
    mid_ref, normed_ref = rest[-2:]
    mid = base_ref[...].astype(F32) + (part_ref[...].astype(F32) + got_ref[...].astype(F32))
    mid_ref[...] = mid
    normed_ref[...] = (mid * mean_square(mid) * gain_ref[...]).astype(BF)


def middle(base, part, got, gain, index, earlier):
    rows, width = part.shape
    tile = min(128, rows)
    block = pl.BlockSpec((tile, width), lambda r: (r, 0))
    place = pl.BlockSpec((tile, width), lambda r: (index * (rows // tile) + r, 0))
    more = [] if earlier is None else [earlier]
    return pl.pallas_call(
        mid_kernel,
        grid=(rows // tile,),
        in_specs=[place, block, block, pl.BlockSpec((1, width), lambda r: (0, 0))]
        + [pl.BlockSpec(memory_space=pl.ANY)] * len(more),
        out_specs=[block, place],
        out_shape=[pltpu.HBM((rows, width), F32), pltpu.HBM(base.shape, BF)],
        input_output_aliases={4: 1} if more else {},
        compiler_params=params(32),
    )(base, part, got, gain, *more)


def norm_back(values, gain, grad):
    scale = mean_square(values)
    scaled = grad * gain
    inner = jnp.mean(scaled * values, axis=-1, keepdims=True)
    grad_values = scale * scaled - values * (scale * scale * scale) * inner
    return grad_values, jnp.sum(grad * values * scale, axis=0, keepdims=True)


def mid_back_kernel(base_ref, part_ref, got_ref, mid_ref, gain_ref, out_ref, low_ref, sum_ref):
    grad = part_ref[...].astype(F32) + got_ref[...].astype(F32)
    back, part = norm_back(mid_ref[...], gain_ref[...], grad)
    total = base_ref[...].astype(F32) + back
    out_ref[...] = total
    low_ref[...] = total.astype(BF)

    @pl.when(pl.program_id(0) == 0)
    def _():
        sum_ref[...] = jnp.zeros_like(sum_ref)

    sum_ref[...] += part


def middle_back(base, part, got, mid, gain, index):
    rows, width = part.shape
    tile = min(128, rows)
    block = pl.BlockSpec((tile, width), lambda r: (r, 0))
    line = pl.BlockSpec((1, width), lambda r: (0, 0))
    return pl.pallas_call(
        mid_back_kernel,
        grid=(rows // tile,),
        in_specs=[pl.BlockSpec((tile, width), lambda r: (index * (rows // tile) + r, 0)), block, block, block, line],
        out_specs=[block, block, line],
        out_shape=[
            pltpu.HBM((rows, width), F32),
            jax.ShapeDtypeStruct((rows, width), BF),
            jax.ShapeDtypeStruct((1, width), F32),
        ],
        compiler_params=params(32),
    )(base, part, got, in_hbm(mid), gain)


def expert_kernel(unit, cols, x_ref, cot_ref, gate_ref, up_ref, down_ref, route_ref, weight_ref, *rest):
    out_ref = rest[-1]
    step, count = pl.program_id(0), pl.num_programs(0)
    rows, block = x_ref.shape[0], gate_ref.shape[1]
    tile = min(256, rows)

    def place(kind):
        return pl.ds(pl.multiple_of((kind * count + step) * block, block), block)

    for r in range(rows // tile):
        part = slice(r * tile, (r + 1) * tile)
        shares = []
        for k in range(block // unit):
            expert = (step * (block // unit) + k) // (cols // unit)
            share = jnp.sum(jnp.where(route_ref[part] == expert, weight_ref[part], 0.0), axis=-1, keepdims=True)
            shares.append(jnp.broadcast_to(share, (tile, unit)))
        share = jnp.concatenate(shares, axis=1)
        gate = dot(x_ref[part], gate_ref[...])
        up = dot(x_ref[part], up_ref[...])
        grad_hidden = dot(cot_ref[part], down_ref[...]) * share
        sigma = 1.0 / (1.0 + jnp.exp(-gate))
        silu = gate * sigma
        out_ref[part, place(0)] = (grad_hidden * up * (sigma + silu * (1.0 - sigma))).astype(BF)
        out_ref[part, place(1)] = (grad_hidden * silu).astype(BF)
        out_ref[part, place(2)] = (silu * up * share).astype(BF)


def expert_part(normed, cot, weights, routes, route_weights, index, experts, earlier):
    width = normed.shape[1]
    flat = weights.shape[1] // 3
    cols = flat // experts
    unit = math.gcd(cols, 128)
    block = 2 * unit if flat % (2 * unit) == 0 else unit
    steps = flat // block
    seq = routes.shape[0]
    rows = seq // 2
    pair = pl.BlockSpec((rows, routes.shape[1]), lambda e: (index, 0))
    half = pl.BlockSpec((rows, width), lambda e: (index, 0))
    more = [] if earlier is None else [earlier]
    return pl.pallas_call(
        functools.partial(expert_kernel, unit, cols),
        grid=(steps,),
        in_specs=[half, half]
        + [pl.BlockSpec((width, block), lambda e, k=k: (0, k * steps + e)) for k in range(3)]
        + [pair, pair]
        + [pl.BlockSpec(memory_space=pl.ANY)] * len(more),
        out_specs=pl.BlockSpec((rows, 3 * flat), lambda e: (index, 0)),
        out_shape=jax.ShapeDtypeStruct((seq, 3 * flat), BF),
        input_output_aliases={7: 0} if more else {},
        compiler_params=params(56),
    )(in_hbm(normed), cot, weights, weights, weights, routes, route_weights, *more)


def expert_weight_kernel(cut, normed_ref, cot_ref, act_ref, out_ref):
    step = pl.program_id(0)

    @pl.when(step < cut)
    def _():
        out_ref[...] = dot_tn(normed_ref[...], act_ref[...]).astype(BF)

    @pl.when(step >= cut)
    def _():
        out_ref[...] = dot_tn(cot_ref[...], act_ref[...]).astype(BF)


def expert_weights(normed, cot, acts, block):
    seq, width = normed.shape
    flat = acts.shape[1] // 3
    full = pl.BlockSpec((seq, width), lambda j: (0, 0))
    return pl.pallas_call(
        functools.partial(expert_weight_kernel, 2 * flat // block),
        grid=(3 * flat // block,),
        in_specs=[full, full, pl.BlockSpec((seq, block), lambda j: (0, j))],
        out_specs=pl.BlockSpec((width, block), lambda j: (0, j)),
        out_shape=jax.ShapeDtypeStruct((width, 3 * flat), BF),
        compiler_params=params(56),
    )(in_hbm(normed), cot, acts)


def product_kernel(count, form, turn_ref, *refs):
    total = form(refs[0][...], refs[count][...])
    for i in range(1, count):
        total = total + form(refs[i][...], refs[count + i][...])
    refs[2 * count][...] = total.astype(refs[2 * count].dtype)


def product(form, lefts, rights, rows, steps, block, kind, turn):
    return pl.pallas_call(
        functools.partial(product_kernel, len(lefts), form),
        grid_spec=pltpu.PrefetchScalarGridSpec(
            num_scalar_prefetch=1,
            grid=(steps,),
            in_specs=[pl.BlockSpec(shape, index) for _, shape, index in lefts + rights],
            out_specs=pl.BlockSpec((rows, block), lambda i, turn_ref: (0, i)),
        ),
        out_shape=jax.ShapeDtypeStruct((rows, steps * block), kind),
        compiler_params=params(56),
    )(turn.reshape(1), *[item[0] for item in lefts + rights])


def fold(keep, received):
    return (keep.astype(F32) + received.astype(F32)).astype(BF)


def sum_all(value):
    for bit in range(bits_of(lax.axis_size("dp"))):
        value = value + swap(value, bit)
    return value + swap_pair(value)


class Reduction:
    def __init__(self, lefts, right, order, ready, *needed):
        self.order = list(order)
        self.lefts, self.right = lefts, right
        self.rows = 2 * lefts[0].shape[1] // lax.axis_size("dp")
        self.axes = list(range(1, bits_of(lax.axis_size("dp"))))
        self.sent = dot_tn(after(lefts[1], *needed), right).astype(BF)
        self.got = swap(tie(self.sent, *ready), 0)

    def total(self, *needed):
        total = dot_tn(after(self.lefts[0], *needed), self.right) + self.got.astype(F32)
        return total.astype(BF).reshape((2,) * len(self.axes) + (self.rows, -1))

    def keep(self, *needed):
        held = self.total(*needed)
        self.send(held)
        return held

    def keep_two(self, other, cut, *needed):
        held = self.total(*needed)
        rest = Reduction.__new__(Reduction)
        rest.order, rest.axes = list(other), list(self.axes)
        self.send(held[..., :cut])
        rest.send(held[..., cut:])
        return rest, held

    def send(self, held):
        axis = self.axes.index(self.order[0])
        self.mine = lax.index_in_dim(held, 0, axis, keepdims=False)
        self.got = swap(lax.index_in_dim(held, 1, axis, keepdims=False), self.order[0])

    def fold(self, *needed):
        self.axes.remove(self.order.pop(0))
        mine = after(self.mine, *needed) if needed else self.mine
        return fold(mine, self.got)

    def step(self, *needed):
        held = self.fold(*needed)
        self.send(held)
        return held

    def join(self, other, *needed):
        held = jnp.concatenate([self.fold(*needed), other.fold(*needed)], axis=-1)
        self.send(held)
        return held

    def finish(self, *needed):
        while len(self.order) > 1:
            self.step(*needed)
        self.axes.remove(self.order.pop(0))
        return after(self.mine, *needed).astype(F32) + self.got.astype(F32)


def body(
    tokens, cotangent, routes, route_weights, query_weight, key_weight, value_weight, out_weight,
    gate_weight, up_weight, down_weight, attn_gain, ffn_gain, query_gain, key_gain,
):
    turn = lax.axis_index("tensor").astype(jnp.int32)
    chunk = tokens.shape[0]
    seq = 2 * chunk
    width = tokens.shape[1]
    order = block_order()
    plain = lax.iota(jnp.int32, order.shape[0])
    cosine, sine = rope_tables(seq)
    experts, hidden_cols = gate_weight.shape[2], gate_weight.shape[3]
    flat = experts * hidden_cols
    q_cols, kv_cols = query_weight.shape[2], key_weight.shape[2]
    bits = bits_of(lax.axis_size("dp"))
    straight = list(range(1, bits))
    crossed = straight if bits < 3 else [2, 1] + straight[2:]
    wide, tall = min(512, 2 * kv_cols), min(512, width)

    def select(zero, one):
        return jnp.where(turn == 0, zero, one)

    attn_w = lax.all_gather(
        jnp.concatenate([out_weight[0], query_weight[0], key_weight[0], value_weight[0]], axis=1),
        "dp", axis=0, tiled=True,
    )
    ffn_w = lax.all_gather(
        jnp.concatenate([w[0].reshape(-1, flat) for w in (gate_weight, up_weight, down_weight)], axis=1),
        "dp", axis=0, tiled=True,
    )

    tokens_other = swap_pair(tokens)
    cot_other = swap_pair(after(cotangent, tokens_other))
    (tokens_all,) = join(tokens, tokens_other, turn, plain, 1)
    resid = tokens_all.astype(F32)
    normed = (resid * mean_square(resid) * attn_gain).astype(BF)
    normed_rel = join(normed[:chunk], normed[chunk:], 0, order, 2)

    raw = product(
        dot,
        [(after(normed, normed_rel), (seq, width), lambda i, t: (0, 0))],
        [(attn_w, (width, wide), lambda i, t: (0, q_cols // wide + i))],
        seq, (q_cols + 2 * kv_cols) // wide, wide, F32, turn,
    )
    lse, part, got = {}, {}, {}
    context = None
    for index in (1, 0):
        context, lse[index] = attention_fwd(
            raw, q_cols, kv_cols, chunk, index, query_gain, key_gain, cosine, sine, context
        )
        part[index] = product(
            dot_nt,
            [(in_hbm(context), (chunk, q_cols), lambda i, t, index=index: (index, 0))],
            [(attn_w, (tall, q_cols), lambda i, t: (i, 0))],
            chunk, width // tall, tall, BF, turn,
        )
        got[index] = swap_pair(part[index])
        last = part[index]
        context = after(context, last)

    cot_other = after(cot_other, last)
    (cot_all,) = join(cotangent, cot_other, turn, plain, 1)
    last = cot_all

    mid, back_part, back_got = {}, {}, {}
    normed_f = None
    acts = None
    for index in (1, 0):
        mid[index], normed_f = middle(tokens_all, after(part[index], last), got[index], ffn_gain, index, normed_f)
        acts = expert_part(normed_f, cot_all, ffn_w, routes[0], route_weights[0], index, experts, acts)
        if index == 0:
            ffn_parts_grad = expert_weights(normed_f, cot_all, acts, wide)
            ffn_grad = lax.psum_scatter(ffn_parts_grad, "dp", scatter_dimension=0, tiled=True).astype(F32)
            acts = after(acts, ffn_parts_grad)
        back_part[index] = product(
            dot_nt,
            [(acts, (chunk, 2 * flat), lambda i, t, index=index: (index, 0))],
            [(ffn_w, (tall, 2 * flat), lambda i, t: (i, 0))],
            chunk, width // tall, tall, BF, turn,
        )
        if index == 0:
            back_part[0] = tie(back_part[0], back_got[1])
        back_got[index] = swap_pair(back_part[index])
        last = back_part[index]
        acts, normed_f = after(acts, last), after(normed_f, last)

    def expert_out(who, *needed):
        return product(
            dot_nt,
            [(after(acts, *needed), (chunk, flat), lambda i, t: (who(t[0]), 2))],
            [(ffn_w, (tall, flat), lambda i, t: (i, 2))],
            chunk, width // tall, tall, BF, turn,
        )

    grad_mid, grad_mid_b, ffn_parts, grad_context = {}, {}, {}, {}
    earlier = None
    for index in (1, 0):
        grad_mid[index], grad_mid_b[index], ffn_parts[index] = middle_back(
            cot_all, after(back_part[index], last), back_got[index], mid[index], ffn_gain, index
        )
        grad_context[index] = product(
            dot,
            [(grad_mid_b[index], (chunk, width), lambda i, t: (0, 0))],
            [(attn_w, (width, wide), lambda i, t: (0, i))],
            chunk, q_cols // wide, wide, BF, turn,
        )
        last = grad_context[index]
        if index == 0:
            grad_mid_rel = join(after(grad_mid_b[0], last), grad_mid_b[1], 0, order, 2)
            out_sum = Reduction(grad_mid_rel, context, straight, [])
            out_theirs = expert_out(lambda t: 1 - t, out_sum.sent)
            out_got = swap_pair(tie(out_theirs, back_got[0]))
            last = out_sum.keep(out_theirs)
        dq, dk, dv, query_part, key_part = attention_bwd(
            raw, q_cols, kv_cols, chunk, index, context, after(grad_context[index], last), lse[index],
            query_gain, key_gain, cosine, sine, earlier, index == 0,
        )
        earlier = (dk, dv, query_part, dq)
        last = dq

    dkv = jnp.concatenate([dk, dv], axis=1)

    def normed_back(who, *needed):
        return product(
            dot_nt,
            [
                (after(dq, *needed), (chunk, q_cols), lambda i, t: (who(t[0]), 0)),
                (dkv, (chunk, 2 * kv_cols), lambda i, t: (who(t[0]), 0)),
            ],
            [
                (attn_w, (tall, q_cols), lambda i, t: (i, 1)),
                (attn_w, (tall, 2 * kv_cols), lambda i, t: (i, q_cols // kv_cols)),
            ],
            chunk, width // tall, tall, BF, turn,
        )

    grad_qkv = jnp.concatenate([dq, dkv], axis=1)
    qkv_sum = Reduction(normed_rel, grad_qkv, straight, [])
    grad_theirs = normed_back(lambda t: 1 - t, qkv_sum.sent)
    rest_sum, last = qkv_sum.keep_two(crossed, grad_qkv.shape[1] // 2, grad_theirs)
    grad_got = swap_pair(grad_theirs)
    last = out_sum.step(last)
    grad_mine = normed_back(lambda t: t, last)
    out_mine = expert_out(lambda t: t, grad_mine)
    last = qkv_sum.step(out_mine)
    last = rest_sum.step(last)
    last = out_sum.step(last)
    output = (select(mid[0], mid[1]) + (after(out_mine, last).astype(F32) + out_got.astype(F32))).astype(BF)
    last = qkv_sum.step(output)
    last = rest_sum.step(last)
    grad_normed = after(grad_mine, last).astype(F32) + grad_got.astype(F32)
    grad_one, attn_part = norm_back(tokens.astype(F32), attn_gain, grad_normed)
    tokens_grad = select(grad_mid[0], grad_mid[1]) + grad_one
    ffn_part = (ffn_parts[0] + ffn_parts[1]) * 0.5
    small = jnp.concatenate([attn_part, ffn_part, query_part, key_part], axis=1)
    small = sum_all(small)
    out_grad = out_sum.finish(tokens_grad)
    rest_grad = rest_sum.finish(out_grad)
    qkv_grad = jnp.concatenate([qkv_sum.finish(rest_grad), rest_grad], axis=1)

    def expert(index):
        return ffn_grad[:, index * flat : (index + 1) * flat].reshape(1, -1, experts, hidden_cols)

    return (
        output,
        tokens_grad,
        qkv_grad[None, :, :q_cols],
        qkv_grad[None, :, q_cols : q_cols + kv_cols],
        qkv_grad[None, :, q_cols + kv_cols :],
        out_grad[None],
        expert(0),
        expert(1),
        expert(2),
        small[:, :width],
        small[:, width : 2 * width],
        small[:, 2 * width : 2 * width + HD],
        small[:, 2 * width + HD :],
    )


def solution(mesh):
    return jax.shard_map(
        body,
        mesh=mesh,
        in_specs=(
            P(("dp", "tensor"), None),
            P(("dp", "tensor"), None),
            P(None, "dp", None),
            P(None, "dp", None),
            P(None, "dp", "tensor"),
            P(None, "dp", "tensor"),
            P(None, "dp", "tensor"),
            P(None, "dp", "tensor"),
            P(None, "dp", None, "tensor"),
            P(None, "dp", None, "tensor"),
            P(None, "dp", None, "tensor"),
            P(),
            P(),
            P(),
            P(),
        ),
        out_specs=(
            P(("dp", "tensor"), None),
            P(("dp", "tensor"), None),
            P(None, "dp", "tensor"),
            P(None, "dp", "tensor"),
            P(None, "dp", "tensor"),
            P(None, "dp", "tensor"),
            P(None, "dp", None, "tensor"),
            P(None, "dp", None, "tensor"),
            P(None, "dp", None, "tensor"),
            P(),
            P(),
            P(),
            P(),
        ),
        check_vma=False,
    )
```

time: 773 us -> 650 us (0.84)
  matrix products: 179 us -> 31.4 us
  Pallas kernels: 167 us -> 286 us
  local copies, waits for them, and re-layouts: 66.1 us -> 33.8 us
  waiting for transfers between devices: 251 us -> 220 us
  other arithmetic: 51.4 us -> 30.4 us
  starting transfers between devices: 38.7 us -> 29 us
    pallas_call x10 -> x26, Pallas kernels: 70.3 us -> 213 us  [the longest x11 112 us: product(): pl.pallas_call(functools.partial(product_kernel, len(lefts), form), grid_...]
    dot_general x11 -> x0, matrix products: 116 us -> none  [the longest x8 78.6 us: dot_nt(): return lax.dot_general(left, right, NT, preferred_element_type=F32)]
    ppermute x9, waiting for transfers between devices: 139 us -> 62 us  [swap_pair(): return lax.ppermute(value, 'tensor', [(0, 1), (1, 0)])]
    all_gather x1, waiting for transfers between devices: 0.7 us -> 36.7 us  [body(): lax.all_gather(jnp.concatenate([out_weight[0], query_weight[0], key_weigh...]
    dot_general x12 -> x4, matrix products: 63.7 us -> 31.4 us  [dot_tn(): lax.dot_general(left, right, (((0,), (0,)), ((), ())), preferred_element_...]
    slice x13 -> x3, local copies, waits for them, and re-layouts: 17.6 us -> 2.47 us  [the longest x1 1.51 us: expert(): ffn_grad[:, index * flat:(index + 1) * flat]]
    pallas_call x2, Pallas kernels: 36.2 us -> 24.6 us  [attention_fwd(): pl.pallas_call(functools.partial(attn_fwd_kernel, min(256, chunk)), grid=...]
    pallas_call x2, Pallas kernels: 60.2 us -> 48.8 us  [attention_bwd(): pl.pallas_call(functools.partial(attn_bwd_kernel, min(256, chunk), keys,...]
  transfers between devices with their start and end apart: 39 -> 27, of which waited for: 20 -> 13; matrix products, arithmetic and copies ran while one was open for 32% -> 11% of each run, Pallas kernels for 18% -> 44%
where the time goes in v3:
time: 650 us; the launch traced here: 645 us
  Pallas kernels  286 us (44%)
  waiting for transfers between devices  220 us (34%)
  local copies, waits for them, and re-layouts  33.8 us (5%)
  matrix products  31.4 us (5%)
  other arithmetic  30.4 us (5%)
  starting transfers between devices  29 us (4%)
  between operations  14.7 us (2%)
    ppermute x15, waiting for transfers between devices, swap(): return lax.ppermute(value, 'dp', [(i, i ^ 1 << bit) for i in range(count)])  114 us
    pallas_call x11, Pallas kernels, product(): pl.pallas_call(functools.partial(product_kernel, len(lefts), form), grid_...  112 us
    ppermute x9, waiting for transfers between devices, swap_pair(): return lax.ppermute(value, 'tensor', [(0, 1), (1, 0)])  62 us
    pallas_call x2, Pallas kernels, attention_bwd(): pl.pallas_call(functools.partial(attn_bwd_kernel, min(256, chunk), keys,...  48.8 us
    all_gather x1, waiting for transfers between devices, body(): lax.all_gather(jnp.concatenate([out_weight[0], query_weight[0], key_weigh...  36.7 us
    pallas_call x2, Pallas kernels, expert_part(): pl.pallas_call(functools.partial(expert_kernel, unit, cols), grid=(steps,...  35.3 us
    dot_general x4, matrix products, dot_tn(): lax.dot_general(left, right, (((0,), (0,)), ((), ())), preferred_element_...  31.4 us
    pallas_call x1, Pallas kernels, expert_weights(): pl.pallas_call(functools.partial(expert_weight_kernel, 2 * flat // block)...  27 us
  transfers between devices with their start and end apart: 27, of which 13 were waited for; matrix products, arithmetic and copies ran while one was open for 11% of the time, Pallas kernels for 44%

profile of v3, /device:TPU:0, one launch (start us, length us, event | category | flops | bytes accessed | tf_op | source)
XLA Modules:
  0.0 645.2 jit_solution(1683916794774510673)
XLA Ops:
  7.3 2.4 pad_maximum_fusion
  11.2 3.0 collective-permute-start
  16.6 43.6 %collective-permute-done.two_ref = bf16[512,2048]{1,0:T(8,128)(2,1)} collective-permute-done((bf16[512,2048]{1,0:T(8,128)(2,1)}, bf16[512,2048]{1,0:T(8,128)(2,1)}, u32[]{:S(2)}, u32[]{:S(2)}) %collective-permute-start) | collective-permute-done | bytes 2097184 | tf_op jit(solution)/shard_map/ppermute | solution.py:318
  61.9 4.9 shard_map.255.base_ref
  75.2 36.7 %all-gather.3.cloned.1.call-done.refs_1_.refs_2_.refs_3_ = bf16[2048,4608]{1,0:T(8,128)(2,1)} async-done(((bf16[128,4608]{1,0:T(8,128)(2,1)}), bf16[2048,4608]{1,0:T(8,128)(2,1)}) %all-gather.3.cloned.1.call-update) | async-done | bytes 18874384 | tf_op jit(solution)/shard_map/all_gather | solution.py:646
  111.9 16.0 %shard_map.257.q_ref.k_ref.v_ref = f32[1024,2560]{1,0:T(8,128)} custom-call(s32[1]{0:T(128)} %bitcast.turn_ref, bf16[1024,2048]{1,0:T(8,128)(2,1)} %copy-done.30, bf16[2048,4608]{1,0:T(8,128)(2,1)} %all-gather.3.cloned.1.call-done.refs_1_.refs_2_.refs_3_), custom_call_target="tpu_custom_call" | custom-call | tf_op jit(solution)/shard_map/pallas_call | solution.py:548
  128.0 13.8 %shard_map.258 = (bf16[1024,2048]{1,0:T(8,128)(2,1)}, f32[16,1,512]{2,1,0:T(1,128)S(1)}) custom-call(f32[1024,2560]{1,0:T(8,128)} %shard_map.257.q_ref.k_ref.v_ref, f32[1024,2560]{1,0:T(8,128)} %shard_map.257.q_ref.k_ref.v_ref, f32[1024,2560]{1,0:T(8,128)} %shard_map.257.q_ref.k_ref.v_ref, f32[1,128]{1,0:T(1,128)S(1)} %copy-done.20, ...), custom_call_target="tpu_custom_call" | custom-call | tf_op jit(solution)/shard_map/pallas_call | solution.py:129
  142.3 8.9 %shard_map.259.part_ref = bf16[512,2048]{1,0:T(8,128)(2,1)} custom-call(s32[1]{0:T(128)} %bitcast.turn_ref, bf16[1024,2048]{1,0:T(8,128)(2,1)} %get-tuple-element.75.refs_0_.rest_0_, bf16[2048,4608]{1,0:T(8,128)(2,1)} %all-gather.3.cloned.1.call-done.refs_1_.refs_2_.refs_3_), custom_call_target="tpu_custom_call" | custom-call | tf_op jit(solution)/shard_map/pallas_call | solution.py:548
  153.0 10.9 %shard_map.260 = (bf16[1024,2048]{1,0:T(8,128)(2,1)}, f32[16,1,512]{2,1,0:T(1,128)S(1)}) custom-call(f32[1024,2560]{1,0:T(8,128)} %shard_map.257.q_ref.k_ref.v_ref, f32[1024,2560]{1,0:T(8,128)} %shard_map.257.q_ref.k_ref.v_ref, f32[1024,2560]{1,0:T(8,128)} %shard_map.257.q_ref.k_ref.v_ref, f32[1,128]{1,0:T(1,128)S(1)} %copy-done.20, ...), custom_call_target="tpu_custom_call", output_to_operand_aliasing={{0}: (9, {})} | custom-call | tf_op jit(solution)/shard_map/pallas_call | solution.py:129
  164.5 8.9 %shard_map.261.part_ref = bf16[512,2048]{1,0:T(8,128)(2,1)} custom-call(s32[1]{0:T(128)} %bitcast.turn_ref, bf16[1024,2048]{1,0:T(8,128)(2,1)} %get-tuple-element.89.refs_0_.ctx_ref, bf16[2048,4608]{1,0:T(8,128)(2,1)} %all-gather.3.cloned.1.call-done.refs_1_.refs_2_.refs_3_), custom_call_target="tpu_custom_call" | custom-call | tf_op jit(solution)/shard_map/pallas_call | solution.py:548
  175.8 4.9 shard_map.262.cot_ref.base_ref
  182.9 17.1 %collective-permute-done.2.got_ref = bf16[512,2048]{1,0:T(8,128)(2,1)} collective-permute-done((bf16[512,2048]{1,0:T(8,128)(2,1)}, bf16[512,2048]{1,0:T(8,128)(2,1)}, u32[]{:S(2)}, u32[]{:S(2)}) %collective-permute-start.2) | collective-permute-done | bytes 2097184 | tf_op jit(solution)/shard_map/ppermute | solution.py:318
  200.0 5.1 shard_map.263
  205.1 7.3 %all-gather.5.cloned.1.call-done.gate_ref.up_ref.down_ref.refs_1_ = bf16[2048,4608]{1,0:T(8,128)(2,1)} async-done(((bf16[128,4608]{1,0:T(8,128)(2,1)}), bf16[2048,4608]{1,0:T(8,128)(2,1)}) %all-gather.5.cloned.1.call-update) | async-done | bytes 18874384 | tf_op jit(solution)/shard_map/all_gather | solution.py:650
  212.5 17.6 %shard_map.264.refs_0_.rest_0_ = bf16[1024,4608]{1,0:T(8,128)(2,1)} custom-call(bf16[1024,2048]{1,0:T(8,128)(2,1)} %get-tuple-element.82.x_ref.rest_0_, bf16[1024,2048]{1,0:T(8,128)(2,1)} %copy-done, bf16[2048,4608]{1,0:T(8,128)(2,1)} %all-gather.5.cloned.1.call-done.gate_ref.up_ref.down_ref.refs_1_, ...), custom_call_target="tpu_custom_call" | custom-call | tf_op jit(solution)/shard_map/pallas_call | solution.py:500
  230.1 11.5 %shard_map.265.part_ref = bf16[512,2048]{1,0:T(8,128)(2,1)} custom-call(s32[1]{0:T(128)} %bitcast.turn_ref, bf16[1024,4608]{1,0:T(8,128)(2,1)} %shard_map.264.refs_0_.rest_0_, bf16[2048,4608]{1,0:T(8,128)(2,1)} %all-gather.5.cloned.1.call-done.gate_ref.up_ref.down_ref.refs_1_), custom_call_target="tpu_custom_call" | custom-call | tf_op jit(solution)/shard_map/pallas_call | solution.py:548
  244.4 5.2 shard_map.266
  249.6 17.7 %shard_map.267.act_ref.refs_0_ = bf16[1024,4608]{1,0:T(8,128)(2,1)} custom-call(bf16[1024,2048]{1,0:T(8,128)(2,1)} %get-tuple-element.85.x_ref.normed_ref, bf16[1024,2048]{1,0:T(8,128)(2,1)} %copy-done, bf16[2048,4608]{1,0:T(8,128)(2,1)} %all-gather.5.cloned.1.call-done.gate_ref.up_ref.down_ref.refs_1_, ...), custom_call_target="tpu_custom_call", output_to_operand_aliasing={{}: (7, {})} | custom-call | tf_op jit(solution)/shard_map/pallas_call | solution.py:500
  267.3 27.0 %shard_map.268 = bf16[2048,4608]{1,0:T(8,128)(2,1)} custom-call(bf16[1024,2048]{1,0:T(8,128)(2,1)} %get-tuple-element.85.x_ref.normed_ref, bf16[1024,2048]{1,0:T(8,128)(2,1)} %copy-done, bf16[1024,4608]{1,0:T(8,128)(2,1)} %shard_map.267.act_ref.refs_0_), custom_call_target="tpu_custom_call" | custom-call | tf_op jit(solution)/shard_map/pallas_call | solution.py:530
  294.3 12.0 %shard_map.269.refs_0_ = bf16[512,2048]{1,0:T(8,128)(2,1)} custom-call(s32[1]{0:T(128)} %bitcast.turn_ref, bf16[1024,4608]{1,0:T(8,128)(2,1)} %shard_map.267.act_ref.refs_0_, bf16[2048,4608]{1,0:T(8,128)(2,1)} %all-gather.5.cloned.1.call-done.gate_ref.up_ref.down_ref.refs_1_), custom_call_target="tpu_custom_call" | custom-call | tf_op jit(solution)/shard_map/pallas_call | solution.py:548
  308.3 3.0 copy-done.1
  311.3 7.8 %shard_map.271 = (f32[512,2048]{1,0:T(8,128)}, bf16[512,2048]{1,0:T(8,128)(2,1)S(1)}, f32[1,2048]{1,0:T(1,128)S(1)}) custom-call(bf16[1024,2048]{1,0:T(8,128)(2,1)S(1)} %copy-done.1, bf16[512,2048]{1,0:T(8,128)(2,1)S(1)} %copy-done.13, bf16[512,2048]{1,0:T(8,128)(2,1)} %collective-permute-done.4.refs_1_.got_ref, f32[512,2048]{1,0:T(8,128)} %get-tuple-element.84.mid_ref, ...), custom_call_target="tpu_custom_call" | custom-call | tf_op jit(solution)/shard_map/pallas_call | solution.py:447
  320.4 9.4 %shard_map.272.grad_ref = bf16[512,2048]{1,0:T(8,128)(2,1)} custom-call(s32[1]{0:T(128)} %bitcast.turn_ref, bf16[512,2048]{1,0:T(8,128)(2,1)} %copy-done.9, bf16[2048,4608]{1,0:T(8,128)(2,1)} %all-gather.3.cloned.1.call-done.refs_1_.refs_2_.refs_3_), custom_call_target="tpu_custom_call" | custom-call | tf_op jit(solution)/shard_map/pallas_call | solution.py:548
  329.8 27.7 %shard_map.273 = (bf16[1024,2048]{1,0:T(8,128)(2,1)}, f32[1024,256]{1,0:T(8,128)}, f32[1024,256]{1,0:T(8,128)}, f32[1,128]{1,0:T(1,128)}, f32[1,128]{1,0:T(1,128)}) custom-call(f32[1024,2560]{1,0:T(8,128)} %shard_map.257.q_ref.k_ref.v_ref, f32[1024,2560]{1,0:T(8,128)} %shard_map.257.q_ref.k_ref.v_ref, f32[1024,2560]{1,0:T(8,128)} %shard_map.257.q_ref.k_ref.v_ref, ...), custom_call_target="tpu_custom_call" | custom-call | tf_op jit(solution)/shard_map/pallas_call | solution.py:268
  359.2 7.2 %shard_map.274 = (f32[512,2048]{1,0:T(8,128)}, bf16[512,2048]{1,0:T(8,128)(2,1)S(1)}, f32[1,2048]{1,0:T(1,128)S(1)}) custom-call(bf16[1024,2048]{1,0:T(8,128)(2,1)S(1)} %copy-done.2, bf16[512,2048]{1,0:T(8,128)(2,1)S(1)} %copy-done.8, bf16[512,2048]{1,0:T(8,128)(2,1)} %collective-permute-done.5.got_ref.refs_1_, f32[512,2048]{1,0:T(8,128)} %get-tuple-element.83.mid_ref, ...), custom_call_target="tpu_custom_call" | custom-call | tf_op jit(solution)/shard_map/pallas_call | solution.py:447
  367.7 9.1 %shard_map.275.grad_ref = bf16[512,2048]{1,0:T(8,128)(2,1)} custom-call(s32[1]{0:T(128)} %bitcast.turn_ref, bf16[512,2048]{1,0:T(8,128)(2,1)} %copy-done.11, bf16[2048,4608]{1,0:T(8,128)(2,1)} %all-gather.3.cloned.1.call-done.refs_1_.refs_2_.refs_3_), custom_call_target="tpu_custom_call" | custom-call | tf_op jit(solution)/shard_map/pallas_call | solution.py:548
  380.0 6.4 convolution_convert_fusion.1.refs_0_
  386.5 21.1 %shard_map.276 = (bf16[1024,2048]{1,0:T(8,128)(2,1)}, bf16[1024,256]{1,0:T(8,128)(2,1)}, bf16[1024,256]{1,0:T(8,128)(2,1)}, f32[1,128]{1,0:T(1,128)}, f32[1,128]{1,0:T(1,128)}) custom-call(f32[1024,2560]{1,0:T(8,128)} %shard_map.257.q_ref.k_ref.v_ref, f32[1024,2560]{1,0:T(8,128)} %shard_map.257.q_ref.k_ref.v_ref, ...), custom_call_target="tpu_custom_call", output_to_operand_aliasing={{0}: (15, {})} | custom-call | tf_op jit(solution)/shard_map/pallas_call | solution.py:268
  407.6 2.7 constant_dynamic-update-slice_fusion.2
  413.1 7.6 %convolution_convert_fusion.refs_0_ = bf16[1024,2560]{1,0:T(8,128)(2,1)} fusion(bf16[1024,1024]{1,0:T(8,128)(2,1)S(1)} %copy-done.27, bf16[1024,2560]{1,0:T(8,128)(2,1)S(1)} %get-tuple-element.157), kind=kOutput, calls=%fused_computation.11 | convolution fusion | flops 5371330560 | bytes 12582912 | tf_op jit(solution)/shard_map/dot_general | solution.py:35
  423.2 10.2 %shard_map.280 = bf16[512,2048]{1,0:T(8,128)(2,1)} custom-call(s32[1]{0:T(128)} %bitcast.turn_ref, bf16[1024,2048]{1,0:T(8,128)(2,1)} %get-tuple-element.111.refs_0_, bf16[1024,512]{1,0:T(8,128)(2,1)} %copy-done.35, bf16[2048,4608]{1,0:T(8,128)(2,1)} %all-gather.3.cloned.1.call-done.refs_1_.refs_2_.refs_3_, ...), custom_call_target="tpu_custom_call" | custom-call | tf_op jit(solution)/shard_map/pallas_call | solution.py:548
  435.2 7.9 %shard_map.278.refs_0_ = bf16[512,2048]{1,0:T(8,128)(2,1)} custom-call(s32[1]{0:T(128)} %bitcast.turn_ref, bf16[1024,4608]{1,0:T(8,128)(2,1)} %shard_map.267.act_ref.refs_0_, bf16[2048,4608]{1,0:T(8,128)(2,1)} %all-gather.5.cloned.1.call-done.gate_ref.up_ref.down_ref.refs_1_), custom_call_target="tpu_custom_call" | custom-call | tf_op jit(solution)/shard_map/pallas_call | solution.py:548
  443.4 9.5 %add_convert_fusion.1 = bf16[1024,2048]{1,0:T(8,128)(2,1)S(1)} fusion(bf16[1024,2048]{1,0:T(8,128)(2,1)} %collective-permute-done.6, bf16[1024,1024]{1,0:T(8,128)(2,1)} %copy-done.28, bf16[1024,2048]{1,0:T(8,128)(2,1)} %get-tuple-element.89.refs_0_.ctx_ref), kind=kOutput, calls=%fused_computation.6 | convolution fusion | flops 4301258752 | bytes 14680064 | tf_op jit(solution)/shard_map/dot_general | solution.py:35
  454.9 7.8 %add_convert_fusion = bf16[1024,2560]{1,0:T(8,128)(2,1)S(1)} fusion(bf16[1024,2560]{1,0:T(8,128)(2,1)} %collective-permute-done.7, bf16[1024,1024]{1,0:T(8,128)(2,1)S(1)} %copy-done.25, bf16[1024,2560]{1,0:T(8,128)(2,1)S(1)} %bitcast.79), kind=kOutput, calls=%fused_computation.2 | convolution fusion | flops 5376573440 | bytes 17825792 | tf_op jit(solution)/shard_map/dot_general | solution.py:35
  465.4 41.7 %collective-permute-done.8 = bf16[2,2,128,2048]{3,2,1,0:T(8,128)(2,1)S(1)} collective-permute-done((bf16[2,2,128,2048]{3,2,1,0:T(8,128)(2,1)S(1)}, bf16[2,2,128,2048]{3,2,1,0:T(8,128)(2,1)S(1)}, u32[]{:S(2)}, u32[]{:S(2)}) %collective-permute-start.8) | collective-permute-done | bytes 2097184 | tf_op jit(solution)/shard_map/ppermute | solution.py:314
  509.0 10.0 %shard_map.282 = bf16[512,2048]{1,0:T(8,128)(2,1)} custom-call(s32[1]{0:T(128)} %bitcast.turn_ref, bf16[1024,2048]{1,0:T(8,128)(2,1)} %get-tuple-element.111.refs_0_, bf16[1024,512]{1,0:T(8,128)(2,1)} %copy-done.35, bf16[2048,4608]{1,0:T(8,128)(2,1)} %all-gather.3.cloned.1.call-done.refs_1_.refs_2_.refs_3_, ...), custom_call_target="tpu_custom_call" | custom-call | tf_op jit(solution)/shard_map/pallas_call | solution.py:548
  520.4 7.6 %shard_map.283 = bf16[512,2048]{1,0:T(8,128)(2,1)} custom-call(s32[1]{0:T(128)} %bitcast.turn_ref, bf16[1024,4608]{1,0:T(8,128)(2,1)} %shard_map.267.act_ref.refs_0_, bf16[2048,4608]{1,0:T(8,128)(2,1)} %all-gather.5.cloned.1.call-done.gate_ref.up_ref.down_ref.refs_1_), custom_call_target="tpu_custom_call" | custom-call | tf_op jit(solution)/shard_map/pallas_call | solution.py:548
  528.0 6.6 %collective-permute-done.9 = bf16[2,2,128,1280]{3,2,1,0:T(8,128)(2,1)} collective-permute-done((bf16[2,2,128,1280]{3,2,1,0:T(8,128)(2,1)S(1)}, bf16[2,2,128,1280]{3,2,1,0:T(8,128)(2,1)}, u32[]{:S(2)}, u32[]{:S(2)}) %collective-permute-start.9) | collective-permute-done | bytes 1310752 | tf_op jit(solution)/shard_map/ppermute | solution.py:314
  538.9 6.5 %collective-permute-done.11 = bf16[2,128,2048]{2,1,0:T(8,128)(2,1)} collective-permute-done((bf16[2,128,2048]{2,1,0:T(8,128)(2,1)}, bf16[2,128,2048]{2,1,0:T(8,128)(2,1)}, u32[]{:S(2)}, u32[]{:S(2)}) %collective-permute-start.11) | collective-permute-done | bytes 1048608 | tf_op jit(solution)/shard_map/ppermute | solution.py:314
  547.1 4.5 add_convert_fusion.2
  551.5 5.6 collective-permute-done.13
  557.6 4.0 fusion.9
  563.4 3.2 collective-permute-done.20
  568.4 2.4 collective-permute-start.18
  571.4 2.4 collective-permute-start.22
  573.8 34.1 %collective-permute-done.22 = f32[1,4352]{1,0:T(1,128)S(1)} collective-permute-done((f32[1,4352]{1,0:T(1,128)S(1)}, f32[1,4352]{1,0:T(1,128)S(1)}, u32[]{:S(2)}, u32[]{:S(2)}) %collective-permute-start.22) | collective-permute-done | bytes 17440 | tf_op jit(solution)/shard_map/ppermute | solution.py:314
  609.4 4.9 fusion.6
  615.5 15.0 %collective-permute-done.17 = bf16[128,1280]{1,0:T(8,128)(2,1)S(1)} collective-permute-done((bf16[128,1280]{1,0:T(8,128)(2,1)S(1)}, bf16[128,1280]{1,0:T(8,128)(2,1)S(1)}, u32[]{:S(2)}, u32[]{:S(2)}) %collective-permute-start.17) | collective-permute-done | bytes 327712 | tf_op jit(solution)/shard_map/ppermute | solution.py:314
  (209 shorter events, 70.2 us)
Async XLA Ops:
  7.2 104.7 %all-gather.3.cloned.1.call-start = ((), (), s32[]{:S(2)}) async-start(), calls=%async_computation.1 | async-start | bytes 20054016 | tf_op jit(solution)/shard_map/all_gather | solution.py:646
  9.7 202.8 %all-gather.5.cloned.1.call-start = ((), (), s32[]{:S(2)}) async-start(), calls=%async_computation.2 | async-start | bytes 20054016 | tf_op jit(solution)/shard_map/all_gather | solution.py:650
  11.1 49.1 %copy-start.16 = (bf16[512,2048]{1,0:T(8,128)(2,1)S(1)}, bf16[512,2048]{1,0:T(8,128)(2,1)}, u32[]{:S(2)}) copy-start(bf16[512,2048]{1,0:T(8,128)(2,1)} %one_ref.3) | copy-start | bytes 6291460
  11.1 622.5 %reduce-scatter.2.cloned.1.call-start = ((), (), s32[]{:S(2)}) async-start(), calls=%async_computation.3 | async-start | bytes 20054016 | tf_op jit(solution)/shard_map/reduce_scatter | solution.py:696
  11.2 49.0 %collective-permute-start = (bf16[512,2048]{1,0:T(8,128)(2,1)}, bf16[512,2048]{1,0:T(8,128)(2,1)}, u32[]{:S(2)}, u32[]{:S(2)}) collective-permute-start(bf16[512,2048]{1,0:T(8,128)(2,1)} %one_ref.2), channel_id=1, source_target_pairs={{0,1},{1,0},{2,3},{3,2},{4,5},{5,4},{6,7},{7,6},{8,9},{9,8},{10,11... | collective-permute-start | bytes 6291464 | tf_op jit(solution)/shard_map/ppermute | solution.py:318
  16.5 136.5 %copy-start.6 = (f32[1024,128]{1,0:T(8,128)}, f32[1024,128]{1,0:T(8,128)S(1)}, u32[]{:S(2)}) copy-start(f32[1024,128]{1,0:T(8,128)S(1)} %get-tuple-element.169.qcos_ref.kcos_ref) | copy-start | bytes 1572868
  16.5 136.5 %copy-start.7 = (f32[1024,128]{1,0:T(8,128)}, f32[1024,128]{1,0:T(8,128)S(1)}, u32[]{:S(2)}) copy-start(f32[1024,128]{1,0:T(8,128)S(1)} %get-tuple-element.170.qsin_ref.ksin_ref) | copy-start | bytes 1572868
  16.6 54.2 %copy-start.22 = (s32[16]{0:T(128)}, s32[16]{0:T(128)S(1)}, u32[]{:S(2)}) copy-start(s32[16]{0:T(128)S(1)} %broadcast_xor_fusion.order_ref) | copy-start | bytes 196
  60.1 115.7 %collective-permute-start.1 = (bf16[512,2048]{1,0:T(8,128)(2,1)S(1)}, bf16[512,2048]{1,0:T(8,128)(2,1)}, u32[]{:S(2)}, u32[]{:S(2)}) collective-permute-start(bf16[512,2048]{1,0:T(8,128)(2,1)S(1)} %copy-done.16), channel_id=1, source_target_pairs={{0,1},{1,0},{2,3},{3,2},{4,5},{5,4},{6,7},{7,6},{8,9},{9,8},{10,11... | collective-permute-start | bytes 6291464 | tf_op jit(solution)/shard_map/ppermute | solution.py:318
  75.2 52.7 %copy-start.20 = (f32[1,128]{1,0:T(1,128)S(1)}, f32[1,128]{1,0:T(1,128)}, u32[]{:S(2)}) copy-start(f32[1,128]{1,0:T(1,128)} %qg_ref.7) | copy-start | bytes 1540
  75.2 52.7 %copy-start.21 = (f32[1,128]{1,0:T(1,128)S(1)}, f32[1,128]{1,0:T(1,128)}, u32[]{:S(2)}) copy-start(f32[1,128]{1,0:T(1,128)} %kg_ref.7) | copy-start | bytes 1540
  151.2 48.8 %collective-permute-start.2 = (bf16[512,2048]{1,0:T(8,128)(2,1)}, bf16[512,2048]{1,0:T(8,128)(2,1)}, u32[]{:S(2)}, u32[]{:S(2)}) collective-permute-start(bf16[512,2048]{1,0:T(8,128)(2,1)} %shard_map.259.part_ref), channel_id=1, source_target_pairs={{0,1},{1,0},{2,3},{3,2},{4,5},{5,4},{6,7},{7,6},{8,9},{9,8},{10,11... | collective-permute-start | bytes 6291464 | tf_op jit(solution)/shard_map/ppermute | solution.py:318
  164.5 9.3 %copy-start.46 = (s32[1,1024,2]{1,2,0:T(2,128)S(1)}, s32[1,1024,2]{1,2,0:T(2,128)}, u32[]{:S(2)}) copy-start(s32[1,1024,2]{1,2,0:T(2,128)} %param.18) | copy-start | bytes 24580
  164.5 10.3 %copy-start.47 = (f32[1,1024,2]{1,2,0:T(2,128)S(1)}, f32[1,1024,2]{1,2,0:T(2,128)}, u32[]{:S(2)}) copy-start(f32[1,1024,2]{1,2,0:T(2,128)} %param.19) | copy-start | bytes 24580
  173.4 71.0 %collective-permute-start.3 = (bf16[512,2048]{1,0:T(8,128)(2,1)}, bf16[512,2048]{1,0:T(8,128)(2,1)}, u32[]{:S(2)}, u32[]{:S(2)}) collective-permute-start(bf16[512,2048]{1,0:T(8,128)(2,1)} %shard_map.261.part_ref), channel_id=1, source_target_pairs={{0,1},{1,0},{2,3},{3,2},{4,5},{5,4},{6,7},{7,6},{8,9},{9,8},{10,11... | collective-permute-start | bytes 6291464 | tf_op jit(solution)/shard_map/ppermute | solution.py:318
  175.8 24.2 %copy-start.4 = (bf16[1024,2048]{1,0:T(8,128)(2,1)S(1)}, bf16[1024,2048]{1,0:T(8,128)(2,1)}, u32[]{:S(2)}) copy-start(bf16[1024,2048]{1,0:T(8,128)(2,1)} %copy-done.3) | copy-start | bytes 12582916
  175.8 24.2 %copy-start.14 = (bf16[512,2048]{1,0:T(8,128)(2,1)S(1)}, bf16[512,2048]{1,0:T(8,128)(2,1)}, u32[]{:S(2)}) copy-start(bf16[512,2048]{1,0:T(8,128)(2,1)} %shard_map.259.part_ref) | copy-start | bytes 6291460
  175.8 24.2 %copy-start.17 = (f32[1,2048]{1,0:T(1,128)S(1)}, f32[1,2048]{1,0:T(1,128)}, u32[]{:S(2)}) copy-start(f32[1,2048]{1,0:T(1,128)} %gain_ref.7) | copy-start | bytes 24580
  230.1 14.3 %copy-start.5 = (bf16[1024,2048]{1,0:T(8,128)(2,1)S(1)}, bf16[1024,2048]{1,0:T(8,128)(2,1)}, u32[]{:S(2)}) copy-start(bf16[1024,2048]{1,0:T(8,128)(2,1)} %copy-done.3) | copy-start | bytes 12582916
  230.1 14.3 %copy-start.15 = (bf16[512,2048]{1,0:T(8,128)(2,1)S(1)}, bf16[512,2048]{1,0:T(8,128)(2,1)}, u32[]{:S(2)}) copy-start(bf16[512,2048]{1,0:T(8,128)(2,1)} %shard_map.261.part_ref) | copy-start | bytes 6291460
  241.6 64.7 %collective-permute-start.4 = (bf16[512,2048]{1,0:T(8,128)(2,1)}, bf16[512,2048]{1,0:T(8,128)(2,1)}, u32[]{:S(2)}, u32[]{:S(2)}) collective-permute-start(bf16[512,2048]{1,0:T(8,128)(2,1)} %shard_map.265.part_ref), channel_id=1, source_target_pairs={{0,1},{1,0},{2,3},{3,2},{4,5},{5,4},{6,7},{7,6},{8,9},{9,8},{10,11... | collective-permute-start | bytes 6291464 | tf_op jit(solution)/shard_map/ppermute | solution.py:318
  306.3 51.3 %collective-permute-start.5 = (bf16[512,2048]{1,0:T(8,128)(2,1)}, bf16[512,2048]{1,0:T(8,128)(2,1)}, u32[]{:S(2)}, u32[]{:S(2)}) collective-permute-start(bf16[512,2048]{1,0:T(8,128)(2,1)} %shard_map.270.part_ref), channel_id=1, source_target_pairs={{0,1},{1,0},{2,3},{3,2},{4,5},{5,4},{6,7},{7,6},{8,9},{9,8},{10,11... | collective-permute-start | bytes 6291464 | tf_op jit(solution)/shard_map/ppermute | solution.py:318
  329.8 27.8 %copy-start.2 = (bf16[1024,2048]{1,0:T(8,128)(2,1)S(1)}, bf16[1024,2048]{1,0:T(8,128)(2,1)}, u32[]{:S(2)}) copy-start(bf16[1024,2048]{1,0:T(8,128)(2,1)} %copy-done) | copy-start | bytes 12582916
  386.4 57.0 %collective-permute-start.6 = (bf16[1024,2048]{1,0:T(8,128)(2,1)}, bf16[1024,2048]{1,0:T(8,128)(2,1)}, u32[]{:S(2)}, u32[]{:S(2)}) collective-permute-start(bf16[1024,2048]{1,0:T(8,128)(2,1)} %shard_map.279), channel_id=1, source_target_pairs={{0,2},{2,0},{4,6},{6,4},{8,10},{10,8},{12,14},{14,12},{16,18},{18,... | collective-permute-start | bytes 12582920 | tf_op jit(solution)/shard_map/ppermute | solution.py:314
  410.5 10.3 %copy-start.35 = (bf16[1024,512]{1,0:T(8,128)(2,1)}, bf16[1024,512]{1,0:T(8,128)(2,1)S(1)}, u32[]{:S(2)}) copy-start(bf16[1024,512]{1,0:T(8,128)(2,1)S(1)} %get-tuple-element.156.refs_1_) | copy-start | bytes 3145732
  420.8 34.1 %collective-permute-start.7 = (bf16[1024,2560]{1,0:T(8,128)(2,1)}, bf16[1024,2560]{1,0:T(8,128)(2,1)}, u32[]{:S(2)}, u32[]{:S(2)}) collective-permute-start(bf16[1024,2560]{1,0:T(8,128)(2,1)} %shard_map.281), channel_id=1, source_target_pairs={{0,2},{2,0},{4,6},{6,4},{8,10},{10,8},{12,14},{14,12},{16,18},{18,... | collective-permute-start | bytes 15728648 | tf_op jit(solution)/shard_map/ppermute | solution.py:314
  433.4 124.1 %collective-permute-start.15 = (bf16[512,2048]{1,0:T(8,128)(2,1)}, bf16[512,2048]{1,0:T(8,128)(2,1)}, u32[]{:S(2)}, u32[]{:S(2)}) collective-permute-start(bf16[512,2048]{1,0:T(8,128)(2,1)} %shard_map.280), channel_id=1, source_target_pairs={{0,1},{1,0},{2,3},{3,2},{4,5},{5,4},{6,7},{7,6},{8,9},{9,8},{10,11... | collective-permute-start | bytes 6291464 | tf_op jit(solution)/shard_map/ppermute | solution.py:318
  443.0 11.8 %slice-start = ((s8[5242880]{0:T(1024)(128)(4,1)}), s8[1048576]{0:T(1024)(128)(4,1)S(1)}, s32[]{:S(2)}) async-start(s8[5242880]{0:T(1024)(128)(4,1)} %bitcast.78), calls=%async_computation.4 | async-start | bytes 2097152
  443.0 104.0 %collective-permute-start.12 = (bf16[512,2048]{1,0:T(8,128)(2,1)}, bf16[512,2048]{1,0:T(8,128)(2,1)}, u32[]{:S(2)}, u32[]{:S(2)}) collective-permute-start(bf16[512,2048]{1,0:T(8,128)(2,1)} %shard_map.284), channel_id=1, source_target_pairs={{0,1},{1,0},{2,3},{3,2},{4,5},{5,4},{6,7},{7,6},{8,9},{9,8},{10,11... | collective-permute-start | bytes 6291464 | tf_op jit(solution)/shard_map/ppermute | solution.py:318
  443.3 11.5 %slice-start.1 = ((s8[5242880]{0:T(1024)(128)(4,1)}), s8[4194304]{0:T(1024)(128)(4,1)S(1)}, s32[]{:S(2)}) async-start(s8[5242880]{0:T(1024)(128)(4,1)} %bitcast.78), calls=%async_computation.5 | async-start | bytes 8388608
  453.5 53.6 %collective-permute-start.8 = (bf16[2,2,128,2048]{3,2,1,0:T(8,128)(2,1)S(1)}, bf16[2,2,128,2048]{3,2,1,0:T(8,128)(2,1)S(1)}, u32[]{:S(2)}, u32[]{:S(2)}) collective-permute-start(bf16[2,2,128,2048]{3,2,1,0:T(8,128)(2,1)S(1)} %bitcast.80), channel_id=1, source_target_pairs={{0,4},{2,6},{4,0},{6,2},{8,12},{10,14},{12,8},{14,10},{16,20},{18,... | collective-permute-start | bytes 6291464 | tf_op jit(solution)/shard_map/ppermute | solution.py:314
  462.9 71.7 %collective-permute-start.9 = (bf16[2,2,128,1280]{3,2,1,0:T(8,128)(2,1)S(1)}, bf16[2,2,128,1280]{3,2,1,0:T(8,128)(2,1)}, u32[]{:S(2)}, u32[]{:S(2)}) collective-permute-start(bf16[2,2,128,1280]{3,2,1,0:T(8,128)(2,1)S(1)} %get-tuple-element.132), channel_id=1, source_target_pairs={{0,4},{2,6},{4,0},{6,2},{8,12},{10,14},{12,8},{14,10},{16,20},{18,... | collective-permute-start | bytes 3932168 | tf_op jit(solution)/shard_map/ppermute | solution.py:314
  464.1 73.8 %collective-permute-start.10 = (bf16[2,2,128,1280]{3,2,1,0:T(8,128)(2,1)S(1)}, bf16[2,2,128,1280]{3,2,1,0:T(8,128)(2,1)S(1)}, u32[]{:S(2)}, u32[]{:S(2)}) collective-permute-start(bf16[2,2,128,1280]{3,2,1,0:T(8,128)(2,1)S(1)} %get-tuple-element.134), channel_id=1, source_target_pairs={{0,8},{2,10},{4,12},{6,14},{8,0},{10,2},{12,4},{14,6},{16,24},{18,... | collective-permute-start | bytes 3932168 | tf_op jit(solution)/shard_map/ppermute | solution.py:314
  519.0 26.4 %collective-permute-start.11 = (bf16[2,128,2048]{2,1,0:T(8,128)(2,1)}, bf16[2,128,2048]{2,1,0:T(8,128)(2,1)}, u32[]{:S(2)}, u32[]{:S(2)}) collective-permute-start(bf16[2,128,2048]{2,1,0:T(8,128)(2,1)} %get-tuple-element.140), channel_id=1, source_target_pairs={{0,8},{2,10},{4,12},{6,14},{8,0},{10,2},{12,4},{14,6},{16,24},{18,... | collective-permute-start | bytes 3145736 | tf_op jit(solution)/shard_map/ppermute | solution.py:314
  536.2 10.8 %copy-start.34 = (bf16[512,2048]{1,0:T(8,128)(2,1)S(1)}, bf16[512,2048]{1,0:T(8,128)(2,1)}, u32[]{:S(2)}) copy-start(bf16[512,2048]{1,0:T(8,128)(2,1)} %shard_map.283) | copy-start | bytes 6291460
  536.3 20.8 %collective-permute-start.13 = (bf16[2,128,1280]{2,1,0:T(8,128)(2,1)S(1)}, bf16[2,128,1280]{2,1,0:T(8,128)(2,1)S(1)}, u32[]{:S(2)}, u32[]{:S(2)}) collective-permute-start(bf16[2,128,1280]{2,1,0:T(8,128)(2,1)S(1)} %get-tuple-element.142), channel_id=1, source_target_pairs={{0,8},{2,10},{4,12},{6,14},{8,0},{10,2},{12,4},{14,6},{16,24},{18,... | collective-permute-start | bytes 1966088 | tf_op jit(solution)/shard_map/ppermute | solution.py:314
  537.9 9.2 %copy-start.33 = (f32[512,2048]{1,0:T(8,128)S(1)}, f32[512,2048]{1,0:T(8,128)}, u32[]{:S(2)}) copy-start(f32[512,2048]{1,0:T(8,128)} %get-tuple-element.83.mid_ref) | copy-start | bytes 12582916
  538.3 19.0 %collective-permute-start.14 = (bf16[2,128,1280]{2,1,0:T(8,128)(2,1)S(1)}, bf16[2,128,1280]{2,1,0:T(8,128)(2,1)S(1)}, u32[]{:S(2)}, u32[]{:S(2)}) collective-permute-start(bf16[2,128,1280]{2,1,0:T(8,128)(2,1)S(1)} %get-tuple-element.144), channel_id=1, source_target_pairs={{0,4},{2,6},{4,0},{6,2},{8,12},{10,14},{12,8},{14,10},{16,20},{18,... | collective-permute-start | bytes 1966088 | tf_op jit(solution)/shard_map/ppermute | solution.py:314
  557.5 51.9 %copy-start.37 = (f32[512,2048]{1,0:T(8,128)S(1)}, f32[512,2048]{1,0:T(8,128)}, u32[]{:S(2)}) copy-start(f32[512,2048]{1,0:T(8,128)} %get-tuple-element.117) | copy-start | bytes 12582916
  561.5 47.9 %copy-start.36 = (f32[512,2048]{1,0:T(8,128)S(1)}, f32[512,2048]{1,0:T(8,128)}, u32[]{:S(2)}) copy-start(f32[512,2048]{1,0:T(8,128)} %get-tuple-element.118) | copy-start | bytes 12582916
  561.6 1.3 collective-permute-start.19
  562.9 3.8 collective-permute-start.20
  566.7 4.7 collective-permute-start.21
  568.4 62.2 %collective-permute-start.18 = (bf16[128,1280]{1,0:T(8,128)(2,1)S(1)}, bf16[128,1280]{1,0:T(8,128)(2,1)S(1)}, u32[]{:S(2)}, u32[]{:S(2)}) collective-permute-start(bf16[128,1280]{1,0:T(8,128)(2,1)S(1)} %get-tuple-element.153), channel_id=1, source_target_pairs={{0,16},{2,18},{4,20},{6,22},{8,24},{10,26},{12,28},{14,30},{16,0},... | collective-permute-start | bytes 983048 | tf_op jit(solution)/shard_map/ppermute | solution.py:314
  570.7 61.7 %collective-permute-start.16 = (bf16[128,2048]{1,0:T(8,128)(2,1)S(1)}, bf16[128,2048]{1,0:T(8,128)(2,1)S(1)}, u32[]{:S(2)}, u32[]{:S(2)}) collective-permute-start(bf16[128,2048]{1,0:T(8,128)(2,1)S(1)} %get-tuple-element.149), channel_id=1, source_target_pairs={{0,16},{2,18},{4,20},{6,22},{8,24},{10,26},{12,28},{14,30},{16,0},... | collective-permute-start | bytes 1572872 | tf_op jit(solution)/shard_map/ppermute | solution.py:314
  571.4 36.4 %collective-permute-start.22 = (f32[1,4352]{1,0:T(1,128)S(1)}, f32[1,4352]{1,0:T(1,128)S(1)}, u32[]{:S(2)}, u32[]{:S(2)}) collective-permute-start(f32[1,4352]{1,0:T(1,128)S(1)} %add.112), channel_id=1, source_target_pairs={{0,16},{2,18},{4,20},{6,22},{8,24},{10,26},{12,28},{14,30},{16,0},... | collective-permute-start | bytes 52232 | tf_op jit(solution)/shard_map/ppermute | solution.py:314
  607.9 6.5 %collective-permute-start.23 = (f32[1,4352]{1,0:T(1,128)S(1)}, f32[1,4352]{1,0:T(1,128)S(1)}, u32[]{:S(2)}, u32[]{:S(2)}) collective-permute-start(f32[1,4352]{1,0:T(1,128)S(1)} %add.113), channel_id=1, source_target_pairs={{0,1},{1,0},{2,3},{3,2},{4,5},{5,4},{6,7},{7,6},{8,9},{9,8},{10,11... | collective-permute-start | bytes 52232 | tf_op jit(solution)/shard_map/ppermute | solution.py:318
  614.3 16.2 %collective-permute-start.17 = (bf16[128,1280]{1,0:T(8,128)(2,1)S(1)}, bf16[128,1280]{1,0:T(8,128)(2,1)S(1)}, u32[]{:S(2)}, u32[]{:S(2)}) collective-permute-start(bf16[128,1280]{1,0:T(8,128)(2,1)S(1)} %get-tuple-element.155), channel_id=1, source_target_pairs={{0,16},{2,18},{4,20},{6,22},{8,24},{10,26},{12,28},{14,30},{16,0},... | collective-permute-start | bytes 983048 | tf_op jit(solution)/shard_map/ppermute | solution.py:314
  (32 other events, 106.9 us)
Sparse Core Ops, SparseCore 0:
  10.2 101.6 all-gather.2
  113.5 98.9 all-gather.4
  294.4 211.4 reduce-scatter.1

commit v4 on v3

--- a/solution.py
+++ b/solution.py
@@ -762,20 +762,26 @@
     grad_theirs = normed_back(lambda t: 1 - t, qkv_sum.sent)
     rest_sum, last = qkv_sum.keep_two(crossed, grad_qkv.shape[1] // 2, grad_theirs)
     grad_got = swap_pair(grad_theirs)
-    last = out_sum.step(last)
     grad_mine = normed_back(lambda t: t, last)
     out_mine = expert_out(lambda t: t, grad_mine)
-    last = qkv_sum.step(out_mine)
+    last = out_sum.step(out_mine)
+    last = qkv_sum.step(last)
     last = rest_sum.step(last)
     last = out_sum.step(last)
     output = (select(mid[0], mid[1]) + (after(out_mine, last).astype(F32) + out_got.astype(F32))).astype(BF)
     last = qkv_sum.step(output)
     last = rest_sum.step(last)
     grad_normed = after(grad_mine, last).astype(F32) + grad_got.astype(F32)
-    grad_one, attn_part = norm_back(tokens.astype(F32), attn_gain, grad_normed)
-    tokens_grad = select(grad_mid[0], grad_mid[1]) + grad_one
+    tokens_grad = select(grad_mid[0], grad_mid[1]) + norm_back(tokens.astype(F32), attn_gain, grad_normed)[0]
+
+    def gain_part(own, grad):
+        values = lax.dynamic_slice_in_dim(tokens_all, own * chunk, chunk, axis=0).astype(F32)
+        return jnp.sum(grad.astype(F32) * values * mean_square(values), axis=0, keepdims=True)
+
+    attn_part = gain_part(turn, after(grad_mine, last)) + gain_part(1 - turn, after(grad_theirs, last))
     ffn_part = (ffn_parts[0] + ffn_parts[1]) * 0.5
     small = jnp.concatenate([attn_part, ffn_part, query_part, key_part], axis=1)
+    small = tie(small, out_sum.got, rest_sum.got, qkv_sum.got)
     small = sum_all(small)
     out_grad = out_sum.finish(tokens_grad)
     rest_grad = rest_sum.finish(out_grad)

time: 650 us -> 644 us (level)
  waiting for transfers between devices: 220 us -> 205 us
    ppermute x15, waiting for transfers between devices: 114 us -> 99.3 us  [swap(): return lax.ppermute(value, 'dp', [(i, i ^ 1 << bit) for i in range(count)])]
    unnamed x113 -> x123, local copies, waits for them, and re-layouts: 24.2 us -> 28.1 us
  transfers between devices with their start and end apart: 27 -> 27, of which waited for: 13 -> 16; matrix products, arithmetic and copies ran while one was open for 11% -> 12% of each run, Pallas kernels for 44% -> 45%
where the time goes in v4:
time: 644 us; the launch traced here: 639 us
  Pallas kernels  287 us (45%)
  waiting for transfers between devices  205 us (32%)
  local copies, waits for them, and re-layouts  37.8 us (6%)
  other arithmetic  35.1 us (5%)
  matrix products  31.6 us (5%)
  starting transfers between devices  27.7 us (4%)
  between operations  14.7 us (2%)
    pallas_call x11, Pallas kernels, product(): pl.pallas_call(functools.partial(product_kernel, len(lefts), form), grid_...  112 us
    ppermute x15, waiting for transfers between devices, swap(): return lax.ppermute(value, 'dp', [(i, i ^ 1 << bit) for i in range(count)])  99.3 us
    ppermute x9, waiting for transfers between devices, swap_pair(): return lax.ppermute(value, 'tensor', [(0, 1), (1, 0)])  63.2 us
    pallas_call x2, Pallas kernels, attention_bwd(): pl.pallas_call(functools.partial(attn_bwd_kernel, min(256, chunk), keys,...  48.9 us
    all_gather x1, waiting for transfers between devices, body(): lax.all_gather(jnp.concatenate([out_weight[0], query_weight[0], key_weigh...  35.4 us
    pallas_call x2, Pallas kernels, expert_part(): pl.pallas_call(functools.partial(expert_kernel, unit, cols), grid=(steps,...  35.3 us
    dot_general x4, matrix products, dot_tn(): lax.dot_general(left, right, (((0,), (0,)), ((), ())), preferred_element_...  31.6 us
    unnamed x123, local copies, waits for them, and re-layouts  28.1 us
  transfers between devices with their start and end apart: 27, of which 16 were waited for; matrix products, arithmetic and copies ran while one was open for 12% of the time, Pallas kernels for 45%

profile of v4, /device:TPU:0, one launch (start us, length us, event | category | flops | bytes accessed | tf_op | source)
XLA Modules:
  0.0 639.1 jit_solution(14108023076362248831)
XLA Ops:
  7.2 2.4 pad_maximum_fusion
  12.1 3.0 collective-permute-start
  17.5 43.6 %collective-permute-done.two_ref = bf16[512,2048]{1,0:T(8,128)(2,1)} collective-permute-done((bf16[512,2048]{1,0:T(8,128)(2,1)}, bf16[512,2048]{1,0:T(8,128)(2,1)}, u32[]{:S(2)}, u32[]{:S(2)}) %collective-permute-start) | collective-permute-done | bytes 2097184 | tf_op jit(solution)/shard_map/ppermute | solution.py:318
  62.9 5.3 shard_map.255.base_ref
  76.5 35.4 %all-gather.3.cloned.1.call-done.refs_1_.refs_2_.refs_3_ = bf16[2048,4608]{1,0:T(8,128)(2,1)} async-done(((bf16[128,4608]{1,0:T(8,128)(2,1)}), bf16[2048,4608]{1,0:T(8,128)(2,1)}) %all-gather.3.cloned.1.call-update) | async-done | bytes 18874384 | tf_op jit(solution)/shard_map/all_gather | solution.py:646
  111.9 16.0 %shard_map.257.q_ref.k_ref.v_ref = f32[1024,2560]{1,0:T(8,128)} custom-call(s32[1]{0:T(128)} %bitcast.turn_ref, bf16[1024,2048]{1,0:T(8,128)(2,1)} %copy-done.31, bf16[2048,4608]{1,0:T(8,128)(2,1)} %all-gather.3.cloned.1.call-done.refs_1_.refs_2_.refs_3_), custom_call_target="tpu_custom_call" | custom-call | tf_op jit(solution)/shard_map/pallas_call | solution.py:548
  127.9 13.7 %shard_map.258 = (bf16[1024,2048]{1,0:T(8,128)(2,1)}, f32[16,1,512]{2,1,0:T(1,128)S(1)}) custom-call(f32[1024,2560]{1,0:T(8,128)} %shard_map.257.q_ref.k_ref.v_ref, f32[1024,2560]{1,0:T(8,128)} %shard_map.257.q_ref.k_ref.v_ref, f32[1024,2560]{1,0:T(8,128)} %shard_map.257.q_ref.k_ref.v_ref, f32[1,128]{1,0:T(1,128)S(1)} %copy-done.21, ...), custom_call_target="tpu_custom_call" | custom-call | tf_op jit(solution)/shard_map/pallas_call | solution.py:129
  142.3 8.9 %shard_map.259.part_ref = bf16[512,2048]{1,0:T(8,128)(2,1)} custom-call(s32[1]{0:T(128)} %bitcast.turn_ref, bf16[1024,2048]{1,0:T(8,128)(2,1)} %get-tuple-element.76.refs_0_.rest_0_, bf16[2048,4608]{1,0:T(8,128)(2,1)} %all-gather.3.cloned.1.call-done.refs_1_.refs_2_.refs_3_), custom_call_target="tpu_custom_call" | custom-call | tf_op jit(solution)/shard_map/pallas_call | solution.py:548
  153.0 10.9 %shard_map.260 = (bf16[1024,2048]{1,0:T(8,128)(2,1)}, f32[16,1,512]{2,1,0:T(1,128)S(1)}) custom-call(f32[1024,2560]{1,0:T(8,128)} %shard_map.257.q_ref.k_ref.v_ref, f32[1024,2560]{1,0:T(8,128)} %shard_map.257.q_ref.k_ref.v_ref, f32[1024,2560]{1,0:T(8,128)} %shard_map.257.q_ref.k_ref.v_ref, f32[1,128]{1,0:T(1,128)S(1)} %copy-done.21, ...), custom_call_target="tpu_custom_call", output_to_operand_aliasing={{0}: (9, {})} | custom-call | tf_op jit(solution)/shard_map/pallas_call | solution.py:129
  164.5 8.9 %shard_map.261.part_ref = bf16[512,2048]{1,0:T(8,128)(2,1)} custom-call(s32[1]{0:T(128)} %bitcast.turn_ref, bf16[1024,2048]{1,0:T(8,128)(2,1)} %get-tuple-element.90.refs_0_.ctx_ref, bf16[2048,4608]{1,0:T(8,128)(2,1)} %all-gather.3.cloned.1.call-done.refs_1_.refs_2_.refs_3_), custom_call_target="tpu_custom_call" | custom-call | tf_op jit(solution)/shard_map/pallas_call | solution.py:548
  175.8 4.9 shard_map.262.cot_ref.base_ref
  182.8 17.1 %collective-permute-done.2.got_ref = bf16[512,2048]{1,0:T(8,128)(2,1)} collective-permute-done((bf16[512,2048]{1,0:T(8,128)(2,1)}, bf16[512,2048]{1,0:T(8,128)(2,1)}, u32[]{:S(2)}, u32[]{:S(2)}) %collective-permute-start.2) | collective-permute-done | bytes 2097184 | tf_op jit(solution)/shard_map/ppermute | solution.py:318
  200.0 5.2 shard_map.263
  205.1 7.3 %all-gather.5.cloned.1.call-done.gate_ref.up_ref.down_ref.refs_1_ = bf16[2048,4608]{1,0:T(8,128)(2,1)} async-done(((bf16[128,4608]{1,0:T(8,128)(2,1)}), bf16[2048,4608]{1,0:T(8,128)(2,1)}) %all-gather.5.cloned.1.call-update) | async-done | bytes 18874384 | tf_op jit(solution)/shard_map/all_gather | solution.py:650
  212.5 17.6 %shard_map.264.refs_0_.rest_0_ = bf16[1024,4608]{1,0:T(8,128)(2,1)} custom-call(bf16[1024,2048]{1,0:T(8,128)(2,1)} %get-tuple-element.83.x_ref.rest_0_, bf16[1024,2048]{1,0:T(8,128)(2,1)} %copy-done.4, bf16[2048,4608]{1,0:T(8,128)(2,1)} %all-gather.5.cloned.1.call-done.gate_ref.up_ref.down_ref.refs_1_, ...), custom_call_target="tpu_custom_call" | custom-call | tf_op jit(solution)/shard_map/pallas_call | solution.py:500
  230.1 11.5 %shard_map.265.part_ref = bf16[512,2048]{1,0:T(8,128)(2,1)} custom-call(s32[1]{0:T(128)} %bitcast.turn_ref, bf16[1024,4608]{1,0:T(8,128)(2,1)} %shard_map.264.refs_0_.rest_0_, bf16[2048,4608]{1,0:T(8,128)(2,1)} %all-gather.5.cloned.1.call-done.gate_ref.up_ref.down_ref.refs_1_), custom_call_target="tpu_custom_call" | custom-call | tf_op jit(solution)/shard_map/pallas_call | solution.py:548
  244.4 5.2 shard_map.266
  249.6 17.7 %shard_map.267.act_ref.refs_0_ = bf16[1024,4608]{1,0:T(8,128)(2,1)} custom-call(bf16[1024,2048]{1,0:T(8,128)(2,1)} %get-tuple-element.86.x_ref.normed_ref, bf16[1024,2048]{1,0:T(8,128)(2,1)} %copy-done.4, bf16[2048,4608]{1,0:T(8,128)(2,1)} %all-gather.5.cloned.1.call-done.gate_ref.up_ref.down_ref.refs_1_, ...), custom_call_target="tpu_custom_call", output_to_operand_aliasing={{}: (7, {})} | custom-call | tf_op jit(solution)/shard_map/pallas_call | solution.py:500
  267.3 26.9 %shard_map.268 = bf16[2048,4608]{1,0:T(8,128)(2,1)} custom-call(bf16[1024,2048]{1,0:T(8,128)(2,1)} %get-tuple-element.86.x_ref.normed_ref, bf16[1024,2048]{1,0:T(8,128)(2,1)} %copy-done.4, bf16[1024,4608]{1,0:T(8,128)(2,1)} %shard_map.267.act_ref.refs_0_), custom_call_target="tpu_custom_call" | custom-call | tf_op jit(solution)/shard_map/pallas_call | solution.py:530
  294.2 12.2 %shard_map.269.refs_0_ = bf16[512,2048]{1,0:T(8,128)(2,1)} custom-call(s32[1]{0:T(128)} %bitcast.turn_ref, bf16[1024,4608]{1,0:T(8,128)(2,1)} %shard_map.267.act_ref.refs_0_, bf16[2048,4608]{1,0:T(8,128)(2,1)} %all-gather.5.cloned.1.call-done.gate_ref.up_ref.down_ref.refs_1_), custom_call_target="tpu_custom_call" | custom-call | tf_op jit(solution)/shard_map/pallas_call | solution.py:548
  308.3 3.0 copy-done.5
  311.4 8.1 %shard_map.271 = (f32[512,2048]{1,0:T(8,128)}, bf16[512,2048]{1,0:T(8,128)(2,1)S(1)}, f32[1,2048]{1,0:T(1,128)S(1)}) custom-call(bf16[1024,2048]{1,0:T(8,128)(2,1)S(1)} %copy-done.5, bf16[512,2048]{1,0:T(8,128)(2,1)S(1)} %copy-done.14, bf16[512,2048]{1,0:T(8,128)(2,1)} %collective-permute-done.4.refs_1_.got_ref, f32[512,2048]{1,0:T(8,128)} %get-tuple-element.85.mid_ref, ...), custom_call_target="tpu_custom_call" | custom-call | tf_op jit(solution)/shard_map/pallas_call | solution.py:447
  320.8 9.2 %shard_map.272.grad_ref = bf16[512,2048]{1,0:T(8,128)(2,1)} custom-call(s32[1]{0:T(128)} %bitcast.turn_ref, bf16[512,2048]{1,0:T(8,128)(2,1)} %copy-done.10, bf16[2048,4608]{1,0:T(8,128)(2,1)} %all-gather.3.cloned.1.call-done.refs_1_.refs_2_.refs_3_), custom_call_target="tpu_custom_call" | custom-call | tf_op jit(solution)/shard_map/pallas_call | solution.py:548
  330.0 27.8 %shard_map.273 = (bf16[1024,2048]{1,0:T(8,128)(2,1)}, f32[1024,256]{1,0:T(8,128)}, f32[1024,256]{1,0:T(8,128)}, f32[1,128]{1,0:T(1,128)}, f32[1,128]{1,0:T(1,128)}) custom-call(f32[1024,2560]{1,0:T(8,128)} %shard_map.257.q_ref.k_ref.v_ref, f32[1024,2560]{1,0:T(8,128)} %shard_map.257.q_ref.k_ref.v_ref, f32[1024,2560]{1,0:T(8,128)} %shard_map.257.q_ref.k_ref.v_ref, ...), custom_call_target="tpu_custom_call" | custom-call | tf_op jit(solution)/shard_map/pallas_call | solution.py:268
  359.4 7.2 %shard_map.274 = (f32[512,2048]{1,0:T(8,128)}, bf16[512,2048]{1,0:T(8,128)(2,1)S(1)}, f32[1,2048]{1,0:T(1,128)S(1)}) custom-call(bf16[1024,2048]{1,0:T(8,128)(2,1)S(1)} %copy-done.6, bf16[512,2048]{1,0:T(8,128)(2,1)S(1)} %copy-done.9, bf16[512,2048]{1,0:T(8,128)(2,1)} %collective-permute-done.5.got_ref.refs_1_, f32[512,2048]{1,0:T(8,128)} %get-tuple-element.84.mid_ref, ...), custom_call_target="tpu_custom_call" | custom-call | tf_op jit(solution)/shard_map/pallas_call | solution.py:447
  367.9 9.2 %shard_map.275.grad_ref = bf16[512,2048]{1,0:T(8,128)(2,1)} custom-call(s32[1]{0:T(128)} %bitcast.turn_ref, bf16[512,2048]{1,0:T(8,128)(2,1)} %copy-done.12, bf16[2048,4608]{1,0:T(8,128)(2,1)} %all-gather.3.cloned.1.call-done.refs_1_.refs_2_.refs_3_), custom_call_target="tpu_custom_call" | custom-call | tf_op jit(solution)/shard_map/pallas_call | solution.py:548
  380.4 6.6 %convolution_convert_fusion.1.refs_0_ = bf16[1024,2048]{1,0:T(8,128)(2,1)} fusion(bf16[1024,1024]{1,0:T(8,128)(2,1)S(1)} %get-tuple-element.110, bf16[1024,2048]{1,0:T(8,128)(2,1)S(1)} %copy-done.30), kind=kOutput, calls=%fused_computation.30 | convolution fusion | flops 4297064448 | bytes 10485760 | tf_op jit(solution)/shard_map/dot_general | solution.py:35
  386.9 21.1 %shard_map.276 = (bf16[1024,2048]{1,0:T(8,128)(2,1)}, bf16[1024,256]{1,0:T(8,128)(2,1)}, bf16[1024,256]{1,0:T(8,128)(2,1)}, f32[1,128]{1,0:T(1,128)}, f32[1,128]{1,0:T(1,128)}) custom-call(f32[1024,2560]{1,0:T(8,128)} %shard_map.257.q_ref.k_ref.v_ref, f32[1024,2560]{1,0:T(8,128)} %shard_map.257.q_ref.k_ref.v_ref, ...), custom_call_target="tpu_custom_call", output_to_operand_aliasing={{0}: (15, {})} | custom-call | tf_op jit(solution)/shard_map/pallas_call | solution.py:268
  408.1 2.7 constant_dynamic-update-slice_fusion.2
  413.3 7.6 %convolution_convert_fusion.refs_0_ = bf16[1024,2560]{1,0:T(8,128)(2,1)} fusion(bf16[1024,1024]{1,0:T(8,128)(2,1)S(1)} %copy-done.28, bf16[1024,2560]{1,0:T(8,128)(2,1)S(1)} %get-tuple-element.162), kind=kOutput, calls=%fused_computation.10 | convolution fusion | flops 5371330560 | bytes 12582912 | tf_op jit(solution)/shard_map/dot_general | solution.py:35
  423.6 10.2 %shard_map.277 = bf16[512,2048]{1,0:T(8,128)(2,1)} custom-call(s32[1]{0:T(128)} %bitcast.turn_ref, bf16[1024,2048]{1,0:T(8,128)(2,1)} %get-tuple-element.106.refs_0_, bf16[1024,512]{1,0:T(8,128)(2,1)} %copy-done.37, bf16[2048,4608]{1,0:T(8,128)(2,1)} %all-gather.3.cloned.1.call-done.refs_1_.refs_2_.refs_3_, ...), custom_call_target="tpu_custom_call" | custom-call | tf_op jit(solution)/shard_map/pallas_call | solution.py:548
  435.1 7.6 %shard_map.282.refs_0_ = bf16[512,2048]{1,0:T(8,128)(2,1)} custom-call(s32[1]{0:T(128)} %bitcast.turn_ref, bf16[1024,4608]{1,0:T(8,128)(2,1)} %shard_map.267.act_ref.refs_0_, bf16[2048,4608]{1,0:T(8,128)(2,1)} %all-gather.5.cloned.1.call-done.gate_ref.up_ref.down_ref.refs_1_), custom_call_target="tpu_custom_call" | custom-call | tf_op jit(solution)/shard_map/pallas_call | solution.py:548
  443.5 9.6 %add_convert_fusion.1 = bf16[1024,2048]{1,0:T(8,128)(2,1)S(1)} fusion(bf16[1024,2048]{1,0:T(8,128)(2,1)} %collective-permute-done.7, bf16[1024,1024]{1,0:T(8,128)(2,1)} %copy-done.29, bf16[1024,2048]{1,0:T(8,128)(2,1)} %get-tuple-element.90.refs_0_.ctx_ref), kind=kOutput, calls=%fused_computation.6 | convolution fusion | flops 4301258752 | bytes 14680064 | tf_op jit(solution)/shard_map/dot_general | solution.py:35
  455.5 7.8 %add_convert_fusion = bf16[1024,2560]{1,0:T(8,128)(2,1)S(1)} fusion(bf16[1024,2560]{1,0:T(8,128)(2,1)} %collective-permute-done.6, bf16[1024,1024]{1,0:T(8,128)(2,1)S(1)} %copy-done.26, bf16[1024,2560]{1,0:T(8,128)(2,1)S(1)} %bitcast.81), kind=kOutput, calls=%fused_computation.2 | convolution fusion | flops 5376573440 | bytes 17825792 | tf_op jit(solution)/shard_map/dot_general | solution.py:35
  465.1 10.1 %shard_map.279 = bf16[512,2048]{1,0:T(8,128)(2,1)} custom-call(s32[1]{0:T(128)} %bitcast.turn_ref, bf16[1024,2048]{1,0:T(8,128)(2,1)} %get-tuple-element.106.refs_0_, bf16[1024,512]{1,0:T(8,128)(2,1)} %copy-done.37, bf16[2048,4608]{1,0:T(8,128)(2,1)} %all-gather.3.cloned.1.call-done.refs_1_.refs_2_.refs_3_, ...), custom_call_target="tpu_custom_call" | custom-call | tf_op jit(solution)/shard_map/pallas_call | solution.py:548
  475.2 7.7 %shard_map.280 = bf16[512,2048]{1,0:T(8,128)(2,1)} custom-call(s32[1]{0:T(128)} %bitcast.turn_ref, bf16[1024,4608]{1,0:T(8,128)(2,1)} %shard_map.267.act_ref.refs_0_, bf16[2048,4608]{1,0:T(8,128)(2,1)} %all-gather.5.cloned.1.call-done.gate_ref.up_ref.down_ref.refs_1_), custom_call_target="tpu_custom_call" | custom-call | tf_op jit(solution)/shard_map/pallas_call | solution.py:548
  483.5 23.5 %collective-permute-done.8 = bf16[2,2,128,2048]{3,2,1,0:T(8,128)(2,1)} collective-permute-done((bf16[2,2,128,2048]{3,2,1,0:T(8,128)(2,1)}, bf16[2,2,128,2048]{3,2,1,0:T(8,128)(2,1)}, u32[]{:S(2)}, u32[]{:S(2)}) %collective-permute-start.8) | collective-permute-done | bytes 2097184 | tf_op jit(solution)/shard_map/ppermute | solution.py:314
  511.0 23.3 %collective-permute-done.9 = bf16[2,2,128,1280]{3,2,1,0:T(8,128)(2,1)} collective-permute-done((bf16[2,2,128,1280]{3,2,1,0:T(8,128)(2,1)S(1)}, bf16[2,2,128,1280]{3,2,1,0:T(8,128)(2,1)}, u32[]{:S(2)}, u32[]{:S(2)}) %collective-permute-start.9) | collective-permute-done | bytes 1310752 | tf_op jit(solution)/shard_map/ppermute | solution.py:314
  540.0 4.5 add_convert_fusion.2
  544.5 7.7 %collective-permute-done.13 = bf16[2,128,1280]{2,1,0:T(8,128)(2,1)S(1)} collective-permute-done((bf16[2,128,1280]{2,1,0:T(8,128)(2,1)S(1)}, bf16[2,128,1280]{2,1,0:T(8,128)(2,1)S(1)}, u32[]{:S(2)}, u32[]{:S(2)}) %collective-permute-start.13) | collective-permute-done | bytes 655392 | tf_op jit(solution)/shard_map/ppermute | solution.py:314
  554.2 2.4 collective-permute-start.18
  558.6 4.0 fusion.5
  563.3 4.8 fusion.13
  568.2 2.4 collective-permute-start.17
  571.3 17.0 %collective-permute-done.18.refs_3_ = bf16[128,1280]{1,0:T(8,128)(2,1)S(1)} collective-permute-done((bf16[128,1280]{1,0:T(8,128)(2,1)S(1)}, bf16[128,1280]{1,0:T(8,128)(2,1)S(1)}, u32[]{:S(2)}, u32[]{:S(2)}) %collective-permute-start.18) | collective-permute-done | bytes 327712 | tf_op jit(solution)/shard_map/ppermute | solution.py:314
  588.3 18.2 %collective-permute-done.17.refs_2_ = bf16[128,1280]{1,0:T(8,128)(2,1)S(1)} collective-permute-done((bf16[128,1280]{1,0:T(8,128)(2,1)S(1)}, bf16[128,1280]{1,0:T(8,128)(2,1)S(1)}, u32[]{:S(2)}, u32[]{:S(2)}) %collective-permute-start.17) | collective-permute-done | bytes 327712 | tf_op jit(solution)/shard_map/ppermute | solution.py:314
  615.1 2.7 collective-permute-done.21
  619.5 2.9 collective-permute-done.22
  (224 shorter events, 81.8 us)
Async XLA Ops:
  7.2 104.7 %all-gather.3.cloned.1.call-start = ((), (), s32[]{:S(2)}) async-start(), calls=%async_computation.1 | async-start | bytes 20054016 | tf_op jit(solution)/shard_map/all_gather | solution.py:646
  9.7 202.8 %all-gather.5.cloned.1.call-start = ((), (), s32[]{:S(2)}) async-start(), calls=%async_computation.2 | async-start | bytes 20054016 | tf_op jit(solution)/shard_map/all_gather | solution.py:650
  10.9 50.2 %copy-start.17 = (bf16[512,2048]{1,0:T(8,128)(2,1)S(1)}, bf16[512,2048]{1,0:T(8,128)(2,1)}, u32[]{:S(2)}) copy-start(bf16[512,2048]{1,0:T(8,128)(2,1)} %one_ref.3) | copy-start | bytes 6291460
  12.1 615.4 %reduce-scatter.2.cloned.1.call-start = ((), (), s32[]{:S(2)}) async-start(), calls=%async_computation.3 | async-start | bytes 20054016 | tf_op jit(solution)/shard_map/reduce_scatter | solution.py:696
  12.1 49.0 %collective-permute-start = (bf16[512,2048]{1,0:T(8,128)(2,1)}, bf16[512,2048]{1,0:T(8,128)(2,1)}, u32[]{:S(2)}, u32[]{:S(2)}) collective-permute-start(bf16[512,2048]{1,0:T(8,128)(2,1)} %one_ref.2), channel_id=1, source_target_pairs={{0,1},{1,0},{2,3},{3,2},{4,5},{5,4},{6,7},{7,6},{8,9},{9,8},{10,11... | collective-permute-start | bytes 6291464 | tf_op jit(solution)/shard_map/ppermute | solution.py:318
  17.5 135.5 %copy-start.7 = (f32[1024,128]{1,0:T(8,128)}, f32[1024,128]{1,0:T(8,128)S(1)}, u32[]{:S(2)}) copy-start(f32[1024,128]{1,0:T(8,128)S(1)} %get-tuple-element.174.qcos_ref.kcos_ref) | copy-start | bytes 1572868
  17.5 135.5 %copy-start.8 = (f32[1024,128]{1,0:T(8,128)}, f32[1024,128]{1,0:T(8,128)S(1)}, u32[]{:S(2)}) copy-start(f32[1024,128]{1,0:T(8,128)S(1)} %get-tuple-element.175.qsin_ref.ksin_ref) | copy-start | bytes 1572868
  17.5 54.6 %copy-start.23 = (s32[16]{0:T(128)}, s32[16]{0:T(128)S(1)}, u32[]{:S(2)}) copy-start(s32[16]{0:T(128)S(1)} %broadcast_xor_fusion.order_ref) | copy-start | bytes 196
  61.1 114.7 %collective-permute-start.1 = (bf16[512,2048]{1,0:T(8,128)(2,1)S(1)}, bf16[512,2048]{1,0:T(8,128)(2,1)}, u32[]{:S(2)}, u32[]{:S(2)}) collective-permute-start(bf16[512,2048]{1,0:T(8,128)(2,1)S(1)} %copy-done.17), channel_id=1, source_target_pairs={{0,1},{1,0},{2,3},{3,2},{4,5},{5,4},{6,7},{7,6},{8,9},{9,8},{10,11... | collective-permute-start | bytes 6291464 | tf_op jit(solution)/shard_map/ppermute | solution.py:318
  76.5 51.4 %copy-start.21 = (f32[1,128]{1,0:T(1,128)S(1)}, f32[1,128]{1,0:T(1,128)}, u32[]{:S(2)}) copy-start(f32[1,128]{1,0:T(1,128)} %qg_ref.7) | copy-start | bytes 1540
  76.5 51.4 %copy-start.22 = (f32[1,128]{1,0:T(1,128)S(1)}, f32[1,128]{1,0:T(1,128)}, u32[]{:S(2)}) copy-start(f32[1,128]{1,0:T(1,128)} %kg_ref.7) | copy-start | bytes 1540
  151.2 48.8 %collective-permute-start.2 = (bf16[512,2048]{1,0:T(8,128)(2,1)}, bf16[512,2048]{1,0:T(8,128)(2,1)}, u32[]{:S(2)}, u32[]{:S(2)}) collective-permute-start(bf16[512,2048]{1,0:T(8,128)(2,1)} %shard_map.259.part_ref), channel_id=1, source_target_pairs={{0,1},{1,0},{2,3},{3,2},{4,5},{5,4},{6,7},{7,6},{8,9},{9,8},{10,11... | collective-permute-start | bytes 6291464 | tf_op jit(solution)/shard_map/ppermute | solution.py:318
  164.5 9.3 %copy-start.51 = (s32[1,1024,2]{1,2,0:T(2,128)S(1)}, s32[1,1024,2]{1,2,0:T(2,128)}, u32[]{:S(2)}) copy-start(s32[1,1024,2]{1,2,0:T(2,128)} %param.18) | copy-start | bytes 24580
  164.5 10.3 %copy-start.52 = (f32[1,1024,2]{1,2,0:T(2,128)S(1)}, f32[1,1024,2]{1,2,0:T(2,128)}, u32[]{:S(2)}) copy-start(f32[1,1024,2]{1,2,0:T(2,128)} %param.19) | copy-start | bytes 24580
  173.4 71.0 %collective-permute-start.3 = (bf16[512,2048]{1,0:T(8,128)(2,1)}, bf16[512,2048]{1,0:T(8,128)(2,1)}, u32[]{:S(2)}, u32[]{:S(2)}) collective-permute-start(bf16[512,2048]{1,0:T(8,128)(2,1)} %shard_map.261.part_ref), channel_id=1, source_target_pairs={{0,1},{1,0},{2,3},{3,2},{4,5},{5,4},{6,7},{7,6},{8,9},{9,8},{10,11... | collective-permute-start | bytes 6291464 | tf_op jit(solution)/shard_map/ppermute | solution.py:318
  175.8 24.1 %copy-start.1 = (bf16[1024,2048]{1,0:T(8,128)(2,1)S(1)}, bf16[1024,2048]{1,0:T(8,128)(2,1)}, u32[]{:S(2)}) copy-start(bf16[1024,2048]{1,0:T(8,128)(2,1)} %copy-done) | copy-start | bytes 12582916
  175.8 24.1 %copy-start.15 = (bf16[512,2048]{1,0:T(8,128)(2,1)S(1)}, bf16[512,2048]{1,0:T(8,128)(2,1)}, u32[]{:S(2)}) copy-start(bf16[512,2048]{1,0:T(8,128)(2,1)} %shard_map.259.part_ref) | copy-start | bytes 6291460
  175.8 24.1 %copy-start.18 = (f32[1,2048]{1,0:T(1,128)S(1)}, f32[1,2048]{1,0:T(1,128)}, u32[]{:S(2)}) copy-start(f32[1,2048]{1,0:T(1,128)} %gain_ref.7) | copy-start | bytes 24580
  230.1 14.3 %copy-start.2 = (bf16[1024,2048]{1,0:T(8,128)(2,1)S(1)}, bf16[1024,2048]{1,0:T(8,128)(2,1)}, u32[]{:S(2)}) copy-start(bf16[1024,2048]{1,0:T(8,128)(2,1)} %copy-done) | copy-start | bytes 12582916
  230.1 14.3 %copy-start.16 = (bf16[512,2048]{1,0:T(8,128)(2,1)S(1)}, bf16[512,2048]{1,0:T(8,128)(2,1)}, u32[]{:S(2)}) copy-start(bf16[512,2048]{1,0:T(8,128)(2,1)} %shard_map.261.part_ref) | copy-start | bytes 6291460
  241.6 64.8 %collective-permute-start.4 = (bf16[512,2048]{1,0:T(8,128)(2,1)}, bf16[512,2048]{1,0:T(8,128)(2,1)}, u32[]{:S(2)}, u32[]{:S(2)}) collective-permute-start(bf16[512,2048]{1,0:T(8,128)(2,1)} %shard_map.265.part_ref), channel_id=1, source_target_pairs={{0,1},{1,0},{2,3},{3,2},{4,5},{5,4},{6,7},{7,6},{8,9},{9,8},{10,11... | collective-permute-start | bytes 6291464 | tf_op jit(solution)/shard_map/ppermute | solution.py:318
  306.4 51.4 %collective-permute-start.5 = (bf16[512,2048]{1,0:T(8,128)(2,1)}, bf16[512,2048]{1,0:T(8,128)(2,1)}, u32[]{:S(2)}, u32[]{:S(2)}) collective-permute-start(bf16[512,2048]{1,0:T(8,128)(2,1)} %shard_map.270.part_ref), channel_id=1, source_target_pairs={{0,1},{1,0},{2,3},{3,2},{4,5},{5,4},{6,7},{7,6},{8,9},{9,8},{10,11... | collective-permute-start | bytes 6291464 | tf_op jit(solution)/shard_map/ppermute | solution.py:318
  330.0 27.8 %copy-start.6 = (bf16[1024,2048]{1,0:T(8,128)(2,1)S(1)}, bf16[1024,2048]{1,0:T(8,128)(2,1)}, u32[]{:S(2)}) copy-start(bf16[1024,2048]{1,0:T(8,128)(2,1)} %copy-done.4) | copy-start | bytes 12582916
  386.9 56.6 %collective-permute-start.7 = (bf16[1024,2048]{1,0:T(8,128)(2,1)}, bf16[1024,2048]{1,0:T(8,128)(2,1)}, u32[]{:S(2)}, u32[]{:S(2)}) collective-permute-start(bf16[1024,2048]{1,0:T(8,128)(2,1)} %shard_map.283), channel_id=1, source_target_pairs={{0,2},{2,0},{4,6},{6,4},{8,10},{10,8},{12,14},{14,12},{16,18},{18,... | collective-permute-start | bytes 12582920 | tf_op jit(solution)/shard_map/ppermute | solution.py:314
  411.0 9.9 %copy-start.37 = (bf16[1024,512]{1,0:T(8,128)(2,1)}, bf16[1024,512]{1,0:T(8,128)(2,1)S(1)}, u32[]{:S(2)}) copy-start(bf16[1024,512]{1,0:T(8,128)(2,1)S(1)} %get-tuple-element.161.refs_1_) | copy-start | bytes 3145732
  420.9 34.5 %collective-permute-start.6 = (bf16[1024,2560]{1,0:T(8,128)(2,1)}, bf16[1024,2560]{1,0:T(8,128)(2,1)}, u32[]{:S(2)}, u32[]{:S(2)}) collective-permute-start(bf16[1024,2560]{1,0:T(8,128)(2,1)} %shard_map.278), channel_id=1, source_target_pairs={{0,2},{2,0},{4,6},{6,4},{8,10},{10,8},{12,14},{14,12},{16,18},{18,... | collective-permute-start | bytes 15728648 | tf_op jit(solution)/shard_map/ppermute | solution.py:314
  433.8 124.8 %collective-permute-start.15 = (bf16[512,2048]{1,0:T(8,128)(2,1)}, bf16[512,2048]{1,0:T(8,128)(2,1)}, u32[]{:S(2)}, u32[]{:S(2)}) collective-permute-start(bf16[512,2048]{1,0:T(8,128)(2,1)} %shard_map.277), channel_id=1, source_target_pairs={{0,1},{1,0},{2,3},{3,2},{4,5},{5,4},{6,7},{7,6},{8,9},{9,8},{10,11... | collective-permute-start | bytes 6291464 | tf_op jit(solution)/shard_map/ppermute | solution.py:318
  442.7 12.8 %slice-start = ((s8[5242880]{0:T(1024)(128)(4,1)}), s8[1048576]{0:T(1024)(128)(4,1)S(1)}, s32[]{:S(2)}) async-start(s8[5242880]{0:T(1024)(128)(4,1)} %bitcast.80), calls=%async_computation.4 | async-start | bytes 2097152
  442.7 96.4 %collective-permute-start.12 = (bf16[512,2048]{1,0:T(8,128)(2,1)}, bf16[512,2048]{1,0:T(8,128)(2,1)}, u32[]{:S(2)}, u32[]{:S(2)}) collective-permute-start(bf16[512,2048]{1,0:T(8,128)(2,1)} %shard_map.284), channel_id=1, source_target_pairs={{0,1},{1,0},{2,3},{3,2},{4,5},{5,4},{6,7},{7,6},{8,9},{9,8},{10,11... | collective-permute-start | bytes 6291464 | tf_op jit(solution)/shard_map/ppermute | solution.py:318
  443.5 11.9 %slice-start.1 = ((s8[5242880]{0:T(1024)(128)(4,1)}), s8[4194304]{0:T(1024)(128)(4,1)S(1)}, s32[]{:S(2)}) async-start(s8[5242880]{0:T(1024)(128)(4,1)} %bitcast.80), calls=%async_computation.5 | async-start | bytes 8388608
  454.8 52.2 %collective-permute-start.8 = (bf16[2,2,128,2048]{3,2,1,0:T(8,128)(2,1)}, bf16[2,2,128,2048]{3,2,1,0:T(8,128)(2,1)}, u32[]{:S(2)}, u32[]{:S(2)}) collective-permute-start(bf16[2,2,128,2048]{3,2,1,0:T(8,128)(2,1)} %bitcast.10), channel_id=1, source_target_pairs={{0,4},{2,6},{4,0},{6,2},{8,12},{10,14},{12,8},{14,10},{16,20},{18,... | collective-permute-start | bytes 6291464 | tf_op jit(solution)/shard_map/ppermute | solution.py:314
  463.5 70.8 %collective-permute-start.9 = (bf16[2,2,128,1280]{3,2,1,0:T(8,128)(2,1)S(1)}, bf16[2,2,128,1280]{3,2,1,0:T(8,128)(2,1)}, u32[]{:S(2)}, u32[]{:S(2)}) collective-permute-start(bf16[2,2,128,1280]{3,2,1,0:T(8,128)(2,1)S(1)} %get-tuple-element.137), channel_id=1, source_target_pairs={{0,4},{2,6},{4,0},{6,2},{8,12},{10,14},{12,8},{14,10},{16,20},{18,... | collective-permute-start | bytes 3932168 | tf_op jit(solution)/shard_map/ppermute | solution.py:314
  482.9 54.7 %collective-permute-start.10 = (bf16[2,2,128,1280]{3,2,1,0:T(8,128)(2,1)S(1)}, bf16[2,2,128,1280]{3,2,1,0:T(8,128)(2,1)S(1)}, u32[]{:S(2)}, u32[]{:S(2)}) collective-permute-start(bf16[2,2,128,1280]{3,2,1,0:T(8,128)(2,1)S(1)} %get-tuple-element.139), channel_id=1, source_target_pairs={{0,8},{2,10},{4,12},{6,14},{8,0},{10,2},{12,4},{14,6},{16,24},{18,... | collective-permute-start | bytes 3932168 | tf_op jit(solution)/shard_map/ppermute | solution.py:314
  509.6 29.1 %collective-permute-start.11 = (bf16[2,128,2048]{2,1,0:T(8,128)(2,1)S(1)}, bf16[2,128,2048]{2,1,0:T(8,128)(2,1)S(1)}, u32[]{:S(2)}, u32[]{:S(2)}) collective-permute-start(bf16[2,128,2048]{2,1,0:T(8,128)(2,1)S(1)} %get-tuple-element.145), channel_id=1, source_target_pairs={{0,8},{2,10},{4,12},{6,14},{8,0},{10,2},{12,4},{14,6},{16,24},{18,... | collective-permute-start | bytes 3145736 | tf_op jit(solution)/shard_map/ppermute | solution.py:314
  536.1 16.1 %collective-permute-start.13 = (bf16[2,128,1280]{2,1,0:T(8,128)(2,1)S(1)}, bf16[2,128,1280]{2,1,0:T(8,128)(2,1)S(1)}, u32[]{:S(2)}, u32[]{:S(2)}) collective-permute-start(bf16[2,128,1280]{2,1,0:T(8,128)(2,1)S(1)} %get-tuple-element.147), channel_id=1, source_target_pairs={{0,8},{2,10},{4,12},{6,14},{8,0},{10,2},{12,4},{14,6},{16,24},{18,... | collective-permute-start | bytes 1966088 | tf_op jit(solution)/shard_map/ppermute | solution.py:314
  538.0 16.0 %collective-permute-start.14 = (bf16[2,128,1280]{2,1,0:T(8,128)(2,1)S(1)}, bf16[2,128,1280]{2,1,0:T(8,128)(2,1)S(1)}, u32[]{:S(2)}, u32[]{:S(2)}) collective-permute-start(bf16[2,128,1280]{2,1,0:T(8,128)(2,1)S(1)} %get-tuple-element.149), channel_id=1, source_target_pairs={{0,4},{2,6},{4,0},{6,2},{8,12},{10,14},{12,8},{14,10},{16,20},{18,... | collective-permute-start | bytes 1966088 | tf_op jit(solution)/shard_map/ppermute | solution.py:314
  544.5 12.9 %copy-start.3 = (bf16[1024,2048]{1,0:T(8,128)(2,1)S(1)}, bf16[1024,2048]{1,0:T(8,128)(2,1)}, u32[]{:S(2)}) copy-start(bf16[1024,2048]{1,0:T(8,128)(2,1)} %copy-done) | copy-start | bytes 12582916
  544.5 12.9 %copy-start.35 = (bf16[512,2048]{1,0:T(8,128)(2,1)S(1)}, bf16[512,2048]{1,0:T(8,128)(2,1)}, u32[]{:S(2)}) copy-start(bf16[512,2048]{1,0:T(8,128)(2,1)} %shard_map.277) | copy-start | bytes 6291460
  554.2 34.0 %collective-permute-start.18 = (bf16[128,1280]{1,0:T(8,128)(2,1)S(1)}, bf16[128,1280]{1,0:T(8,128)(2,1)S(1)}, u32[]{:S(2)}, u32[]{:S(2)}) collective-permute-start(bf16[128,1280]{1,0:T(8,128)(2,1)S(1)} %get-tuple-element.158), channel_id=1, source_target_pairs={{0,16},{2,18},{4,20},{6,22},{8,24},{10,26},{12,28},{14,30},{16,0},... | collective-permute-start | bytes 983048 | tf_op jit(solution)/shard_map/ppermute | solution.py:314
  556.8 49.6 %collective-permute-start.16 = (bf16[128,2048]{1,0:T(8,128)(2,1)S(1)}, bf16[128,2048]{1,0:T(8,128)(2,1)S(1)}, u32[]{:S(2)}, u32[]{:S(2)}) collective-permute-start(bf16[128,2048]{1,0:T(8,128)(2,1)S(1)} %get-tuple-element.154), channel_id=1, source_target_pairs={{0,16},{2,18},{4,20},{6,22},{8,24},{10,26},{12,28},{14,30},{16,0},... | collective-permute-start | bytes 1572872 | tf_op jit(solution)/shard_map/ppermute | solution.py:314
  568.2 38.2 %collective-permute-start.17 = (bf16[128,1280]{1,0:T(8,128)(2,1)S(1)}, bf16[128,1280]{1,0:T(8,128)(2,1)S(1)}, u32[]{:S(2)}, u32[]{:S(2)}) collective-permute-start(bf16[128,1280]{1,0:T(8,128)(2,1)S(1)} %get-tuple-element.160), channel_id=1, source_target_pairs={{0,16},{2,18},{4,20},{6,22},{8,24},{10,26},{12,28},{14,30},{16,0},... | collective-permute-start | bytes 983048 | tf_op jit(solution)/shard_map/ppermute | solution.py:314
  588.3 18.2 %copy-start.43 = (bf16[128,1280]{1,0:T(8,128)(2,1)}, bf16[128,1280]{1,0:T(8,128)(2,1)S(1)}, u32[]{:S(2)}) copy-start(bf16[128,1280]{1,0:T(8,128)(2,1)S(1)} %collective-permute-done.18.refs_3_) | copy-start | bytes 983044
  607.9 16.1 %copy-start.42 = (bf16[128,2048]{1,0:T(8,128)(2,1)S(1)}, bf16[128,2048]{1,0:T(8,128)(2,1)}, u32[]{:S(2)}) copy-start(bf16[128,2048]{1,0:T(8,128)(2,1)} %copy-done.41) | copy-start | bytes 1572868
  607.9 1.4 collective-permute-start.19
  610.1 3.8 collective-permute-start.20
  613.9 3.8 collective-permute-start.21
  617.8 4.7 collective-permute-start.22
  622.5 3.8 collective-permute-start.23
  (37 other events, 125.5 us)
Sparse Core Ops, SparseCore 0:
  10.2 101.6 all-gather.2
  113.5 98.9 all-gather.4
  294.3 194.4 reduce-scatter.1

commit v5 on v4

--- a/solution.py
+++ b/solution.py
@@ -541,21 +541,22 @@
     total = form(refs[0][...], refs[count][...])
     for i in range(1, count):
         total = total + form(refs[i][...], refs[count + i][...])
-    refs[2 * count][...] = total.astype(refs[2 * count].dtype)
-
-
-def product(form, lefts, rights, rows, steps, block, kind, turn):
+    refs[-1][...] = total.astype(refs[-1].dtype)
+
+
+def product(form, lefts, rights, rows, steps, block, kind, turn, needed=()):
     return pl.pallas_call(
         functools.partial(product_kernel, len(lefts), form),
         grid_spec=pltpu.PrefetchScalarGridSpec(
             num_scalar_prefetch=1,
             grid=(steps,),
-            in_specs=[pl.BlockSpec(shape, index) for _, shape, index in lefts + rights],
+            in_specs=[pl.BlockSpec(shape, index) for _, shape, index in lefts + rights]
+            + [pl.BlockSpec(memory_space=pl.ANY)] * len(needed),
             out_specs=pl.BlockSpec((rows, block), lambda i, turn_ref: (0, i)),
         ),
         out_shape=jax.ShapeDtypeStruct((rows, steps * block), kind),
         compiler_params=params(56),
-    )(turn.reshape(1), *[item[0] for item in lefts + rights])
+    )(turn.reshape(1), *[item[0] for item in lefts + rights], *needed)
 
 
 def fold(keep, received):
@@ -710,9 +711,9 @@
     def expert_out(who, *needed):
         return product(
             dot_nt,
-            [(after(acts, *needed), (chunk, flat), lambda i, t: (who(t[0]), 2))],
+            [(acts, (chunk, flat), lambda i, t: (who(t[0]), 2))],
             [(ffn_w, (tall, flat), lambda i, t: (i, 2))],
-            chunk, width // tall, tall, BF, turn,
+            chunk, width // tall, tall, BF, turn, needed,
         )
 
     grad_mid, grad_mid_b, ffn_parts, grad_context = {}, {}, {}, {}
@@ -731,9 +732,7 @@
         if index == 0:
             grad_mid_rel = join(after(grad_mid_b[0], last), grad_mid_b[1], 0, order, 2)
             out_sum = Reduction(grad_mid_rel, context, straight, [])
-            out_theirs = expert_out(lambda t: 1 - t, out_sum.sent)
-            out_got = swap_pair(tie(out_theirs, back_got[0]))
-            last = out_sum.keep(out_theirs)
+            last = out_sum.keep(out_sum.sent)
         dq, dk, dv, query_part, key_part = attention_bwd(
             raw, q_cols, kv_cols, chunk, index, context, after(grad_context[index], last), lse[index],
             query_gain, key_gain, cosine, sine, earlier, index == 0,
@@ -763,7 +762,9 @@
     rest_sum, last = qkv_sum.keep_two(crossed, grad_qkv.shape[1] // 2, grad_theirs)
     grad_got = swap_pair(grad_theirs)
     grad_mine = normed_back(lambda t: t, last)
-    out_mine = expert_out(lambda t: t, grad_mine)
+    out_theirs = expert_out(lambda t: 1 - t, grad_mine)
+    out_got = swap_pair(out_theirs)
+    out_mine = expert_out(lambda t: t, out_theirs)
     last = out_sum.step(out_mine)
     last = qkv_sum.step(last)
     last = rest_sum.step(last)

time: 644 us -> 649 us (level)
  waiting for transfers between devices: 205 us -> 214 us
    ppermute x15, waiting for transfers between devices: 99.3 us -> 108 us  [swap(): return lax.ppermute(value, 'dp', [(i, i ^ 1 << bit) for i in range(count)])]
  transfers between devices with their start and end apart: 27 -> 27, of which waited for: 16 -> 16; matrix products, arithmetic and copies ran while one was open for 12% -> 11% of each run, Pallas kernels for 45% -> 44%
where the time goes in v5:
time: 649 us; the launch traced here: 644 us
  Pallas kernels  287 us (44%)
  waiting for transfers between devices  214 us (33%)
  local copies, waits for them, and re-layouts  36.9 us (6%)
  other arithmetic  33.5 us (5%)
  matrix products  30.3 us (5%)
  starting transfers between devices  28.4 us (4%)
  between operations  14.7 us (2%)
    pallas_call x11, Pallas kernels, product(): pl.pallas_call(functools.partial(product_kernel, len(lefts), form), grid_...  112 us
    ppermute x15, waiting for transfers between devices, swap(): return lax.ppermute(value, 'dp', [(i, i ^ 1 << bit) for i in range(count)])  108 us
    ppermute x9, waiting for transfers between devices, swap_pair(): return lax.ppermute(value, 'tensor', [(0, 1), (1, 0)])  63.2 us
    pallas_call x2, Pallas kernels, attention_bwd(): pl.pallas_call(functools.partial(attn_bwd_kernel, min(256, chunk), keys,...  48.8 us
    pallas_call x2, Pallas kernels, expert_part(): pl.pallas_call(functools.partial(expert_kernel, unit, cols), grid=(steps,...  35.4 us
    all_gather x1, waiting for transfers between devices, body(): lax.all_gather(jnp.concatenate([out_weight[0], query_weight[0], key_weigh...  35.3 us
    dot_general x4, matrix products, dot_tn(): lax.dot_general(left, right, (((0,), (0,)), ((), ())), preferred_element_...  30.3 us
    pallas_call x1, Pallas kernels, expert_weights(): pl.pallas_call(functools.partial(expert_weight_kernel, 2 * flat // block)...  26.9 us
  transfers between devices with their start and end apart: 27, of which 16 were waited for; matrix products, arithmetic and copies ran while one was open for 11% of the time, Pallas kernels for 44%

profile of v5, /device:TPU:0, one launch (start us, length us, event | category | flops | bytes accessed | tf_op | source)
XLA Modules:
  0.0 644.4 jit_solution(5295239668786898498)
XLA Ops:
  12.1 3.0 collective-permute-start
  17.5 43.6 %collective-permute-done.two_ref = bf16[512,2048]{1,0:T(8,128)(2,1)} collective-permute-done((bf16[512,2048]{1,0:T(8,128)(2,1)}, bf16[512,2048]{1,0:T(8,128)(2,1)}, u32[]{:S(2)}, u32[]{:S(2)}) %collective-permute-start) | collective-permute-done | bytes 2097184 | tf_op jit(solution)/shard_map/ppermute | solution.py:318
  62.8 5.3 shard_map.255.base_ref
  76.6 35.3 %all-gather.3.cloned.1.call-done.refs_1_.refs_2_.refs_3_ = bf16[2048,4608]{1,0:T(8,128)(2,1)} async-done(((bf16[128,4608]{1,0:T(8,128)(2,1)}), bf16[2048,4608]{1,0:T(8,128)(2,1)}) %all-gather.3.cloned.1.call-update) | async-done | bytes 18874384 | tf_op jit(solution)/shard_map/all_gather | solution.py:647
  111.9 16.0 %shard_map.257.q_ref.k_ref.v_ref = f32[1024,2560]{1,0:T(8,128)} custom-call(s32[1]{0:T(128)} %bitcast.turn_ref, bf16[1024,2048]{1,0:T(8,128)(2,1)} %copy-done.33, bf16[2048,4608]{1,0:T(8,128)(2,1)} %all-gather.3.cloned.1.call-done.refs_1_.refs_2_.refs_3_), custom_call_target="tpu_custom_call" | custom-call | tf_op jit(solution)/shard_map/pallas_call | solution.py:548
  127.9 13.7 %shard_map.258 = (bf16[1024,2048]{1,0:T(8,128)(2,1)}, f32[16,1,512]{2,1,0:T(1,128)S(1)}) custom-call(f32[1024,2560]{1,0:T(8,128)} %shard_map.257.q_ref.k_ref.v_ref, f32[1024,2560]{1,0:T(8,128)} %shard_map.257.q_ref.k_ref.v_ref, f32[1024,2560]{1,0:T(8,128)} %shard_map.257.q_ref.k_ref.v_ref, f32[1,128]{1,0:T(1,128)S(1)} %copy-done.21, ...), custom_call_target="tpu_custom_call" | custom-call | tf_op jit(solution)/shard_map/pallas_call | solution.py:129
  142.3 9.0 %shard_map.259.part_ref = bf16[512,2048]{1,0:T(8,128)(2,1)} custom-call(s32[1]{0:T(128)} %bitcast.turn_ref, bf16[1024,2048]{1,0:T(8,128)(2,1)} %get-tuple-element.74.refs_0_.rest_0_, bf16[2048,4608]{1,0:T(8,128)(2,1)} %all-gather.3.cloned.1.call-done.refs_1_.refs_2_.refs_3_), custom_call_target="tpu_custom_call" | custom-call | tf_op jit(solution)/shard_map/pallas_call | solution.py:548
  153.0 10.9 %shard_map.260 = (bf16[1024,2048]{1,0:T(8,128)(2,1)}, f32[16,1,512]{2,1,0:T(1,128)S(1)}) custom-call(f32[1024,2560]{1,0:T(8,128)} %shard_map.257.q_ref.k_ref.v_ref, f32[1024,2560]{1,0:T(8,128)} %shard_map.257.q_ref.k_ref.v_ref, f32[1024,2560]{1,0:T(8,128)} %shard_map.257.q_ref.k_ref.v_ref, f32[1,128]{1,0:T(1,128)S(1)} %copy-done.21, ...), custom_call_target="tpu_custom_call", output_to_operand_aliasing={{0}: (9, {})} | custom-call | tf_op jit(solution)/shard_map/pallas_call | solution.py:129
  164.5 8.9 %shard_map.261.part_ref = bf16[512,2048]{1,0:T(8,128)(2,1)} custom-call(s32[1]{0:T(128)} %bitcast.turn_ref, bf16[1024,2048]{1,0:T(8,128)(2,1)} %get-tuple-element.88.refs_0_.ctx_ref, bf16[2048,4608]{1,0:T(8,128)(2,1)} %all-gather.3.cloned.1.call-done.refs_1_.refs_2_.refs_3_), custom_call_target="tpu_custom_call" | custom-call | tf_op jit(solution)/shard_map/pallas_call | solution.py:548
  175.8 4.9 shard_map.262.cot_ref.base_ref
  182.8 17.1 %collective-permute-done.2.got_ref = bf16[512,2048]{1,0:T(8,128)(2,1)} collective-permute-done((bf16[512,2048]{1,0:T(8,128)(2,1)}, bf16[512,2048]{1,0:T(8,128)(2,1)}, u32[]{:S(2)}, u32[]{:S(2)}) %collective-permute-start.2) | collective-permute-done | bytes 2097184 | tf_op jit(solution)/shard_map/ppermute | solution.py:318
  200.0 5.2 shard_map.263
  205.2 7.3 %all-gather.5.cloned.1.call-done.gate_ref.up_ref.down_ref.refs_1_ = bf16[2048,4608]{1,0:T(8,128)(2,1)} async-done(((bf16[128,4608]{1,0:T(8,128)(2,1)}), bf16[2048,4608]{1,0:T(8,128)(2,1)}) %all-gather.5.cloned.1.call-update) | async-done | bytes 18874384 | tf_op jit(solution)/shard_map/all_gather | solution.py:651
  212.5 17.7 %shard_map.264.refs_0_.rest_0_ = bf16[1024,4608]{1,0:T(8,128)(2,1)} custom-call(bf16[1024,2048]{1,0:T(8,128)(2,1)} %get-tuple-element.81.x_ref.rest_0_, bf16[1024,2048]{1,0:T(8,128)(2,1)} %copy-done.4, bf16[2048,4608]{1,0:T(8,128)(2,1)} %all-gather.5.cloned.1.call-done.gate_ref.up_ref.down_ref.refs_1_, ...), custom_call_target="tpu_custom_call" | custom-call | tf_op jit(solution)/shard_map/pallas_call | solution.py:500
  230.2 11.5 %shard_map.265.part_ref = bf16[512,2048]{1,0:T(8,128)(2,1)} custom-call(s32[1]{0:T(128)} %bitcast.turn_ref, bf16[1024,4608]{1,0:T(8,128)(2,1)} %shard_map.264.refs_0_.rest_0_, bf16[2048,4608]{1,0:T(8,128)(2,1)} %all-gather.5.cloned.1.call-done.gate_ref.up_ref.down_ref.refs_1_), custom_call_target="tpu_custom_call" | custom-call | tf_op jit(solution)/shard_map/pallas_call | solution.py:548
  244.5 5.2 shard_map.266
  249.6 17.7 %shard_map.267.act_ref.refs_0_ = bf16[1024,4608]{1,0:T(8,128)(2,1)} custom-call(bf16[1024,2048]{1,0:T(8,128)(2,1)} %get-tuple-element.84.x_ref.normed_ref, bf16[1024,2048]{1,0:T(8,128)(2,1)} %copy-done.4, bf16[2048,4608]{1,0:T(8,128)(2,1)} %all-gather.5.cloned.1.call-done.gate_ref.up_ref.down_ref.refs_1_, ...), custom_call_target="tpu_custom_call", output_to_operand_aliasing={{}: (7, {})} | custom-call | tf_op jit(solution)/shard_map/pallas_call | solution.py:500
  267.3 26.9 %shard_map.268 = bf16[2048,4608]{1,0:T(8,128)(2,1)} custom-call(bf16[1024,2048]{1,0:T(8,128)(2,1)} %get-tuple-element.84.x_ref.normed_ref, bf16[1024,2048]{1,0:T(8,128)(2,1)} %copy-done.4, bf16[1024,4608]{1,0:T(8,128)(2,1)} %shard_map.267.act_ref.refs_0_), custom_call_target="tpu_custom_call" | custom-call | tf_op jit(solution)/shard_map/pallas_call | solution.py:530
  294.2 12.1 %shard_map.269.refs_0_ = bf16[512,2048]{1,0:T(8,128)(2,1)} custom-call(s32[1]{0:T(128)} %bitcast.turn_ref, bf16[1024,4608]{1,0:T(8,128)(2,1)} %shard_map.267.act_ref.refs_0_, bf16[2048,4608]{1,0:T(8,128)(2,1)} %all-gather.5.cloned.1.call-done.gate_ref.up_ref.down_ref.refs_1_), custom_call_target="tpu_custom_call" | custom-call | tf_op jit(solution)/shard_map/pallas_call | solution.py:548
  308.3 3.0 copy-done.5
  311.3 8.0 %shard_map.271 = (f32[512,2048]{1,0:T(8,128)}, bf16[512,2048]{1,0:T(8,128)(2,1)S(1)}, f32[1,2048]{1,0:T(1,128)S(1)}) custom-call(bf16[1024,2048]{1,0:T(8,128)(2,1)S(1)} %copy-done.5, bf16[512,2048]{1,0:T(8,128)(2,1)S(1)} %copy-done.14, bf16[512,2048]{1,0:T(8,128)(2,1)} %collective-permute-done.4.refs_1_.got_ref, f32[512,2048]{1,0:T(8,128)} %get-tuple-element.83.mid_ref, ...), custom_call_target="tpu_custom_call" | custom-call | tf_op jit(solution)/shard_map/pallas_call | solution.py:447
  320.6 9.3 %shard_map.272.grad_ref = bf16[512,2048]{1,0:T(8,128)(2,1)} custom-call(s32[1]{0:T(128)} %bitcast.turn_ref, bf16[512,2048]{1,0:T(8,128)(2,1)} %copy-done.10, bf16[2048,4608]{1,0:T(8,128)(2,1)} %all-gather.3.cloned.1.call-done.refs_1_.refs_2_.refs_3_), custom_call_target="tpu_custom_call" | custom-call | tf_op jit(solution)/shard_map/pallas_call | solution.py:548
  329.9 27.7 %shard_map.273 = (bf16[1024,2048]{1,0:T(8,128)(2,1)}, f32[1024,256]{1,0:T(8,128)}, f32[1024,256]{1,0:T(8,128)}, f32[1,128]{1,0:T(1,128)}, f32[1,128]{1,0:T(1,128)}) custom-call(f32[1024,2560]{1,0:T(8,128)} %shard_map.257.q_ref.k_ref.v_ref, f32[1024,2560]{1,0:T(8,128)} %shard_map.257.q_ref.k_ref.v_ref, f32[1024,2560]{1,0:T(8,128)} %shard_map.257.q_ref.k_ref.v_ref, ...), custom_call_target="tpu_custom_call" | custom-call | tf_op jit(solution)/shard_map/pallas_call | solution.py:268
  359.3 7.2 %shard_map.274 = (f32[512,2048]{1,0:T(8,128)}, bf16[512,2048]{1,0:T(8,128)(2,1)S(1)}, f32[1,2048]{1,0:T(1,128)S(1)}) custom-call(bf16[1024,2048]{1,0:T(8,128)(2,1)S(1)} %copy-done.6, bf16[512,2048]{1,0:T(8,128)(2,1)S(1)} %copy-done.9, bf16[512,2048]{1,0:T(8,128)(2,1)} %collective-permute-done.5.got_ref, f32[512,2048]{1,0:T(8,128)} %get-tuple-element.82.mid_ref, ...), custom_call_target="tpu_custom_call" | custom-call | tf_op jit(solution)/shard_map/pallas_call | solution.py:447
  367.8 9.2 %shard_map.275.grad_ref = bf16[512,2048]{1,0:T(8,128)(2,1)} custom-call(s32[1]{0:T(128)} %bitcast.turn_ref, bf16[512,2048]{1,0:T(8,128)(2,1)} %copy-done.12, bf16[2048,4608]{1,0:T(8,128)(2,1)} %all-gather.3.cloned.1.call-done.refs_1_.refs_2_.refs_3_), custom_call_target="tpu_custom_call" | custom-call | tf_op jit(solution)/shard_map/pallas_call | solution.py:548
  379.1 6.6 %convolution_convert_fusion.1.refs_0_ = bf16[1024,2048]{1,0:T(8,128)(2,1)} fusion(bf16[1024,1024]{1,0:T(8,128)(2,1)S(1)} %get-tuple-element.107, bf16[1024,2048]{1,0:T(8,128)(2,1)S(1)} %copy-done.31), kind=kOutput, calls=%fused_computation.30 | convolution fusion | flops 4297064448 | bytes 10485760 | tf_op jit(solution)/shard_map/dot_general | solution.py:35
  385.7 21.1 %shard_map.276 = (bf16[1024,2048]{1,0:T(8,128)(2,1)}, bf16[1024,256]{1,0:T(8,128)(2,1)}, bf16[1024,256]{1,0:T(8,128)(2,1)}, f32[1,128]{1,0:T(1,128)}, f32[1,128]{1,0:T(1,128)}) custom-call(f32[1024,2560]{1,0:T(8,128)} %shard_map.257.q_ref.k_ref.v_ref, f32[1024,2560]{1,0:T(8,128)} %shard_map.257.q_ref.k_ref.v_ref, ...), custom_call_target="tpu_custom_call", output_to_operand_aliasing={{0}: (15, {})} | custom-call | tf_op jit(solution)/shard_map/pallas_call | solution.py:268
  406.9 2.9 constant_dynamic-update-slice_fusion.2
  412.2 7.6 %convolution_convert_fusion.refs_0_ = bf16[1024,2560]{1,0:T(8,128)(2,1)} fusion(bf16[1024,1024]{1,0:T(8,128)(2,1)S(1)} %copy-done.28, bf16[1024,2560]{1,0:T(8,128)(2,1)S(1)} %get-tuple-element.158), kind=kOutput, calls=%fused_computation.10 | convolution fusion | flops 5371330560 | bytes 12582912 | tf_op jit(solution)/shard_map/dot_general | solution.py:35
  422.4 10.4 %shard_map.277 = bf16[512,2048]{1,0:T(8,128)(2,1)} custom-call(s32[1]{0:T(128)} %bitcast.turn_ref, bf16[1024,2048]{1,0:T(8,128)(2,1)} %get-tuple-element.104.refs_0_, bf16[1024,512]{1,0:T(8,128)(2,1)} %copy-done.39, bf16[2048,4608]{1,0:T(8,128)(2,1)} %all-gather.3.cloned.1.call-done.refs_1_.refs_2_.refs_3_, ...), custom_call_target="tpu_custom_call" | custom-call | tf_op jit(solution)/shard_map/pallas_call | solution.py:548
  434.2 6.6 %add_convert_fusion.1 = bf16[1024,2048]{1,0:T(8,128)(2,1)S(1)} fusion(bf16[1024,2048]{1,0:T(8,128)(2,1)} %collective-permute-done.7, bf16[1024,1024]{1,0:T(8,128)(2,1)S(1)} %copy-done.30, bf16[1024,2048]{1,0:T(8,128)(2,1)S(1)} %copy-done.32), kind=kOutput, calls=%fused_computation.6 | convolution fusion | flops 4301258752 | bytes 14680064 | tf_op jit(solution)/shard_map/dot_general | solution.py:35
  443.9 9.5 %add_convert_fusion = bf16[1024,2560]{1,0:T(8,128)(2,1)S(1)} fusion(bf16[1024,2560]{1,0:T(8,128)(2,1)} %collective-permute-done.6, bf16[1024,1024]{1,0:T(8,128)(2,1)S(1)} %copy-done.26, bf16[1024,2560]{1,0:T(8,128)(2,1)} %copy-done.42), kind=kOutput, calls=%fused_computation.2 | convolution fusion | flops 5376573440 | bytes 17825792 | tf_op jit(solution)/shard_map/dot_general | solution.py:35
  455.2 10.0 %shard_map.279.refs_2_ = bf16[512,2048]{1,0:T(8,128)(2,1)} custom-call(s32[1]{0:T(128)} %bitcast.turn_ref, bf16[1024,2048]{1,0:T(8,128)(2,1)} %get-tuple-element.104.refs_0_, bf16[1024,512]{1,0:T(8,128)(2,1)} %copy-done.39, bf16[2048,4608]{1,0:T(8,128)(2,1)} %all-gather.3.cloned.1.call-done.refs_1_.refs_2_.refs_3_, ...), custom_call_target="tpu_custom_call" | custom-call | tf_op jit(solution)/shard_map/pallas_call | solution.py:548
  465.2 7.5 %shard_map.280.refs_2_ = bf16[512,2048]{1,0:T(8,128)(2,1)} custom-call(s32[1]{0:T(128)} %bitcast.turn_ref, bf16[1024,4608]{1,0:T(8,128)(2,1)} %shard_map.267.act_ref.refs_0_, bf16[2048,4608]{1,0:T(8,128)(2,1)} %all-gather.5.cloned.1.call-done.gate_ref.up_ref.down_ref.refs_1_, bf16[512,2048]{1,0:T(8,128)(2,1)} %shard_map.279.refs_2_), custom_call_target="tpu_custom_call" | custom-call | tf_op jit(solution)/shard_map/pallas_call | solution.py:548
  473.2 7.7 %shard_map.281 = bf16[512,2048]{1,0:T(8,128)(2,1)} custom-call(s32[1]{0:T(128)} %bitcast.turn_ref, bf16[1024,4608]{1,0:T(8,128)(2,1)} %shard_map.267.act_ref.refs_0_, bf16[2048,4608]{1,0:T(8,128)(2,1)} %all-gather.5.cloned.1.call-done.gate_ref.up_ref.down_ref.refs_1_, bf16[512,2048]{1,0:T(8,128)(2,1)} %shard_map.280.refs_2_), custom_call_target="tpu_custom_call" | custom-call | tf_op jit(solution)/shard_map/pallas_call | solution.py:548
  482.2 21.6 %collective-permute-done.8 = bf16[2,2,128,2048]{3,2,1,0:T(8,128)(2,1)S(1)} collective-permute-done((bf16[2,2,128,2048]{3,2,1,0:T(8,128)(2,1)}, bf16[2,2,128,2048]{3,2,1,0:T(8,128)(2,1)S(1)}, u32[]{:S(2)}, u32[]{:S(2)}) %collective-permute-start.8) | collective-permute-done | bytes 2097184 | tf_op jit(solution)/shard_map/ppermute | solution.py:314
  506.1 24.7 %collective-permute-done.9 = bf16[2,2,128,1280]{3,2,1,0:T(8,128)(2,1)} collective-permute-done((bf16[2,2,128,1280]{3,2,1,0:T(8,128)(2,1)}, bf16[2,2,128,1280]{3,2,1,0:T(8,128)(2,1)}, u32[]{:S(2)}, u32[]{:S(2)}) %collective-permute-start.9) | collective-permute-done | bytes 1310752 | tf_op jit(solution)/shard_map/ppermute | solution.py:314
  535.6 8.2 %collective-permute-done.11 = bf16[2,128,2048]{2,1,0:T(8,128)(2,1)S(1)} collective-permute-done((bf16[2,128,2048]{2,1,0:T(8,128)(2,1)S(1)}, bf16[2,128,2048]{2,1,0:T(8,128)(2,1)S(1)}, u32[]{:S(2)}, u32[]{:S(2)}) %collective-permute-start.11) | collective-permute-done | bytes 1048608 | tf_op jit(solution)/shard_map/ppermute | solution.py:314
  544.2 4.5 add_convert_fusion.2
  548.6 8.9 %collective-permute-done.13 = bf16[2,128,1280]{2,1,0:T(8,128)(2,1)S(1)} collective-permute-done((bf16[2,128,1280]{2,1,0:T(8,128)(2,1)S(1)}, bf16[2,128,1280]{2,1,0:T(8,128)(2,1)S(1)}, u32[]{:S(2)}, u32[]{:S(2)}) %collective-permute-start.13) | collective-permute-done | bytes 655392 | tf_op jit(solution)/shard_map/ppermute | solution.py:314
  558.0 2.5 collective-permute-start.18
  562.4 4.0 fusion.5
  567.1 4.8 fusion.13
  571.9 2.5 collective-permute-start.17
  575.0 18.5 %collective-permute-done.18.refs_3_ = bf16[128,1280]{1,0:T(8,128)(2,1)S(1)} collective-permute-done((bf16[128,1280]{1,0:T(8,128)(2,1)S(1)}, bf16[128,1280]{1,0:T(8,128)(2,1)S(1)}, u32[]{:S(2)}, u32[]{:S(2)}) %collective-permute-start.18) | collective-permute-done | bytes 327712 | tf_op jit(solution)/shard_map/ppermute | solution.py:314
  593.5 18.2 %collective-permute-done.17.refs_2_ = bf16[128,1280]{1,0:T(8,128)(2,1)S(1)} collective-permute-done((bf16[128,1280]{1,0:T(8,128)(2,1)S(1)}, bf16[128,1280]{1,0:T(8,128)(2,1)S(1)}, u32[]{:S(2)}, u32[]{:S(2)}) %collective-permute-start.17) | collective-permute-done | bytes 327712 | tf_op jit(solution)/shard_map/ppermute | solution.py:314
  620.4 2.7 collective-permute-done.21
  625.0 2.8 collective-permute-done.22
  (222 shorter events, 80.4 us)
Async XLA Ops:
  7.2 104.7 %all-gather.3.cloned.1.call-start = ((), (), s32[]{:S(2)}) async-start(), calls=%async_computation.1 | async-start | bytes 20054016 | tf_op jit(solution)/shard_map/all_gather | solution.py:647
  9.7 202.8 %all-gather.5.cloned.1.call-start = ((), (), s32[]{:S(2)}) async-start(), calls=%async_computation.2 | async-start | bytes 20054016 | tf_op jit(solution)/shard_map/all_gather | solution.py:651
  10.9 50.2 %copy-start.17 = (bf16[512,2048]{1,0:T(8,128)(2,1)S(1)}, bf16[512,2048]{1,0:T(8,128)(2,1)}, u32[]{:S(2)}) copy-start(bf16[512,2048]{1,0:T(8,128)(2,1)} %one_ref.3) | copy-start | bytes 6291460
  12.1 620.7 %reduce-scatter.2.cloned.1.call-start = ((), (), s32[]{:S(2)}) async-start(), calls=%async_computation.3 | async-start | bytes 20054016 | tf_op jit(solution)/shard_map/reduce_scatter | solution.py:697
  12.1 49.0 %collective-permute-start = (bf16[512,2048]{1,0:T(8,128)(2,1)}, bf16[512,2048]{1,0:T(8,128)(2,1)}, u32[]{:S(2)}, u32[]{:S(2)}) collective-permute-start(bf16[512,2048]{1,0:T(8,128)(2,1)} %one_ref.2), channel_id=1, source_target_pairs={{0,1},{1,0},{2,3},{3,2},{4,5},{5,4},{6,7},{7,6},{8,9},{9,8},{10,11... | collective-permute-start | bytes 6291464 | tf_op jit(solution)/shard_map/ppermute | solution.py:318
  17.5 135.5 %copy-start.7 = (f32[1024,128]{1,0:T(8,128)}, f32[1024,128]{1,0:T(8,128)S(1)}, u32[]{:S(2)}) copy-start(f32[1024,128]{1,0:T(8,128)S(1)} %get-tuple-element.170.qcos_ref.kcos_ref) | copy-start | bytes 1572868
  17.5 135.5 %copy-start.8 = (f32[1024,128]{1,0:T(8,128)}, f32[1024,128]{1,0:T(8,128)S(1)}, u32[]{:S(2)}) copy-start(f32[1024,128]{1,0:T(8,128)S(1)} %get-tuple-element.171.qsin_ref.ksin_ref) | copy-start | bytes 1572868
  17.5 54.6 %copy-start.23 = (s32[16]{0:T(128)}, s32[16]{0:T(128)S(1)}, u32[]{:S(2)}) copy-start(s32[16]{0:T(128)S(1)} %broadcast_xor_fusion.order_ref) | copy-start | bytes 196
  61.1 114.7 %collective-permute-start.1 = (bf16[512,2048]{1,0:T(8,128)(2,1)S(1)}, bf16[512,2048]{1,0:T(8,128)(2,1)}, u32[]{:S(2)}, u32[]{:S(2)}) collective-permute-start(bf16[512,2048]{1,0:T(8,128)(2,1)S(1)} %copy-done.17), channel_id=1, source_target_pairs={{0,1},{1,0},{2,3},{3,2},{4,5},{5,4},{6,7},{7,6},{8,9},{9,8},{10,11... | collective-permute-start | bytes 6291464 | tf_op jit(solution)/shard_map/ppermute | solution.py:318
  76.5 51.4 %copy-start.21 = (f32[1,128]{1,0:T(1,128)S(1)}, f32[1,128]{1,0:T(1,128)}, u32[]{:S(2)}) copy-start(f32[1,128]{1,0:T(1,128)} %qg_ref.7) | copy-start | bytes 1540
  76.5 51.4 %copy-start.22 = (f32[1,128]{1,0:T(1,128)S(1)}, f32[1,128]{1,0:T(1,128)}, u32[]{:S(2)}) copy-start(f32[1,128]{1,0:T(1,128)} %kg_ref.7) | copy-start | bytes 1540
  151.2 48.8 %collective-permute-start.2 = (bf16[512,2048]{1,0:T(8,128)(2,1)}, bf16[512,2048]{1,0:T(8,128)(2,1)}, u32[]{:S(2)}, u32[]{:S(2)}) collective-permute-start(bf16[512,2048]{1,0:T(8,128)(2,1)} %shard_map.259.part_ref), channel_id=1, source_target_pairs={{0,1},{1,0},{2,3},{3,2},{4,5},{5,4},{6,7},{7,6},{8,9},{9,8},{10,11... | collective-permute-start | bytes 6291464 | tf_op jit(solution)/shard_map/ppermute | solution.py:318
  173.4 71.0 %collective-permute-start.3 = (bf16[512,2048]{1,0:T(8,128)(2,1)}, bf16[512,2048]{1,0:T(8,128)(2,1)}, u32[]{:S(2)}, u32[]{:S(2)}) collective-permute-start(bf16[512,2048]{1,0:T(8,128)(2,1)} %shard_map.261.part_ref), channel_id=1, source_target_pairs={{0,1},{1,0},{2,3},{3,2},{4,5},{5,4},{6,7},{7,6},{8,9},{9,8},{10,11... | collective-permute-start | bytes 6291464 | tf_op jit(solution)/shard_map/ppermute | solution.py:318
  175.8 24.2 %copy-start.1 = (bf16[1024,2048]{1,0:T(8,128)(2,1)S(1)}, bf16[1024,2048]{1,0:T(8,128)(2,1)}, u32[]{:S(2)}) copy-start(bf16[1024,2048]{1,0:T(8,128)(2,1)} %copy-done) | copy-start | bytes 12582916
  175.8 24.2 %copy-start.15 = (bf16[512,2048]{1,0:T(8,128)(2,1)S(1)}, bf16[512,2048]{1,0:T(8,128)(2,1)}, u32[]{:S(2)}) copy-start(bf16[512,2048]{1,0:T(8,128)(2,1)} %shard_map.259.part_ref) | copy-start | bytes 6291460
  175.8 24.2 %copy-start.18 = (f32[1,2048]{1,0:T(1,128)S(1)}, f32[1,2048]{1,0:T(1,128)}, u32[]{:S(2)}) copy-start(f32[1,2048]{1,0:T(1,128)} %gain_ref.7) | copy-start | bytes 24580
  230.2 14.2 %copy-start.2 = (bf16[1024,2048]{1,0:T(8,128)(2,1)S(1)}, bf16[1024,2048]{1,0:T(8,128)(2,1)}, u32[]{:S(2)}) copy-start(bf16[1024,2048]{1,0:T(8,128)(2,1)} %copy-done) | copy-start | bytes 12582916
  230.2 14.2 %copy-start.16 = (bf16[512,2048]{1,0:T(8,128)(2,1)S(1)}, bf16[512,2048]{1,0:T(8,128)(2,1)}, u32[]{:S(2)}) copy-start(bf16[512,2048]{1,0:T(8,128)(2,1)} %shard_map.261.part_ref) | copy-start | bytes 6291460
  241.7 64.7 %collective-permute-start.4 = (bf16[512,2048]{1,0:T(8,128)(2,1)}, bf16[512,2048]{1,0:T(8,128)(2,1)}, u32[]{:S(2)}, u32[]{:S(2)}) collective-permute-start(bf16[512,2048]{1,0:T(8,128)(2,1)} %shard_map.265.part_ref), channel_id=1, source_target_pairs={{0,1},{1,0},{2,3},{3,2},{4,5},{5,4},{6,7},{7,6},{8,9},{9,8},{10,11... | collective-permute-start | bytes 6291464 | tf_op jit(solution)/shard_map/ppermute | solution.py:318
  306.4 51.3 %collective-permute-start.5 = (bf16[512,2048]{1,0:T(8,128)(2,1)}, bf16[512,2048]{1,0:T(8,128)(2,1)}, u32[]{:S(2)}, u32[]{:S(2)}) collective-permute-start(bf16[512,2048]{1,0:T(8,128)(2,1)} %shard_map.270.part_ref), channel_id=1, source_target_pairs={{0,1},{1,0},{2,3},{3,2},{4,5},{5,4},{6,7},{7,6},{8,9},{9,8},{10,11... | collective-permute-start | bytes 6291464 | tf_op jit(solution)/shard_map/ppermute | solution.py:318
  329.9 27.8 %copy-start.6 = (bf16[1024,2048]{1,0:T(8,128)(2,1)S(1)}, bf16[1024,2048]{1,0:T(8,128)(2,1)}, u32[]{:S(2)}) copy-start(bf16[1024,2048]{1,0:T(8,128)(2,1)} %copy-done.4) | copy-start | bytes 12582916
  385.7 48.4 %collective-permute-start.7 = (bf16[1024,2048]{1,0:T(8,128)(2,1)}, bf16[1024,2048]{1,0:T(8,128)(2,1)}, u32[]{:S(2)}, u32[]{:S(2)}) collective-permute-start(bf16[1024,2048]{1,0:T(8,128)(2,1)} %shard_map.283), channel_id=1, source_target_pairs={{0,2},{2,0},{4,6},{6,4},{8,10},{10,8},{12,14},{14,12},{16,18},{18,... | collective-permute-start | bytes 12582920 | tf_op jit(solution)/shard_map/ppermute | solution.py:314
  419.8 24.1 %collective-permute-start.6 = (bf16[1024,2560]{1,0:T(8,128)(2,1)}, bf16[1024,2560]{1,0:T(8,128)(2,1)}, u32[]{:S(2)}, u32[]{:S(2)}) collective-permute-start(bf16[1024,2560]{1,0:T(8,128)(2,1)} %shard_map.278), channel_id=1, source_target_pairs={{0,2},{2,0},{4,6},{6,4},{8,10},{10,8},{12,14},{14,12},{16,18},{18,... | collective-permute-start | bytes 15728648 | tf_op jit(solution)/shard_map/ppermute | solution.py:314
  422.3 11.9 %copy-start.30 = (bf16[1024,1024]{1,0:T(8,128)(2,1)S(1)}, bf16[1024,1024]{1,0:T(8,128)(2,1)}, u32[]{:S(2)}) copy-start(bf16[1024,1024]{1,0:T(8,128)(2,1)} %copy-done.29) | copy-start | bytes 6291460
  422.3 11.9 %copy-start.32 = (bf16[1024,2048]{1,0:T(8,128)(2,1)S(1)}, bf16[1024,2048]{1,0:T(8,128)(2,1)}, u32[]{:S(2)}) copy-start(bf16[1024,2048]{1,0:T(8,128)(2,1)} %get-tuple-element.88.refs_0_.ctx_ref) | copy-start | bytes 12582916
  432.8 129.6 %collective-permute-start.15 = (bf16[512,2048]{1,0:T(8,128)(2,1)}, bf16[512,2048]{1,0:T(8,128)(2,1)}, u32[]{:S(2)}, u32[]{:S(2)}) collective-permute-start(bf16[512,2048]{1,0:T(8,128)(2,1)} %shard_map.277), channel_id=1, source_target_pairs={{0,1},{1,0},{2,3},{3,2},{4,5},{5,4},{6,7},{7,6},{8,9},{9,8},{10,11... | collective-permute-start | bytes 6291464 | tf_op jit(solution)/shard_map/ppermute | solution.py:318
  442.4 61.4 %collective-permute-start.8 = (bf16[2,2,128,2048]{3,2,1,0:T(8,128)(2,1)}, bf16[2,2,128,2048]{3,2,1,0:T(8,128)(2,1)S(1)}, u32[]{:S(2)}, u32[]{:S(2)}) collective-permute-start(bf16[2,2,128,2048]{3,2,1,0:T(8,128)(2,1)} %bitcast.10), channel_id=1, source_target_pairs={{0,4},{2,6},{4,0},{6,2},{8,12},{10,14},{12,8},{14,10},{16,20},{18,... | collective-permute-start | bytes 6291464 | tf_op jit(solution)/shard_map/ppermute | solution.py:314
  454.7 76.2 %collective-permute-start.9 = (bf16[2,2,128,1280]{3,2,1,0:T(8,128)(2,1)}, bf16[2,2,128,1280]{3,2,1,0:T(8,128)(2,1)}, u32[]{:S(2)}, u32[]{:S(2)}) collective-permute-start(bf16[2,2,128,1280]{3,2,1,0:T(8,128)(2,1)} %get-tuple-element.133), channel_id=1, source_target_pairs={{0,4},{2,6},{4,0},{6,2},{8,12},{10,14},{12,8},{14,10},{16,20},{18,... | collective-permute-start | bytes 3932168 | tf_op jit(solution)/shard_map/ppermute | solution.py:314
  472.7 71.4 %collective-permute-start.12 = (bf16[512,2048]{1,0:T(8,128)(2,1)}, bf16[512,2048]{1,0:T(8,128)(2,1)}, u32[]{:S(2)}, u32[]{:S(2)}) collective-permute-start(bf16[512,2048]{1,0:T(8,128)(2,1)} %shard_map.280.refs_2_), channel_id=1, source_target_pairs={{0,1},{1,0},{2,3},{3,2},{4,5},{5,4},{6,7},{7,6},{8,9},{9,8},{10,11... | collective-permute-start | bytes 6291464 | tf_op jit(solution)/shard_map/ppermute | solution.py:318
  480.9 52.9 %collective-permute-start.10 = (bf16[2,2,128,1280]{3,2,1,0:T(8,128)(2,1)S(1)}, bf16[2,2,128,1280]{3,2,1,0:T(8,128)(2,1)S(1)}, u32[]{:S(2)}, u32[]{:S(2)}) collective-permute-start(bf16[2,2,128,1280]{3,2,1,0:T(8,128)(2,1)S(1)} %get-tuple-element.135), channel_id=1, source_target_pairs={{0,8},{2,10},{4,12},{6,14},{8,0},{10,2},{12,4},{14,6},{16,24},{18,... | collective-permute-start | bytes 3932168 | tf_op jit(solution)/shard_map/ppermute | solution.py:314
  504.8 39.0 %collective-permute-start.11 = (bf16[2,128,2048]{2,1,0:T(8,128)(2,1)S(1)}, bf16[2,128,2048]{2,1,0:T(8,128)(2,1)S(1)}, u32[]{:S(2)}, u32[]{:S(2)}) collective-permute-start(bf16[2,128,2048]{2,1,0:T(8,128)(2,1)S(1)} %get-tuple-element.141), channel_id=1, source_target_pairs={{0,8},{2,10},{4,12},{6,14},{8,0},{10,2},{12,4},{14,6},{16,24},{18,... | collective-permute-start | bytes 3145736 | tf_op jit(solution)/shard_map/ppermute | solution.py:314
  532.5 11.7 %copy-start.38 = (bf16[512,2048]{1,0:T(8,128)(2,1)S(1)}, bf16[512,2048]{1,0:T(8,128)(2,1)}, u32[]{:S(2)}) copy-start(bf16[512,2048]{1,0:T(8,128)(2,1)} %shard_map.281) | copy-start | bytes 6291460
  532.6 11.6 %copy-start.35 = (f32[512,2048]{1,0:T(8,128)S(1)}, f32[512,2048]{1,0:T(8,128)}, u32[]{:S(2)}) copy-start(f32[512,2048]{1,0:T(8,128)} %get-tuple-element.83.mid_ref) | copy-start | bytes 12582916
  532.6 11.6 %copy-start.36 = (f32[512,2048]{1,0:T(8,128)S(1)}, f32[512,2048]{1,0:T(8,128)}, u32[]{:S(2)}) copy-start(f32[512,2048]{1,0:T(8,128)} %get-tuple-element.82.mid_ref) | copy-start | bytes 12582916
  532.6 24.9 %collective-permute-start.13 = (bf16[2,128,1280]{2,1,0:T(8,128)(2,1)S(1)}, bf16[2,128,1280]{2,1,0:T(8,128)(2,1)S(1)}, u32[]{:S(2)}, u32[]{:S(2)}) collective-permute-start(bf16[2,128,1280]{2,1,0:T(8,128)(2,1)S(1)} %get-tuple-element.143), channel_id=1, source_target_pairs={{0,8},{2,10},{4,12},{6,14},{8,0},{10,2},{12,4},{14,6},{16,24},{18,... | collective-permute-start | bytes 1966088 | tf_op jit(solution)/shard_map/ppermute | solution.py:314
  534.2 23.5 %collective-permute-start.14 = (bf16[2,128,1280]{2,1,0:T(8,128)(2,1)S(1)}, bf16[2,128,1280]{2,1,0:T(8,128)(2,1)S(1)}, u32[]{:S(2)}, u32[]{:S(2)}) collective-permute-start(bf16[2,128,1280]{2,1,0:T(8,128)(2,1)S(1)} %get-tuple-element.145), channel_id=1, source_target_pairs={{0,4},{2,6},{4,0},{6,2},{8,12},{10,14},{12,8},{14,10},{16,20},{18,... | collective-permute-start | bytes 1966088 | tf_op jit(solution)/shard_map/ppermute | solution.py:314
  548.6 12.5 %copy-start.3 = (bf16[1024,2048]{1,0:T(8,128)(2,1)S(1)}, bf16[1024,2048]{1,0:T(8,128)(2,1)}, u32[]{:S(2)}) copy-start(bf16[1024,2048]{1,0:T(8,128)(2,1)} %copy-done) | copy-start | bytes 12582916
  548.6 12.5 %copy-start.37 = (bf16[512,2048]{1,0:T(8,128)(2,1)S(1)}, bf16[512,2048]{1,0:T(8,128)(2,1)}, u32[]{:S(2)}) copy-start(bf16[512,2048]{1,0:T(8,128)(2,1)} %shard_map.277) | copy-start | bytes 6291460
  558.0 35.6 %collective-permute-start.18 = (bf16[128,1280]{1,0:T(8,128)(2,1)S(1)}, bf16[128,1280]{1,0:T(8,128)(2,1)S(1)}, u32[]{:S(2)}, u32[]{:S(2)}) collective-permute-start(bf16[128,1280]{1,0:T(8,128)(2,1)S(1)} %get-tuple-element.154), channel_id=1, source_target_pairs={{0,16},{2,18},{4,20},{6,22},{8,24},{10,26},{12,28},{14,30},{16,0},... | collective-permute-start | bytes 983048 | tf_op jit(solution)/shard_map/ppermute | solution.py:314
  560.6 51.1 %collective-permute-start.16 = (bf16[128,2048]{1,0:T(8,128)(2,1)S(1)}, bf16[128,2048]{1,0:T(8,128)(2,1)S(1)}, u32[]{:S(2)}, u32[]{:S(2)}) collective-permute-start(bf16[128,2048]{1,0:T(8,128)(2,1)S(1)} %get-tuple-element.150), channel_id=1, source_target_pairs={{0,16},{2,18},{4,20},{6,22},{8,24},{10,26},{12,28},{14,30},{16,0},... | collective-permute-start | bytes 1572872 | tf_op jit(solution)/shard_map/ppermute | solution.py:314
  571.9 39.8 %collective-permute-start.17 = (bf16[128,1280]{1,0:T(8,128)(2,1)S(1)}, bf16[128,1280]{1,0:T(8,128)(2,1)S(1)}, u32[]{:S(2)}, u32[]{:S(2)}) collective-permute-start(bf16[128,1280]{1,0:T(8,128)(2,1)S(1)} %get-tuple-element.156), channel_id=1, source_target_pairs={{0,16},{2,18},{4,20},{6,22},{8,24},{10,26},{12,28},{14,30},{16,0},... | collective-permute-start | bytes 983048 | tf_op jit(solution)/shard_map/ppermute | solution.py:314
  593.5 18.2 %copy-start.45 = (bf16[128,1280]{1,0:T(8,128)(2,1)}, bf16[128,1280]{1,0:T(8,128)(2,1)S(1)}, u32[]{:S(2)}) copy-start(bf16[128,1280]{1,0:T(8,128)(2,1)S(1)} %collective-permute-done.18.refs_3_) | copy-start | bytes 983044
  613.2 16.1 %copy-start.44 = (bf16[128,2048]{1,0:T(8,128)(2,1)S(1)}, bf16[128,2048]{1,0:T(8,128)(2,1)}, u32[]{:S(2)}) copy-start(bf16[128,2048]{1,0:T(8,128)(2,1)} %copy-done.43) | copy-start | bytes 1572868
  613.2 1.4 collective-permute-start.19
  615.4 3.8 collective-permute-start.20
  619.2 3.8 collective-permute-start.21
  623.0 4.7 collective-permute-start.22
  627.8 3.8 collective-permute-start.23
  (37 other events, 150.4 us)
Sparse Core Ops, SparseCore 0:
  10.2 101.6 all-gather.2
  113.5 98.9 all-gather.4
  294.3 207.3 reduce-scatter.1
